TPU v7x, 32 devices: a whole 2x2x4 slice. The times are simulated.
32 devices in a mesh: rep: 4 (over z), lat: 8 (over y, x, core).
Axes of the slice: x: 2, y: 2, z: 4, core: 2. Of those that a mesh axis runs over, the one named last changes fastest.
Arguments:
- residual: bfloat16 [4096, 768], P(('rep', 'lat')), may hold values from -6 to 6
- valid_mask: int32 [4096], P(('rep', 'lat')), may hold values from 0 to 1
- top_idx: int32 [4096, 32], P(('rep', 'lat')), may hold values from 0 to 32767, as said below
- aux_idx: int32 [4096, 512], P(('rep', 'lat')), may hold values from 0 to 32767, as said below
- dead_flags: int32 [32768], replicated, may hold values 0 or 1
- norm_params: float32 [6, 768], replicated
- biases: float32 [6912], replicated, may hold values from -1 to 1
- w_qkv: bfloat16 [768, 2304], P('lat'), may hold values from -0.21875 to 0.21875
- w_out: bfloat16 [768, 768], P('lat'), may hold values from -0.21875 to 0.21875
- w_fc: bfloat16 [768, 3072], P('lat'), may hold values from -0.21875 to 0.21875
- w_proj: bfloat16 [3072, 768], P('lat'), may hold values from -0.109375 to 0.109375
- head_table: bfloat16 [53248, 768], P('lat')
- w_enc: float32 [768, 32768], P(None, 'lat'), may hold values from -0.21875 to 0.21875
- encoder_bias_vec: float32 [32768], P('lat'), may hold values from -3 to 3
- w_dec: float32 [32768, 768], P('lat'), may hold values from -0.21875 to 0.21875
- decoder_bias_vec: float32 [768], replicated, may hold values from -3 to 3
- mom_enc: float32 [768, 32768], P(None, 'lat'), may hold values from -0.0005126953 to 0.0005126953
- mom_benc: float32 [32768], P('lat'), may hold values from -0.00029296876 to 0.00029296876
- mom_dec: float32 [32768, 768], P('lat'), may hold values from -0.0004394531 to 0.0004394531
- mom_bdec: float32 [768], replicated, may hold values from -0.001875 to 0.001875
- q_enc: float32 [32768, 8], P('lat'), may hold values from -5 to 5
- q_dec: float32 [32768, 8], P('lat'), may hold values from -5 to 5
- err_enc: float32 [4, 768, 32768], P('rep', None, 'lat'), may hold values from -0.0043945312 to 0.0043945312
- err_dec: float32 [4, 32768, 768], P('rep', 'lat'), may hold values from -0.0043945312 to 0.0043945312
Outputs:
- loss_sum: float32 [], replicated
- valid_total: float32 [], replicated
- w_enc_new: float32 [768, 32768], P(None, 'lat')
- b_enc_new: float32 [32768], P('lat')
- w_dec_new: float32 [32768, 768], P('lat')
- b_dec_new: float32 [768], replicated
- mom_enc_new: float32 [768, 32768], P(None, 'lat')
- mom_benc_new: float32 [32768], P('lat')
- mom_dec_new: float32 [32768, 768], P('lat')
- mom_bdec_new: float32 [768], replicated
- q_enc_new: float32 [32768, 8], P('lat')
- q_dec_new: float32 [32768, 8], P('lat')
- err_enc_new: float32 [4, 768, 32768], P('rep', None, 'lat')
- err_dec_new: float32 [4, 32768, 768], P('rep', 'lat')
Inputs may be any that keep to these rules, and one draw needn't show every extreme that they name: `top_idx`: each row names 32 different latents. `aux_idx`: each row names 512 different latents.
All inputs are finite; a program needn't handle non-finite values.
Results may differ from a plain program's by a relative error of at most 0.01.
Values may be sent and summed in bfloat16 or wider, within the bound.
No kernel may reach another device: no remote copies, remote signals or barrier semaphores. Data moves between devices by JAX's collectives and lax.ppermute only.
A program may use at most 512 MiB of HBM per device.

v0:
```python
import math

import jax
import jax.numpy as jnp
from jax import lax
from jax.sharding import PartitionSpec as P

HEADS = 12


pack_base = 32768
aux_weight = 1.0 / 32.0
momentum_decay = 0.9
rate_enc = 3000.0
rate_dec = 3000.0
rate_benc = 10000.0
rate_bdec = 500.0
largest_values = lax.Precision.HIGHEST
contract_cols = (((1,), (1,)), ((), ()))
contract_rows = (((0,), (0,)), ((), ()))


def layer_norm(values, gain_row, shift_row):
    center = values - jnp.mean(values, axis=-1, keepdims=True)
    spread = jnp.mean(center * center, axis=-1, keepdims=True)
    return center * lax.rsqrt(spread + 1e-05) * gain_row + shift_row


def frozen_block(residual, norm_params, biases, w_qkv, w_out, w_fc, w_proj):
    seq_len = residual.shape[0]
    model_width = residual.shape[1]
    hidden_units = w_fc.shape[1]
    head_dim = model_width // HEADS
    stream = residual.astype(jnp.float32)
    normed = layer_norm(stream, norm_params[0], norm_params[1]).astype(jnp.bfloat16)
    joined = jnp.dot(normed, w_qkv, preferred_element_type=jnp.float32) + biases[: 3 * model_width]
    joined = joined.astype(jnp.bfloat16).reshape(seq_len, 3, HEADS, head_dim)
    scores = jnp.einsum(
        "qhd,khd->hqk", joined[:, 0], joined[:, 1], preferred_element_type=jnp.float32
    ) / math.sqrt(head_dim)
    causal = jnp.arange(seq_len)[:, None] >= jnp.arange(seq_len)[None, :]
    scores = jnp.where(causal, scores, -1e30)
    weights = jax.nn.softmax(scores, axis=-1).astype(jnp.bfloat16)
    attended = jnp.einsum("hqk,khd->qhd", weights, joined[:, 2], preferred_element_type=jnp.float32)
    attended = attended.astype(jnp.bfloat16).reshape(seq_len, model_width)
    stream = (
        stream
        + jnp.dot(attended, w_out, preferred_element_type=jnp.float32)
        + biases[3 * model_width : 4 * model_width]
    )
    normed = layer_norm(stream, norm_params[2], norm_params[3]).astype(jnp.bfloat16)
    inner_in = (
        jnp.dot(normed, w_fc, preferred_element_type=jnp.float32)
        + biases[4 * model_width : 4 * model_width + hidden_units]
    )
    activated = jax.nn.gelu(inner_in, approximate=True).astype(jnp.bfloat16)
    return (
        stream
        + jnp.dot(activated, w_proj, preferred_element_type=jnp.float32)
        + biases[4 * model_width + hidden_units :]
    )


def partial_stats(logits_orig, logits_rec):
    top_orig = jnp.max(logits_orig, axis=1)
    exp_orig = jnp.exp(logits_orig - top_orig[:, None])
    total_orig = jnp.sum(exp_orig, axis=1)
    cross_sum = jnp.sum(exp_orig * (logits_orig - logits_rec), axis=1)
    top_rec = jnp.max(logits_rec, axis=1)
    total_rec = jnp.sum(jnp.exp(logits_rec - top_rec[:, None]), axis=1)
    return (top_orig, total_orig, cross_sum, top_rec, total_rec)


def finish_stats(stats):
    lse_orig = stats[0] + jnp.log(stats[1])
    lse_rec = stats[3] + jnp.log(stats[4])
    return (lse_orig, lse_rec, stats[2] / stats[1] - lse_orig + lse_rec)


def logit_grad(weight_row, logits_orig, logits_rec, lse_orig, lse_rec):
    spread_diff = jnp.exp(logits_rec - lse_rec[:, None]) - jnp.exp(logits_orig - lse_orig[:, None])
    return (weight_row[:, None] * spread_diff).astype(jnp.bfloat16)


def orthonormal(left_factor):
    gram_matrix = jnp.dot(left_factor.T, left_factor, precision=largest_values)
    cholesky_low = jnp.linalg.cholesky(gram_matrix)
    return lax.linalg.triangular_solve(
        cholesky_low, left_factor, left_side=False, lower=True, transpose_a=True
    )


def per_device(
    residual,
    valid_mask,
    top_idx,
    aux_idx,
    dead_flags,
    norm_params,
    biases,
    w_qkv,
    w_out,
    w_fc,
    w_proj,
    head_table,
    w_enc,
    encoder_bias_vec,
    w_dec,
    decoder_bias_vec,
    mom_enc,
    mom_benc,
    mom_dec,
    mom_bdec,
    q_enc,
    q_dec,
    err_enc,
    err_dec,
):
    lat_count = lax.axis_size("lat")
    rep_count = lax.axis_size("rep")
    lat_index = lax.axis_index("lat")
    tok_dev = residual.shape[0]
    model_width = residual.shape[1]
    lat_dev = w_enc.shape[1]
    group_rows = tok_dev * lat_count
    top_count = top_idx.shape[1]
    qkv_all, out_all, fc_all, proj_all = (
        lax.all_gather(w_qkv, "lat", axis=0, tiled=True),
        lax.all_gather(w_out, "lat", axis=0, tiled=True),
        lax.all_gather(w_fc, "lat", axis=0, tiled=True),
        lax.all_gather(w_proj, "lat", axis=0, tiled=True),
    )
    valid_float = valid_mask.astype(jnp.float32)
    valid_total = lax.psum(jnp.sum(valid_float), ("rep", "lat"))
    stream = frozen_block(residual, norm_params, biases, qkv_all, out_all, fc_all, proj_all)
    mean_removed = (stream - decoder_bias_vec).astype(jnp.bfloat16)
    centered_group = lax.all_gather(mean_removed, "lat", axis=0, tiled=True)
    enc_weight = w_enc.astype(jnp.bfloat16)
    pre_scores = (
        jnp.dot(centered_group, enc_weight, preferred_element_type=jnp.float32) + encoder_bias_vec
    )
    all_ids = jnp.concatenate([top_idx, aux_idx], axis=1)
    packed = all_ids[:, 0::2] * pack_base + all_ids[:, 1::2]
    packed_group, valid_group = (
        lax.all_gather(packed, "lat", axis=0, tiled=True),
        lax.all_gather(valid_mask, "lat", axis=0, tiled=True),
    )
    pick_ids = jnp.stack([packed_group // pack_base, packed_group % pack_base], axis=2).reshape(
        group_rows, -1
    )
    local_ids = pick_ids - lat_index * lat_dev
    inside = (local_ids >= 0) & (local_ids < lat_dev)
    local_ids = jnp.where(inside, local_ids, lat_dev)
    row_ids = jnp.arange(group_rows)[:, None]
    zero_mask = jnp.zeros((group_rows, lat_dev), jnp.float32)
    dead_local = lax.dynamic_slice_in_dim(dead_flags, lat_index * lat_dev, lat_dev).astype(
        jnp.float32
    )
    mask_top = zero_mask.at[row_ids, local_ids[:, :top_count]].set(1.0, mode="drop")
    mask_aux = zero_mask.at[row_ids, local_ids[:, top_count:]].set(1.0, mode="drop") * dead_local
    topk_code = (mask_top * pre_scores).astype(jnp.bfloat16)
    auxiliary_code = (mask_aux * pre_scores).astype(jnp.bfloat16)
    dec_weight = w_dec.astype(jnp.bfloat16)
    decoded = lax.psum_scatter(
        jnp.concatenate(
            [
                jnp.dot(topk_code, dec_weight, preferred_element_type=jnp.float32),
                jnp.dot(auxiliary_code, dec_weight, preferred_element_type=jnp.float32),
            ],
            axis=1,
        ),
        "lat",
        scatter_dimension=0,
        tiled=True,
    )
    rebuilt_input = decoded[:, :model_width] + decoder_bias_vec
    auxiliary_rebuilt = decoded[:, model_width:]

    def final_norm(values):
        return layer_norm(values, norm_params[4], norm_params[5])

    orig_normed = final_norm(stream).astype(jnp.bfloat16)
    rec_float, norm_back = jax.vjp(final_norm, rebuilt_input)
    rec_normed = rec_float.astype(jnp.bfloat16)
    weight_own = valid_float / valid_total
    table_full = lax.all_gather(head_table, "lat", axis=0, tiled=True)
    logits_orig = lax.dot_general(
        orig_normed, table_full, contract_cols, preferred_element_type=jnp.float32
    )
    logits_rec = lax.dot_general(
        rec_normed, table_full, contract_cols, preferred_element_type=jnp.float32
    )
    lse_orig, lse_rec, kl_own = finish_stats(partial_stats(logits_orig, logits_rec))
    grad_logits = logit_grad(weight_own, logits_orig, logits_rec, lse_orig, lse_rec)
    grad_normed = jnp.dot(grad_logits, table_full, preferred_element_type=jnp.float32)
    (grad_head,) = norm_back(grad_normed)
    resid_err = stream - rebuilt_input - auxiliary_rebuilt
    per_token = kl_own + aux_weight * jnp.sum(resid_err * resid_err, axis=1)
    loss_own = jnp.sum(valid_float * per_token)
    aux_pull = -(2.0 * aux_weight) * weight_own[:, None] * resid_err
    grad_recon = (grad_head + aux_pull).astype(jnp.bfloat16)
    grad_aux = aux_pull.astype(jnp.bfloat16)
    recon_group, aux_group = (
        lax.all_gather(grad_recon, "lat", axis=0, tiled=True),
        lax.all_gather(grad_aux, "lat", axis=0, tiled=True),
    )
    top_back = lax.dot_general(
        recon_group, dec_weight, contract_cols, preferred_element_type=jnp.float32
    )
    aux_back = lax.dot_general(
        aux_group, dec_weight, contract_cols, preferred_element_type=jnp.float32
    )
    grad_top = (mask_top * top_back).astype(jnp.bfloat16)
    grad_auxpre = (mask_aux * aux_back).astype(jnp.bfloat16)
    grad_dec = lax.dot_general(
        topk_code, recon_group, contract_rows, preferred_element_type=jnp.float32
    ) + lax.dot_general(
        auxiliary_code, aux_group, contract_rows, preferred_element_type=jnp.float32
    )
    grad_enc = lax.dot_general(
        centered_group, grad_top, contract_rows, preferred_element_type=jnp.float32
    ) + lax.dot_general(
        centered_group, grad_auxpre, contract_rows, preferred_element_type=jnp.float32
    )
    grad_benc = jnp.sum(grad_top.astype(jnp.float32), axis=0) + jnp.sum(
        grad_auxpre.astype(jnp.float32), axis=0
    )
    grad_bdec = jnp.sum(grad_recon.astype(jnp.float32), axis=0) - jnp.dot(
        enc_weight.astype(jnp.float32), grad_benc, precision=largest_values
    )
    full_enc = grad_enc + err_enc[0]
    full_dec = grad_dec + err_dec[0]
    left_enc = jnp.dot(full_enc, q_enc, precision=largest_values)
    left_dec = lax.dot_general(full_dec, q_dec, contract_rows, precision=largest_values)
    left_enc, left_dec, grad_bdec, loss_sum = lax.psum(
        (left_enc, left_dec, grad_bdec, loss_own), ("rep", "lat")
    )
    ortho_enc = orthonormal(left_enc)
    ortho_dec = orthonormal(left_dec)
    right_enc = lax.dot_general(full_enc, ortho_enc, contract_rows, precision=largest_values)
    right_dec = jnp.dot(full_dec, ortho_dec, precision=largest_values)
    right_enc, right_dec, grad_benc = (
        lax.psum(right_enc.astype(jnp.bfloat16), "rep").astype(jnp.float32),
        lax.psum(right_dec.astype(jnp.bfloat16), "rep").astype(jnp.float32),
        lax.psum(grad_benc.astype(jnp.bfloat16), "rep").astype(jnp.float32),
    )
    approx_enc = jnp.dot(ortho_enc, right_enc.T, precision=largest_values)
    approx_dec = jnp.dot(right_dec, ortho_dec.T, precision=largest_values)
    err_enc_new = (full_enc - approx_enc / rep_count)[None]
    err_dec_new = (full_dec - approx_dec / rep_count)[None]
    mom_enc_new = momentum_decay * mom_enc + approx_enc
    mom_benc_new = momentum_decay * mom_benc + grad_benc
    mom_dec_new = momentum_decay * mom_dec + approx_dec
    mom_bdec_new = momentum_decay * mom_bdec + grad_bdec
    w_enc_new = w_enc - rate_enc * mom_enc_new
    b_enc_new = encoder_bias_vec - rate_benc * mom_benc_new
    b_dec_new = decoder_bias_vec - rate_bdec * mom_bdec_new
    dec_step = w_dec - rate_dec * mom_dec_new
    w_dec_new = dec_step * lax.rsqrt(jnp.sum(dec_step * dec_step, axis=1, keepdims=True) + 1e-06)
    return (
        loss_sum,
        valid_total,
        w_enc_new,
        b_enc_new,
        w_dec_new,
        b_dec_new,
        mom_enc_new,
        mom_benc_new,
        mom_dec_new,
        mom_bdec_new,
        right_enc,
        right_dec,
        err_enc_new,
        err_dec_new,
    )


def solution(mesh):
    in_specs = (
        P(("rep", "lat"), None),
        P(("rep", "lat")),
        P(("rep", "lat"), None),
        P(("rep", "lat"), None),
        P(),
        P(),
        P(),
        P("lat", None),
        P("lat", None),
        P("lat", None),
        P("lat", None),
        P("lat", None),
        P(None, "lat"),
        P("lat"),
        P("lat", None),
        P(),
        P(None, "lat"),
        P("lat"),
        P("lat", None),
        P(),
        P("lat", None),
        P("lat", None),
        P("rep", None, "lat"),
        P("rep", "lat", None),
    )
    out_specs = (
        P(),
        P(),
        P(None, "lat"),
        P("lat"),
        P("lat", None),
        P(),
        P(None, "lat"),
        P("lat"),
        P("lat", None),
        P(),
        P("lat", None),
        P("lat", None),
        P("rep", None, "lat"),
        P("rep", "lat", None),
    )
    return jax.shard_map(
        per_device, mesh=mesh, in_specs=in_specs, out_specs=out_specs, check_vma=False
    )
```

profile of v0, /device:TPU:0, one launch (start us, length us, event | category | flops | bytes accessed | tf_op | source)
XLA Modules:
  0.0 3350.5 jit_solution(10935672828311183727)
XLA Ops:
  10.0 1.1 copy.104
  11.2 0.7 pad_add_fusion.1
  14.3 1.0 slice_reduce_fusion.1
  15.3 1.0 convert_reduce_fusion.2
  16.4 1.1 fusion.39
  17.5 29.1 all-gather.10.cloned.1.call-done
  46.6 2.8 fusion.10
  50.9 21.7 all-gather.12.cloned.1.call-done
  72.6 1.7 fusion.87
  74.5 38.9 %all-gather.16.cloned.1.call-done = bf16[3072,768]{1,0:T(8,128)(2,1)} async-done(((bf16[384,768]{1,0:T(8,128)(2,1)}), bf16[3072,768]{1,0:T(8,128)(2,1)}) %all-gather.16.cloned.1.call-update) | async-done | bytes 4718608 | tf_op jit(solution)/shard_map/all_gather | solution.py:131
  113.4 40.7 %all-gather.14.cloned.1.call-done = bf16[768,3072]{1,0:T(8,128)(2,1)} async-done(((bf16[96,3072]{1,0:T(8,128)(2,1)}), bf16[768,3072]{1,0:T(8,128)(2,1)}) %all-gather.14.cloned.1.call-update) | async-done | bytes 4718608 | tf_op jit(solution)/shard_map/all_gather | solution.py:130
  154.1 6.3 fusion.84
  161.5 8.0 convert_element_type.107
  169.5 10.8 all-gather.20.cloned.1.call-done
  180.3 2.2 fusion.30
  182.7 1.7 copy.105
  184.4 2.6 sub.144
  187.0 1.9 and_select_fusion
  189.6 127.0 %scatter_custom_fusion = f32[4194304]{0:T(1024)} fusion(s32[32768]{0:T(1024)S(1)} %reshape.154, f32[32768]{0:T(1024)S(1)} %broadcast.182, f32[]{:T(128)} %constant.107.clone.1), kind=kCustom, calls=%fused_computation.29 | custom fusion | bytes 16777220
  316.6 18.2 reshape.147
  336.2 0.8 and_reduce_fusion
  337.6 1.8 copy.107
  339.4 3.4 copy.122
  343.0 1921.2 %scatter_custom_fusion.1 = f32[4194304]{0:T(1024)} fusion(s32[524288]{0:T(1024)} %bitcast.113, f32[524288]{0:T(1024)S(1)} %broadcast.184, f32[]{:T(128)} %constant.107.clone.1), kind=kCustom, calls=%fused_computation.27 | custom fusion | bytes 16777728
  2264.1 18.2 reshape.151
  2282.4 24.3 multiply_convert_fusion.4
  2306.6 11.0 fusion.91
  2317.7 9.0 fusion.90
  2326.7 3.7 pad_maximum_fusion
  2331.3 60.9 %reduce-scatter.2.cloned.1.call-done = f32[128,1536]{1,0:T(8,128)} async-done(((f32[1024,1536]{1,0:T(8,128)}), f32[128,1536]{1,0:T(8,128)}) %reduce-scatter.2.cloned.1.call-update) | async-done | bytes 786448 | tf_op jit(solution)/shard_map/reduce_scatter | solution.py:164
  2392.3 1.1 fusion.66
  2393.4 1.3 multiply_reduce_fusion.4
  2394.8 365.1 %all-gather.18.cloned.1.call-done = bf16[53248,768]{1,0:T(8,128)(2,1)} async-done(((bf16[6656,768]{1,0:T(8,128)(2,1)}), bf16[53248,768]{1,0:T(8,128)(2,1)}) %all-gather.18.cloned.1.call-update) | async-done | bytes 81788944 | tf_op jit(solution)/shard_map/all_gather | solution.py:186
  2759.9 43.8 %fusion.88 = (f32[128]{0:T(128)S(1)}, f32[128,53248]{1,0:T(8,128)}) fusion(bf16[53248,768]{1,0:T(8,128)(2,1)} %all-gather.18.cloned.1.call-done, f32[128,768]{1,0:T(8,128)S(1)} %get-tuple-element.137, f32[768]{0:T(1024)S(1)} %get-tuple-element.94, f32[768]{0:T(1024)S(1)} %get-tuple-element.89, f32[128]{0:T(128)S(1)} %get-tuple-element.149, ...), kind=kOutput, calls=%fused_computation.195 | convolution fusion | flops 10476290048 | bytes 109452800 | tf_op jit(solution)/shard_map/dot_general | solution.py:187
  2803.7 43.8 %fusion.89 = (f32[128]{0:T(128)S(1)}, f32[128,53248]{1,0:T(8,128)}) fusion(bf16[53248,768]{1,0:T(8,128)(2,1)} %all-gather.18.cloned.1.call-done, f32[128]{0:T(128)S(1)} %get-tuple-element.150, f32[128]{0:T(128)S(1)} %broadcast_multiply_fusion.2, f32[768]{0:T(1024)S(1)} %get-tuple-element.94, f32[768]{0:T(1024)S(1)} %get-tuple-element.89, ...), kind=kOutput, calls=%fused_computation.196 | convolution fusion | flops 10476388352 | bytes 109458944 | tf_op jit(solution)/shard_map/dot_general | solution.py:190
  2847.5 20.2 multiply_reduce_fusion
  2868.2 39.5 %psum.57 = f32[]{:T(128)} all-reduce(f32[]{:T(128)} %get-tuple-element.95), channel_id=1, replica_groups=mesh['rep'=4,'lat'=8] {'rep','lat'}, use_global_device_ids=true, to_apply=%region_22.23 | all-reduce | flops 1 | bytes 8 | tf_op jit(solution)/shard_map/psum | solution.py:134
  2908.4 44.3 %multiply_reduce_fusion.3 = (f32[128]{0:T(128)S(1)}, f32[128,768]{1,0:T(8,128)S(1)}) fusion(f32[128]{0:T(128)S(1)} %broadcast_multiply_fusion.2, f32[768]{0:T(1024)S(1)} %copy-done.6, f32[128,1536]{1,0:T(8,128)S(1)} %copy-done.2, f32[768]{0:T(1024)S(1)} %get-tuple-element.89, bf16[53248,768]{1,0:T(8,128)(2,1)} %all-gather.18.cloned.1.call-done, ...), kind=kOutput, calls=%fused_computation.96 | convolution fusion | flops 10503553024 | bytes 137110016 | tf_op jit(solution)/shard_map/dot_general | solution.py:195
  2953.0 0.9 convert_reduce_fusion.3
  2954.7 12.6 copy.115
  2967.4 12.7 copy.112
  2980.7 13.7 convert_reduce_fusion.1
  2994.4 14.5 all-gather.26.cloned.1.call-done
  3008.9 13.7 convert_reduce_fusion
  3022.7 8.1 fusion.33
  3030.7 9.6 fusion.92
  3040.3 17.5 bitcast_add_fusion.1
  3057.9 13.4 fusion.93
  3071.3 13.0 fusion.95
  3084.3 20.2 bitcast_add_fusion
  3104.5 9.4 fusion.96
  3113.9 40.4 %all-reduce = (f32[]{:T(128)}, f32[768,8]{0,1:T(8,128)S(1)}, f32[768,8]{0,1:T(8,128)S(1)}, f32[768]{0:T(1024)S(1)}) all-reduce(f32[]{:T(128)} %get-tuple-element.96, f32[768,8]{0,1:T(8,128)S(1)} %fusion.93, f32[768,8]{0,1:T(8,128)S(1)} %fusion.96, f32[768]{0:T(1024)S(1)} %sub.163), channel_id=1, replica_groups=mesh['rep'=4,'lat'=8] {'rep','lat'}, use_global_device_ids=true, to_apply=%region_20.21 | all-reduce | flops 13057 | bytes 104456 | tf_op jit(solution)/shard_map/psum | solution.py:235
  3157.5 9.6 convolution_convert_fusion.1
  3170.3 13.7 convolution_convert_fusion
  3184.0 10.7 psum.60
  3196.0 32.4 all-reduce.4.cloned.1.call-done
  3228.4 1.5 convert_element_type.123
  3229.9 30.2 multiply_subtract_fusion.1
  3260.7 16.8 multiply_reduce_fusion.1
  3277.5 12.6 copy.118
  3290.1 14.3 broadcast_multiply_fusion
  3304.4 12.6 copy.117
  3317.0 12.6 copy.116
  3329.6 14.0 subtract_bitcast_fusion
  (128 shorter events, 22.8 us)
Async XLA Ops:
  7.2 3050.7 %copy-start = (f32[4096,8]{0,1:T(8,128)S(1)}, f32[4096,8]{0,1:T(8,128)}, u32[]{:S(2)}) copy-start(f32[4096,8]{0,1:T(8,128)} %param.47) | copy-start | bytes 393220
  7.2 65.4 %copy-start.3 = (bf16[128,768]{1,0:T(8,128)(2,1)S(1)}, bf16[128,768]{1,0:T(8,128)(2,1)}, u32[]{:S(2)}) copy-start(bf16[128,768]{1,0:T(8,128)(2,1)} %param.27) | copy-start | bytes 589828
  7.2 39.4 %all-gather.10.cloned.1.call-start = ((), (), s32[]{:S(2)}) async-start(), calls=%async_computation.1 | async-start | bytes 3981312 | tf_op jit(solution)/shard_map/all_gather | solution.py:128
  7.9 64.7 %all-gather.12.cloned.1.call-start = ((), (), s32[]{:S(2)}) async-start(), calls=%async_computation.2 | async-start | bytes 1327104 | tf_op jit(solution)/shard_map/all_gather | solution.py:129
  8.7 104.8 %all-gather.16.cloned.1.call-start = ((), (), s32[]{:S(2)}) async-start(), calls=%async_computation.4 | async-start | bytes 5308416 | tf_op jit(solution)/shard_map/all_gather | solution.py:131
  9.4 144.7 %all-gather.14.cloned.1.call-start = ((), (), s32[]{:S(2)}) async-start(), calls=%async_computation.3 | async-start | bytes 5308416 | tf_op jit(solution)/shard_map/all_gather | solution.py:130
  10.0 170.3 %all-gather.20.cloned.1.call-start = ((), (), s32[]{:S(2)}) async-start(), calls=%async_computation.6 | async-start | bytes 1253376 | tf_op jit(solution)/shard_map/all_gather | solution.py:145
  11.1 143.0 %copy-start.6 = (f32[768]{0:T(1024)S(1)}, f32[768]{0:T(1024)}, u32[]{:S(2)}) copy-start(f32[768]{0:T(1024)} %param.42) | copy-start | bytes 9220
  11.1 143.0 %slice-start = ((f32[6912]{0:T(1024)}), f32[3072]{0:T(1024)S(1)}, s32[]{:S(2)}) async-start(f32[6912]{0:T(1024)} %param.33), calls=%async_computation.12 | async-start | bytes 24576 | tf_op jit(solution)/shard_map/slice | solution.py:54
  12.8 2269.6 %all-gather.22.cloned.1.call-start = ((), (), s32[]{:S(2)}) async-start(), calls=%async_computation.7 | async-start | bytes 1769472 | tf_op jit(solution)/shard_map/all_gather | solution.py:137
  160.5 2231.8 %reduce-scatter.2.cloned.1.call-start = ((), (), s32[]{:S(2)}) async-start(), calls=%async_computation.8 | async-start | bytes 7077888 | tf_op jit(solution)/shard_map/reduce_scatter | solution.py:164
  161.5 2120.9 %copy-start.7 = (f32[4096]{0:T(1024)}, f32[4096]{0:T(1024)S(1)}, u32[]{:S(2)}) copy-start(f32[4096]{0:T(1024)S(1)} %dynamic-slice_convert_fusion) | copy-start | bytes 49156
  182.5 6.5 copy-start.15
  182.5 6.6 copy-start.14
  2264.1 18.2 copy-start.9
  2306.6 11.1 copy-start.1
  2330.4 429.5 %all-gather.18.cloned.1.call-start = ((), (), s32[]{:S(2)}) async-start(), calls=%async_computation.5 | async-start | bytes 92012544 | tf_op jit(solution)/shard_map/all_gather | solution.py:186
  2331.1 649.6 %all-gather.24.cloned.1.call-start = ((), (), s32[]{:S(2)}) async-start(), calls=%async_computation.9 | async-start | bytes 1769472 | tf_op jit(solution)/shard_map/all_gather | solution.py:204
  2759.9 43.8 %copy-start.2 = (f32[128,1536]{1,0:T(8,128)S(1)}, f32[128,1536]{1,0:T(8,128)}, u32[]{:S(2)}) copy-start(f32[128,1536]{1,0:T(8,128)} %reduce-scatter.2.cloned.1.call-done) | copy-start | bytes 2359300
  2847.5 20.2 copy-start.16
  2953.9 55.0 %all-gather.26.cloned.1.call-start = ((), (), s32[]{:S(2)}) async-start(), calls=%async_computation.10 | async-start | bytes 1769472 | tf_op jit(solution)/shard_map/all_gather | solution.py:205
  2954.5 273.9 %all-reduce.4.cloned.1.call-start = ((), (), s32[]{:S(2)}) async-start(), calls=%async_computation.11 | async-start | bytes 262144 | tf_op jit(solution)/shard_map/psum | solution.py:243
  2980.0 28.9 copy-start.8
  3022.6 8.1 copy-start.4
  3022.6 8.1 copy-start.19
  3057.9 13.4 copy-start.17
  3071.3 13.0 copy-start.18
  3084.3 20.2 copy-start.11
  3170.3 24.5 copy-start.10
  3170.3 24.5 copy-start.12
  3170.3 25.1 copy-start.13
  3229.9 30.2 copy-start.5
Sparse Core Ops, SparseCore 0:
  9.9 36.6 all-gather.9
  48.5 24.0 all-gather.11
  74.5 38.9 all-gather.15
  115.2 38.9 all-gather.13
  156.4 23.8 all-gather.19
  182.6 25.6 all-gather.21
  2330.5 61.7 reduce-scatter.1
  2394.4 365.4 all-gather.17
  2954.0 26.6 all-gather.23
  2983.2 25.6 all-gather.25
  3194.9 33.4 all-reduce.3
where the time goes:
time: 3360 us; the launch traced here: 3350 us
  local copies, waits for them, and re-layouts  2160 us (64%)
  waiting for transfers between devices  619 us (18%)
  matrix products  378 us (11%)
  blocking collectives  90.7 us (3%)
  other arithmetic  85.4 us (3%)
    unnamed x53, local copies, waits for them, and re-layouts  2110 us
    all_gather x1, waiting for transfers between devices, per_device(): table_full = lax.all_gather(head_table, 'lat', axis=0, tiled=True)  365 us
  transfers between devices with their start and end apart: 11, of which 10 were waited for; matrix products, arithmetic and copies ran while one was open for 65% of the time, Pallas kernels for 0%

commit v1 on v0

v1 whole, which is shorter than its diff:
```python
import functools
import math

import jax
import jax.numpy as jnp
from jax import lax
from jax.experimental import pallas as pl
from jax.experimental.pallas import tpu as pltpu
from jax.sharding import PartitionSpec as P

HEADS = 12

pack_base = 32768
aux_weight = 1.0 / 32.0
momentum_decay = 0.9
rate_enc = 3000.0
rate_dec = 3000.0
rate_benc = 10000.0
rate_bdec = 500.0
lanes = 128
vmem_most = 60 * 2**20
largest_values = lax.Precision.HIGHEST
contract_cols = (((1,), (1,)), ((), ()))
contract_rows = (((0,), (0,)), ((), ()))
contract_plain = (((1,), (0,)), ((), ()))
f32 = jnp.float32
bf16 = jnp.bfloat16


def swap(values, axis, bit):
    count = lax.axis_size(axis)
    return lax.ppermute(values, axis, [(i, i ^ bit) for i in range(count)])


def bits_of(axis):
    count = lax.axis_size(axis)
    return [1 << k for k in range(count.bit_length() - 1)]


def gather_blocks(own):
    count = lax.axis_size("lat")
    if count == 8:
        half = own.shape[0] // 2
        blocks = {0: own, 2: swap(own, "lat", 2), 4: swap(own, "lat", 4)}
        blocks[1] = swap(own, "lat", 1)
        diag = [swap(blocks[4][:half], "lat", 2), swap(blocks[2][half:], "lat", 4)]
        blocks[3] = swap(blocks[2], "lat", 1)
        blocks[5] = swap(blocks[4], "lat", 1)
        blocks[6] = jnp.concatenate(diag, axis=0)
        blocks[7] = swap(blocks[6], "lat", 1)
    else:
        blocks = {0: own}
        for bit in bits_of("lat")[1:] + [1]:
            order = sorted(blocks)
            moved = swap(jnp.stack([blocks[j] for j in order]), "lat", bit)
            for at, j in enumerate(order):
                blocks[j ^ bit] = moved[at]
    return [blocks[j] for j in range(count)]


def gather_tokens(own):
    return jnp.concatenate(gather_blocks(own), axis=0)


def scatter_paths():
    others = bits_of("lat")[1:]
    if len(others) == 2:
        return [(0, 2, others), (1, 2, others[::-1])]
    return [(0, 1, others)]


def scatter_sum(partial):
    count = lax.axis_size("lat")
    rows, cols = partial.shape[0] // count, partial.shape[1]
    partial = partial.reshape(count, rows, cols)
    moved = swap(partial[1::2], "lat", 1)
    chip = partial[0::2] + moved
    done = []
    for part, parts, order in scatter_paths():
        width = cols // parts
        held = {2 * k: chip[k][:, part * width : (part + 1) * width] for k in range(count // 2)}
        for bit in order:
            sent = [j for j in sorted(held) if j & bit]
            got = swap(jnp.stack([held[j] for j in sent]).astype(bf16), "lat", bit)
            for at, j in enumerate(sent):
                held[j ^ bit] = held[j ^ bit] + got[at].astype(f32)
                del held[j]
        done.append(held[0])
    return jnp.concatenate(done, axis=1)


def merge(mean_a, lse_a, mean_b, lse_b):
    top = jnp.maximum(lse_a, lse_b)
    exp_a, exp_b = jnp.exp(lse_a - top), jnp.exp(lse_b - top)
    total = exp_a + exp_b
    mixed = mean_a.astype(f32) * (exp_a / total) + mean_b.astype(f32) * (exp_b / total)
    return mixed, top + jnp.log(total)


def scatter_mean(means, lses):
    count = lax.axis_size("lat")
    rows, cols = means.shape[0] // count, means.shape[1]
    means = means.reshape(count, rows, cols)
    lses = lses.reshape(count, rows, 1)
    chip, chip_lse = merge(
        means[0::2], lses[0::2], swap(means[1::2], "lat", 1), swap(lses[1::2], "lat", 1)
    )
    done = []
    for part, parts, order in scatter_paths():
        width = cols // parts
        held = {
            2 * k: (chip[k][:, part * width : (part + 1) * width], chip_lse[k])
            for k in range(count // 2)
        }
        for bit in order:
            sent = [j for j in sorted(held) if j & bit]
            got = swap(jnp.stack([held[j][0] for j in sent]).astype(bf16), "lat", bit)
            got_lse = swap(jnp.stack([held[j][1] for j in sent]), "lat", bit)
            for at, j in enumerate(sent):
                held[j ^ bit] = merge(*held[j ^ bit], got[at], got_lse[at])
                del held[j]
        done.append(held[0])
    return jnp.concatenate([mean for mean, _ in done], axis=1), done[0][1]


def sum_over(values, axes, sent_as=None):
    for axis in axes:
        for bit in bits_of(axis):
            if sent_as is not None:
                values = values.astype(sent_as)
            values = values.astype(f32) + swap(values, axis, bit).astype(f32)
    return values


def mask_kernel(tokens, hi_count, aux_count, ids_ref, dead_ref, out_ref, scratch):
    width = ids_ref.shape[1]
    hi_rows = lax.broadcasted_iota(jnp.int32, (hi_count, width), 0)
    lo_rows = lax.broadcasted_iota(jnp.int32, (lanes, width), 0)
    is_aux = lax.broadcasted_iota(jnp.int32, (hi_count, width), 1) < aux_count
    weight = jnp.where(is_aux, 2.0, 1.0)

    def one_token(t, carry):
        row = ids_ref[pl.ds(t, 1), :]
        hi_hot = jnp.where(hi_rows == (row >> 7), weight, 0.0).astype(bf16)
        lo_hot = jnp.where(lo_rows == (row & 127), 1.0, 0.0).astype(bf16)
        picked = lax.dot_general(hi_hot, lo_hot, contract_cols, preferred_element_type=f32)
        scratch[pl.ds(pl.multiple_of(t * hi_count, hi_count), hi_count), :] = picked
        return carry

    lax.fori_loop(0, tokens, one_token, 0, unroll=16)
    for hi in range(hi_count):
        code = scratch[pl.ds(hi, tokens, stride=hi_count), :]
        at = slice(hi * lanes, (hi + 1) * lanes)
        aux = jnp.where(code >= 2.0, 2.0, 0.0)
        out_ref[:, at] = (code - aux + aux * dead_ref[:, at]).astype(bf16)


def build_mask(local_ids, dead_local, aux_count):
    group, width = local_ids.shape
    lat_dev = dead_local.shape[1]
    hi_count, tokens = lat_dev // lanes, 64
    return pl.pallas_call(
        functools.partial(mask_kernel, tokens, hi_count, aux_count),
        out_shape=jax.ShapeDtypeStruct((group, lat_dev), bf16),
        grid=(group // tokens,),
        in_specs=[
            pl.BlockSpec((tokens, width), lambda i: (i, 0)),
            pl.BlockSpec((1, lat_dev), lambda i: (0, 0)),
        ],
        out_specs=pl.BlockSpec((tokens, lat_dev), lambda i: (i, 0)),
        scratch_shapes=[pltpu.VMEM((tokens * hi_count, lanes), f32)],
        compiler_params=pltpu.CompilerParams(vmem_limit_bytes=vmem_most),
        cost_estimate=pl.CostEstimate(
            flops=64 * group * lat_dev * width // 4, bytes_accessed=2 * group * lat_dev, transcendentals=0
        ),
        name="build_mask",
    )(local_ids, dead_local)


def head_kernel(chunk, chunks, normed_ref, table_ref, mean_ref, lse_ref):
    normed = normed_ref[...]

    def logits_of(c):
        return lax.dot_general(
            normed, table_ref[c * chunk : (c + 1) * chunk, :], contract_cols, preferred_element_type=f32
        )

    def fold(values, op):
        folded = values[:, :lanes]
        for k in range(1, chunk // lanes):
            folded = op(folded, values[:, k * lanes : (k + 1) * lanes])
        return folded

    top = total = mean = None
    logits = logits_of(0)
    for c in range(chunks):
        later = logits_of(c + 1) if c + 1 < chunks else None
        chunk_top = jnp.max(fold(logits, jnp.maximum), axis=1, keepdims=True)
        new_top = chunk_top if top is None else jnp.maximum(top, chunk_top)
        grown = jnp.exp(logits - new_top).astype(bf16)
        chunk_total = fold(grown.astype(f32), jnp.add)
        chunk_mean = lax.dot_general(
            grown, table_ref[c * chunk : (c + 1) * chunk, :], contract_plain, preferred_element_type=f32
        )
        if top is None:
            total, mean = chunk_total, chunk_mean
        else:
            shrink = jnp.exp(top - new_top)
            total, mean = total * shrink + chunk_total, mean * shrink + chunk_mean
        top, logits = new_top, later
    total = jnp.sum(total, axis=1, keepdims=True)
    mean_ref[...] = mean / total
    lse_ref[...] = top + jnp.log(total)


def head_part(normed, table):
    rows, width = normed.shape
    entries = table.shape[0]
    tiles = entries // lanes
    chunk = lanes * max(d for d in range(1, 14) if tiles % d == 0)
    block = 256
    return pl.pallas_call(
        functools.partial(head_kernel, chunk, entries // chunk),
        out_shape=(jax.ShapeDtypeStruct((rows, width), f32), jax.ShapeDtypeStruct((rows, 1), f32)),
        grid=(rows // block,),
        in_specs=[
            pl.BlockSpec((block, width), lambda i: (i, 0)),
            pl.BlockSpec((entries, width), lambda i: (0, 0), pipeline_mode=pl.Buffered(1)),
        ],
        out_specs=(
            pl.BlockSpec((block, width), lambda i: (i, 0)),
            pl.BlockSpec((block, 1), lambda i: (i, 0)),
        ),
        compiler_params=pltpu.CompilerParams(vmem_limit_bytes=vmem_most),
        cost_estimate=pl.CostEstimate(
            flops=6 * rows * entries * width,
            bytes_accessed=2 * entries * width + 6 * rows * width,
            transcendentals=rows * entries,
        ),
        name="head_part",
    )(normed, table)


def split_three(values):
    first = values.astype(bf16)
    rest = values - first.astype(f32)
    second = rest.astype(bf16)
    return first, second, (rest - second.astype(f32)).astype(bf16)


def enc_final_kernel(rep_count, left_ref, right_ref, full_ref, mom_ref, w_ref, w_out, mom_out, err_out):
    approx = lax.dot_general(
        left_ref[...], right_ref[...], contract_rows, preferred_element_type=f32
    )
    err_out[...] = full_ref[...] - approx * (1.0 / rep_count)
    mom = momentum_decay * mom_ref[...] + approx
    mom_out[...] = mom
    w_out[...] = w_ref[...] - rate_enc * mom


def dec_final_kernel(rep_count, left_ref, right_ref, full_ref, mom_ref, w_ref, w_out, mom_out, err_out):
    approx = lax.dot_general(
        right_ref[...], left_ref[...], contract_rows, preferred_element_type=f32
    )
    err_out[...] = full_ref[...] - approx * (1.0 / rep_count)
    mom = momentum_decay * mom_ref[...] + approx
    mom_out[...] = mom
    step = w_ref[...] - rate_dec * mom
    w_out[...] = step * lax.rsqrt(jnp.sum(step * step, axis=1, keepdims=True) + 1e-06)


def final_update(kernel, by_rows, rep_count, left, right, full, mom, weight):
    l1, l2, l3 = split_three(left)
    r1, r2, r3 = split_three(right)
    left = jnp.concatenate([l1, l1, l2, l2, l1, l3], axis=0)
    right = jnp.concatenate([r1, r2, r1, r2, r3, r1], axis=0)
    latents, width = right.shape[1], left.shape[1]
    block = 512
    if by_rows:
        big = pl.BlockSpec((block, width), lambda i: (i, 0))
    else:
        big = pl.BlockSpec((width, block), lambda i: (0, i))
    return pl.pallas_call(
        functools.partial(kernel, rep_count),
        out_shape=(jax.ShapeDtypeStruct(full.shape, f32),) * 3,
        grid=(latents // block,),
        in_specs=[
            pl.BlockSpec(left.shape, lambda i: (0, 0)),
            pl.BlockSpec((right.shape[0], block), lambda i: (0, i)),
            big,
            big,
            big,
        ],
        out_specs=(big, big, big),
        compiler_params=pltpu.CompilerParams(vmem_limit_bytes=vmem_most),
        cost_estimate=pl.CostEstimate(
            flops=2 * 48 * latents * width, bytes_accessed=24 * latents * width, transcendentals=0
        ),
        name="final_update",
    )(left, right, full, mom, weight)


def layer_norm(values, gain_row, shift_row):
    center = values - jnp.mean(values, axis=-1, keepdims=True)
    spread = jnp.mean(center * center, axis=-1, keepdims=True)
    return center * lax.rsqrt(spread + 1e-05) * gain_row + shift_row


def frozen_block(residual, norm_params, biases, qkv, w_out, fc, w_proj):
    seq_len = residual.shape[0]
    model_width = residual.shape[1]
    hidden_units = w_proj.shape[0]
    head_dim = model_width // HEADS
    stream = residual.astype(f32)
    normed = layer_norm(stream, norm_params[0], norm_params[1]).astype(bf16)

    def times(values, parts, bias):
        width = parts[0].shape[1]
        return [
            jnp.dot(values, part, preferred_element_type=f32) + bias[k * width : (k + 1) * width]
            for k, part in enumerate(parts)
        ]

    queries, keys, values = [
        part.astype(bf16).reshape(seq_len, HEADS, head_dim)
        for part in times(normed, qkv, biases[: 3 * model_width])
    ]
    scores = jnp.einsum("qhd,khd->hqk", queries, keys, preferred_element_type=f32) / math.sqrt(head_dim)
    causal = jnp.arange(seq_len)[:, None] >= jnp.arange(seq_len)[None, :]
    scores = jnp.where(causal, scores, -1e30)
    weights = jax.nn.softmax(scores, axis=-1).astype(bf16)
    attended = jnp.einsum("hqk,khd->qhd", weights, values, preferred_element_type=f32)
    attended = attended.astype(bf16).reshape(seq_len, model_width)
    stream = (
        stream
        + jnp.dot(attended, w_out, preferred_element_type=f32)
        + biases[3 * model_width : 4 * model_width]
    )
    normed = layer_norm(stream, norm_params[2], norm_params[3]).astype(bf16)
    inner_in = times(normed, fc, biases[4 * model_width : 4 * model_width + hidden_units])
    activated = jnp.concatenate(
        [jax.nn.gelu(part, approximate=True).astype(bf16) for part in inner_in], axis=1
    )
    return (
        stream
        + jnp.dot(activated, w_proj, preferred_element_type=f32)
        + biases[4 * model_width + hidden_units :]
    )


def orthonormal(left_factor):
    gram_matrix = jnp.dot(left_factor.T, left_factor, precision=largest_values)
    cholesky_low = jnp.linalg.cholesky(gram_matrix)
    return lax.linalg.triangular_solve(
        cholesky_low, left_factor, left_side=False, lower=True, transpose_a=True
    )


def times_factor(values, factor, numbers):
    rank = factor.shape[1]
    pieces = jnp.concatenate(split_three(factor), axis=1)
    product = lax.dot_general(values, pieces, numbers, preferred_element_type=f32)
    return product[:, :rank] + product[:, rank : 2 * rank] + product[:, 2 * rank :]


def per_device(
    residual,
    valid_mask,
    top_idx,
    aux_idx,
    dead_flags,
    norm_params,
    biases,
    w_qkv,
    w_out,
    w_fc,
    w_proj,
    head_table,
    w_enc,
    encoder_bias_vec,
    w_dec,
    decoder_bias_vec,
    mom_enc,
    mom_benc,
    mom_dec,
    mom_bdec,
    q_enc,
    q_dec,
    err_enc,
    err_dec,
):
    lat_count = lax.axis_size("lat")
    rep_count = lax.axis_size("rep")
    lat_index = lax.axis_index("lat")
    model_width = residual.shape[1]
    hidden_units = w_fc.shape[1]
    lat_dev = w_enc.shape[1]
    top_count, aux_count = top_idx.shape[1], aux_idx.shape[1]

    def side_by_side(weight):
        return [weight[:, k : k + model_width] for k in range(0, weight.shape[1], model_width)]

    share = w_qkv.shape[0]
    stacked = jnp.concatenate(side_by_side(w_qkv) + [w_out] + side_by_side(w_fc) + [w_proj], axis=0)
    gathered = lax.all_gather(stacked, "lat", axis=0)
    squares = [
        gathered[:, k * share : (k + 1) * share].reshape(model_width, model_width)
        for k in range(4 + hidden_units // model_width)
    ]
    proj_all = gathered[:, len(squares) * share :].reshape(hidden_units, model_width)

    half = aux_count // 2
    packed = jnp.concatenate([aux_idx[:, :half] * pack_base + aux_idx[:, half:], top_idx], axis=1)
    packed = gather_tokens(packed)
    group_rows = packed.shape[0]
    ids = jnp.concatenate([packed[:, :half] // pack_base, packed[:, :half] % pack_base, packed[:, half:]], axis=1)
    ids = ids - lat_index * lat_dev
    padding = -ids.shape[1] % lanes
    ids = jnp.concatenate([ids, jnp.full((group_rows, padding), -1, jnp.int32)], axis=1)
    dead_local = lax.dynamic_slice_in_dim(dead_flags, lat_index * lat_dev, lat_dev).astype(f32)
    mask = build_mask(ids, dead_local[None, :], aux_count)

    valid_float = valid_mask.astype(f32)
    valid_total = sum_over(jnp.full((1, lanes), jnp.sum(valid_float)), ("lat", "rep"))[0, 0]
    weight_own = (valid_float / valid_total)[:, None]

    enc_weight = w_enc.astype(bf16)
    dec_weight = w_dec.astype(bf16)
    err_left_enc = jnp.dot(err_enc[0], q_enc, precision=largest_values)
    err_left_dec = lax.dot_general(err_dec[0], q_dec, contract_rows, precision=largest_values)

    stream = frozen_block(
        residual, norm_params, biases, squares[:3], squares[3], squares[4:], proj_all
    )
    centered_group = gather_tokens((stream - decoder_bias_vec).astype(bf16))

    def final_norm(values):
        return layer_norm(values, norm_params[4], norm_params[5])

    orig_normed = final_norm(stream)
    orig_group = gather_tokens(orig_normed.astype(bf16))

    mask_top = (mask == 1.0) | (mask == 3.0)
    mask_aux = mask >= 2.0
    nothing = jnp.zeros((), bf16)
    code = (
        jnp.dot(centered_group, enc_weight, preferred_element_type=f32) + encoder_bias_vec
    ).astype(bf16)
    topk_code = jnp.where(mask_top, code, nothing)
    auxiliary_code = jnp.where(mask_aux, code, nothing)
    rebuilt_input = (
        scatter_sum(jnp.dot(topk_code, dec_weight, preferred_element_type=f32)) + decoder_bias_vec
    )
    rec_float, norm_back = jax.vjp(final_norm, rebuilt_input)
    rec_group = gather_tokens(rec_float.astype(bf16))

    orig_mean, orig_lse = head_part(orig_group, head_table)
    auxiliary_rebuilt = scatter_sum(jnp.dot(auxiliary_code, dec_weight, preferred_element_type=f32))
    orig_mean, orig_lse = scatter_mean(orig_mean, orig_lse)

    resid_err = stream - rebuilt_input - auxiliary_rebuilt
    aux_pull = -(2.0 * aux_weight) * weight_own * resid_err
    aux_group = gather_tokens(aux_pull.astype(bf16))

    rec_mean, rec_lse = head_part(rec_group, head_table)
    rec_mean, rec_lse = scatter_mean(rec_mean, rec_lse)

    gap = orig_normed.astype(bf16).astype(f32) - rec_float.astype(bf16).astype(f32)
    kl_own = jnp.sum(gap * orig_mean, axis=1) - orig_lse[:, 0] + rec_lse[:, 0]
    per_token = kl_own + aux_weight * jnp.sum(resid_err * resid_err, axis=1)
    loss_own = jnp.sum(valid_float * per_token)
    (grad_head,) = norm_back(weight_own * (rec_mean - orig_mean))
    grad_recon = (grad_head + aux_pull).astype(bf16)
    recon_group = gather_tokens(grad_recon)

    aux_back = lax.dot_general(aux_group, dec_weight, contract_cols, preferred_element_type=f32)
    grad_auxpre = jnp.where(mask_aux, aux_back.astype(bf16), nothing)
    top_back = lax.dot_general(recon_group, dec_weight, contract_cols, preferred_element_type=f32)
    grad_pre = jnp.where(mask_top, top_back.astype(bf16), nothing).astype(f32) + grad_auxpre.astype(f32)
    grad_benc = jnp.sum(grad_pre, axis=0)
    grad_pre = grad_pre.astype(bf16)

    left_enc = err_left_enc + times_factor(
        centered_group, times_factor(grad_pre, q_enc, contract_plain), contract_rows
    )
    left_dec = (
        err_left_dec
        + times_factor(recon_group, times_factor(topk_code, q_dec, contract_plain), contract_rows)
        + times_factor(aux_group, times_factor(auxiliary_code, q_dec, contract_plain), contract_rows)
    )
    grad_bdec = jnp.sum(grad_recon.astype(f32), axis=0) - jnp.dot(
        enc_weight.astype(f32), grad_benc, precision=largest_values
    )
    rank = q_enc.shape[1]
    small = jnp.concatenate(
        [left_enc.T, left_dec.T, grad_bdec[None], jnp.full((1, model_width), loss_own)], axis=0
    )
    small = sum_over(small, ("lat", "rep"))
    left_enc, left_dec = small[:rank].T, small[rank : 2 * rank].T
    grad_bdec, loss_sum = small[2 * rank], small[2 * rank + 1, 0]

    full_enc = (
        lax.dot_general(centered_group, grad_pre, contract_rows, preferred_element_type=f32) + err_enc[0]
    )
    full_dec = (
        lax.dot_general(topk_code, recon_group, contract_rows, preferred_element_type=f32)
        + lax.dot_general(auxiliary_code, aux_group, contract_rows, preferred_element_type=f32)
        + err_dec[0]
    )
    ortho_enc = orthonormal(left_enc)
    ortho_dec = orthonormal(left_dec)
    right_enc = lax.dot_general(ortho_enc, full_enc, contract_rows, precision=largest_values)
    right_dec = lax.dot_general(
        ortho_dec, full_dec, (((0,), (1,)), ((), ())), precision=largest_values
    )
    rights = sum_over(
        jnp.concatenate([right_enc, right_dec, grad_benc[None]], axis=0), ("rep",), sent_as=bf16
    )
    right_enc, right_dec, grad_benc = rights[:rank], rights[rank : 2 * rank], rights[2 * rank]

    w_enc_new, mom_enc_new, err_enc_new = final_update(
        enc_final_kernel, False, rep_count, ortho_enc.T, right_enc, full_enc, mom_enc, w_enc
    )
    w_dec_new, mom_dec_new, err_dec_new = final_update(
        dec_final_kernel, True, rep_count, ortho_dec.T, right_dec, full_dec, mom_dec, w_dec
    )
    mom_benc_new = momentum_decay * mom_benc + grad_benc
    mom_bdec_new = momentum_decay * mom_bdec + grad_bdec
    b_enc_new = encoder_bias_vec - rate_benc * mom_benc_new
    b_dec_new = decoder_bias_vec - rate_bdec * mom_bdec_new
    return (
        loss_sum,
        valid_total,
        w_enc_new,
        b_enc_new,
        w_dec_new,
        b_dec_new,
        mom_enc_new,
        mom_benc_new,
        mom_dec_new,
        mom_bdec_new,
        right_enc.T,
        right_dec.T,
        err_enc_new[None],
        err_dec_new[None],
    )


def solution(mesh):
    in_specs = (
        P(("rep", "lat"), None),
        P(("rep", "lat")),
        P(("rep", "lat"), None),
        P(("rep", "lat"), None),
        P(),
        P(),
        P(),
        P("lat", None),
        P("lat", None),
        P("lat", None),
        P("lat", None),
        P("lat", None),
        P(None, "lat"),
        P("lat"),
        P("lat", None),
        P(),
        P(None, "lat"),
        P("lat"),
        P("lat", None),
        P(),
        P("lat", None),
        P("lat", None),
        P("rep", None, "lat"),
        P("rep", "lat", None),
    )
    out_specs = (
        P(),
        P(),
        P(None, "lat"),
        P("lat"),
        P("lat", None),
        P(),
        P(None, "lat"),
        P("lat"),
        P("lat", None),
        P(),
        P("lat", None),
        P("lat", None),
        P("rep", None, "lat"),
        P("rep", "lat", None),
    )
    return jax.shard_map(
        per_device, mesh=mesh, in_specs=in_specs, out_specs=out_specs, check_vma=False
    )
```

time: 3360 us -> 627 us (0.19)
  local copies, waits for them, and re-layouts: 2160 us -> 46.3 us
  waiting for transfers between devices: 619 us -> 69.3 us
  matrix products: 378 us -> 184 us
  Pallas kernels: 0 us -> 193 us
  blocking collectives: 90.7 us -> 0 us
  starting transfers between devices: 1.03 us -> 72 us
  other arithmetic: 85.4 us -> 41.7 us
    unnamed x53 -> x236, local copies, waits for them, and re-layouts: 2110 us -> 19.8 us
    all_gather x9 -> x1, waiting for transfers between devices: 522 us -> 0.01 us  [per_device(): gathered = lax.all_gather(stacked, 'lat', axis=0)]
    pallas_call x0 -> x5, Pallas kernels: none -> 193 us  [the longest x1 81 us: build_mask(): pl.pallas_call(functools.partial(mask_kernel, tokens, hi_count, aux_count...]
    dot_general x20 -> x26, matrix products: 316 us -> 123 us  [the longest x1 18.1 us: per_device(): lax.dot_general(centered_group, grad_pre, contract_rows, preferred_elemen...]
    psum x3 -> x0, blocking collectives: 90.7 us -> none  [the longest x1 40.4 us: per_device(): lax.psum((left_enc, left_dec, grad_bdec, loss_own), ('rep', 'lat'))]
    ppermute x0 -> x90, starting transfers between devices: none -> 72 us  [swap(): return lax.ppermute(values, axis, [(i, i ^ bit) for i in range(count)])]
    ppermute x0 -> x90, waiting for transfers between devices: none -> 69.3 us  [swap(): return lax.ppermute(values, axis, [(i, i ^ bit) for i in range(count)])]
    reduce_scatter x1 -> x0, waiting for transfers between devices: 60.9 us -> none  [per_device(): lax.psum_scatter(jnp.concatenate([jnp.dot(topk_code, dec_weight, preferre...]
  transfers between devices with their start and end apart: 11 -> 91, of which waited for: 10 -> 40; matrix products, arithmetic and copies ran while one was open for 65% -> 24% of each run, Pallas kernels for 0% -> 18%
where the time goes in v1:
time: 627 us; the launch traced here: 623 us
  Pallas kernels  193 us (31%)
  matrix products  184 us (29%)
  starting transfers between devices  72 us (11%)
  waiting for transfers between devices  69.3 us (11%)
  local copies, waits for them, and re-layouts  46.3 us (7%)
  other arithmetic  41.7 us (7%)
  between operations  16.7 us (3%)
    pallas_call x1, Pallas kernels, build_mask(): pl.pallas_call(functools.partial(mask_kernel, tokens, hi_count, aux_count...  81 us
    ppermute x90, starting transfers between devices, swap(): return lax.ppermute(values, axis, [(i, i ^ bit) for i in range(count)])  72 us
    ppermute x90, waiting for transfers between devices, swap(): return lax.ppermute(values, axis, [(i, i ^ bit) for i in range(count)])  69.3 us
    pallas_call x2, Pallas kernels, head_part(): pl.pallas_call(functools.partial(head_kernel, chunk, entries // chunk), o...  59 us
    pallas_call x2, Pallas kernels, final_update(): pl.pallas_call(functools.partial(kernel, rep_count), out_shape=(jax.Shape...  52.5 us
    dot_general x1, matrix products, per_device(): lax.dot_general(topk_code, recon_group, contract_rows, preferred_element_...  22.2 us
    unnamed x236, local copies, waits for them, and re-layouts  19.8 us
    dot_general x1, matrix products, per_device(): lax.dot_general(centered_group, grad_pre, contract_rows, preferred_elemen...  18.1 us
  transfers between devices with their start and end apart: 91, of which 40 were waited for; matrix products, arithmetic and copies ran while one was open for 24% of the time, Pallas kernels for 18%

profile of v1, /device:TPU:0, one launch (start us, length us, event | category | flops | bytes accessed | tf_op | source)
XLA Modules:
  0.0 622.5 jit_solution(9124391379425810982)
XLA Ops:
  13.6 3.0 collective-permute-start.9
  24.1 2.9 collective-permute-done.17
  28.3 3.0 collective-permute-done.18
  31.3 1.6 collective-permute-start.19
  32.9 2.0 collective-permute-done.19
  34.9 2.6 collective-permute-start.20
  38.8 7.9 %convert_element_type.470 = bf16[4096,768]{1,0:T(8,128)(2,1)} convert(f32[4096,768]{1,0:T(8,128)} %w_ref.3) | non-fusion elementwise | flops 3145728 | bytes 18874368 | tf_op jit(solution)/shard_map/convert_element_type | solution.py:428
  49.1 2.9 collective-permute-done.14
  55.5 1.7 concatenate.112.ids_ref
  57.2 81.0 %build_mask.1 = bf16[1024,4096]{1,0:T(8,128)(2,1)} custom-call(s32[1024,640]{1,0:T(8,128)} %concatenate.112.ids_ref, f32[1,4096]{1,0:T(1,128)} %bitcast.650), custom_call_target="tpu_custom_call" | custom-call | flops 42949672960 | bytes 8388608 | tf_op jit(solution)/shard_map/build_mask/pallas_call | solution.py:162
  138.2 4.8 slice.728
  143.0 6.4 %fusion.232 = (bf16[8,96,768]{2,1,0:T(8,128)(2,1)S(1)}, bf16[8,96,768]{2,1,0:T(8,128)(2,1)}, bf16[8,96,768]{2,1,0:T(8,128)(2,1)}, bf16[8,96,768]{2,1,0:T(8,128)(...) fusion(bf16[8,1152,768]{2,1,0:T(8,128)(2,1)} %bitcast.614), kind=kLoop, calls=%fused_computation.616 | loop fusion | bytes 18874368 | tf_op jit(solution)/shard_map/slice | solution.py:407
  150.1 1.7 fusion.21
  153.7 1.6 fusion.20
  155.5 1.7 convolution_convert_fusion.2
  160.4 3.4 fusion.240
  168.9 4.4 compare_or_fusion
  173.3 1.6 collective-permute-start.6
  174.9 2.6 collective-permute-done.47
  179.7 1.6 collective-permute-start.50
  187.1 9.1 %add_convert_fusion = bf16[1024,4096]{1,0:T(8,128)(2,1)} fusion(f32[4096]{0:T(1024)S(1)} %copy-done.39, bf16[1024,768]{1,0:T(8,128)(2,1)S(1)} %constant_dynamic-update-slice_fusion.9, f32[768,4096]{1,0:T(8,128)S(1)} %bitcast.610), kind=kOutput, calls=%fused_computation.2 | convolution fusion | flops 6453985280 | bytes 22560768 | tf_op jit(solution)/shard_map/dot_general | solution.py:447
  196.2 12.3 %fusion.225 = f32[1024,768]{1,0:T(8,128)} fusion(bf16[4096,768]{1,0:T(8,128)(2,1)} %convert_element_type.470, bf16[1024,4096]{1,0:T(8,128)(2,1)} %add_convert_fusion, bf16[1024,4096]{1,0:T(8,128)(2,1)S(1)} %bitcast.616), kind=kOutput, calls=%fused_computation.611 | convolution fusion | flops 6450839552 | bytes 26214400 | tf_op jit(solution)/shard_map/dot_general | solution.py:458
  208.6 11.2 %fusion.14 = f32[1024,768]{1,0:T(8,128)} fusion(bf16[4096,768]{1,0:T(8,128)(2,1)} %convert_element_type.470, pred[1024,4096]{1,0:T(32,128)(4,1)S(1)} %copy-done.3, bf16[1024,4096]{1,0:T(8,128)(2,1)S(1)} %copy-done.74), kind=kOutput, calls=%fused_computation.24 | convolution fusion | flops 6446645248 | bytes 22020096 | tf_op jit(solution)/shard_map/dot_general | solution.py:452
  219.8 2.3 fusion.132
  222.1 2.3 fusion.13
  224.4 1.6 constant_dynamic-update-slice_fusion.36.normed_ref
  226.1 29.4 %head_part.3 = (f32[1024,768]{1,0:T(8,128)}, f32[1024,1]{1,0:T(8,128)}) custom-call(bf16[1024,768]{1,0:T(8,128)(2,1)} %constant_dynamic-update-slice_fusion.36.normed_ref, bf16[6656,768]{1,0:T(8,128)(2,1)} %table_ref.3), custom_call_target="tpu_custom_call" | custom-call | flops 31406948352 | bytes 14942208 | tf_op jit(solution)/shard_map/head_part/pallas_call | solution.py:222
  256.8 3.0 slice.648
  265.3 1.6 collective-permute-start.56
  271.9 1.7 multiply_add_fusion
  276.2 1.6 collective-permute-start.65
  279.8 2.7 collective-permute-done.59
  284.1 5.1 collective-permute-done.24
  292.8 2.3 collective-permute-done.25
  299.8 3.2 collective-permute-done.29
  304.1 1.9 collective-permute-start.32
  308.8 1.7 collective-permute-start.66
  315.1 29.6 %head_part.2 = (f32[1024,768]{1,0:T(8,128)}, f32[1024,1]{1,0:T(8,128)}) custom-call(bf16[1024,768]{1,0:T(8,128)(2,1)} %constant_dynamic-update-slice_fusion.27.normed_ref, bf16[6656,768]{1,0:T(8,128)(2,1)} %table_ref.3), custom_call_target="tpu_custom_call" | custom-call | flops 31406948352 | bytes 14942208 | tf_op jit(solution)/shard_map/head_part/pallas_call | solution.py:222
  346.8 1.7 slice.618
  348.9 1.7 collective-permute-start.36
  352.5 1.7 collective-permute-done.40
  356.2 1.6 collective-permute-done.38
  358.8 1.8 collective-permute-start.41
  361.0 3.5 collective-permute-done.41
  364.6 2.0 collective-permute-start.43
  369.3 2.3 collective-permute-done.39
  395.9 9.1 %convert_select_fusion.1 = bf16[1024,4096]{1,0:T(8,128)(2,1)} fusion(pred[1024,4096]{1,0:T(32,128)(4,1)S(1)} %copy-done.4, bf16[1024,768]{1,0:T(8,128)(2,1)S(1)} %constant_dynamic-update-slice_fusion.45, bf16[4096,768]{1,0:T(8,128)(2,1)S(1)} %bitcast.618), kind=kOutput, calls=%fused_computation.13 | convolution fusion | flops 6450839552 | bytes 20447232 | tf_op jit(solution)/shard_map/dot_general | solution.py:478
  405.8 13.8 %fusion.1 = (f32[4096]{0:T(1024)S(1)}, bf16[1024,4096]{1,0:T(8,128)(2,1)}) fusion(bf16[1024,4096]{1,0:T(8,128)(2,1)} %convert_select_fusion.1, bf16[1024,768]{1,0:T(8,128)(2,1)} %constant_dynamic-update-slice_fusion.54, bf16[4096,768]{1,0:T(8,128)(2,1)S(1)} %bitcast.620, bf16[1024,4096]{1,0:T(8,128)(2,1)} %build_mask.1), kind=kOutput, calls=%fused_computation.4 | convolution fusion | flops 6471806976 | bytes 33046528 | tf_op jit(solution)/shard_map/dot_general | solution.py:476
  419.6 8.3 %fusion.8 = f32[1024,24]{0,1:T(8,128)S(1)} fusion(bf16[1024,4096]{1,0:T(8,128)(2,1)} %get-tuple-element.202, bf16[1024,4096]{1,0:T(8,128)(2,1)} %convert_select_fusion.1, bf16[4096,8]{0,1:T(8,128)(2,1)S(1)} %copy-done.27, bf16[4096,8]{0,1:T(8,128)(2,1)S(1)} %copy-done.28, bf16[4096,8]{0,1:T(8,128)(2,1)S(1)} %copy-done.26), kind=kOutput, calls=%fused_computation.18 | convolution fusion | flops 218693632 | bytes 17072128 | tf_op jit(solution)/shard_map/dot_general | solution.py:362
  428.0 8.3 %fusion.23 = f32[768]{0:T(1024)S(1)} fusion(f32[4096,1]{0,1:T(1,128)S(1)} %bitcast.644, f32[768,4096]{1,0:T(8,128)} %w_ref.2), kind=kOutput, calls=%fused_computation.53 | convolution fusion | flops 40894464 | bytes 12602368 | tf_op jit(solution)/shard_map/dot_general | solution.py:491
  437.2 10.4 %fusion.155 = f32[8,768]{1,0:T(8,128)S(1)} fusion(f32[768,24]{0,1:T(8,128)S(1)} %fusion.133, f32[4096,8]{0,1:T(8,128)S(1)} %copy-done.23, f32[1,768,4096]{2,1,0:T(8,128)S(1)} %bitcast.608), kind=kOutput, calls=%fused_computation.424 | convolution fusion | flops 302008320 | bytes 12812288 | tf_op jit(solution)/shard_map/dot_general | solution.py:429
  447.6 1.8 fusion.145
  449.8 7.0 %fusion.152 = f32[8,768]{1,0:T(8,128)S(1)} fusion(f32[768,24]{0,1:T(8,128)S(1)} %fusion.145, f32[768,24]{0,1:T(8,128)S(1)} %fusion.139, f32[4096,8]{0,1:T(8,128)S(1)} %copy-done.25, f32[1,4096,768]{2,1,0:T(8,128)S(1)} %bitcast.612), kind=kOutput, calls=%fused_computation.417 | convolution fusion | flops 302026752 | bytes 12886016 | tf_op jit(solution)/shard_map/dot_general | solution.py:430
  459.1 3.6 collective-permute-done.84
  463.7 14.1 %fusion.224 = f32[4096,768]{1,0:T(8,128)} fusion(bf16[1024,768]{1,0:T(8,128)(2,1)} %constant_dynamic-update-slice_fusion.54, bf16[1024,4096]{1,0:T(8,128)(2,1)} %add_convert_fusion, bf16[1024,4096]{1,0:T(8,128)(2,1)} %build_mask.1), kind=kOutput, calls=%fused_computation.610 | convolution fusion | flops 6450839552 | bytes 30932992 | tf_op jit(solution)/shard_map/dot_general | solution.py:507
  479.0 22.2 %bitcast_add_fusion.full_ref = f32[4096,768]{1,0:T(8,128)} fusion(f32[1,4096,768]{2,1,0:T(8,128)} %param.50, f32[4096,768]{1,0:T(8,128)} %fusion.224, bf16[1024,768]{1,0:T(8,128)(2,1)S(1)} %constant_dynamic-update-slice_fusion.45, pred[1024,4096]{1,0:T(32,128)(4,1)} %compare_or_fusion, bf16[1024,4096]{1,0:T(8,128)(2,1)} %add_convert_fusion), kind=kOutput, calls=%fused_computation.6 | convolution fusion | flops 6452936704 | bytes 51904512 | tf_op jit(solution)/shard_map/dot_general | solution.py:506
  502.0 18.1 %bitcast_add_fusion.1.full_ref = f32[768,4096]{1,0:T(8,128)} fusion(f32[1,768,4096]{2,1,0:T(8,128)} %param.49, bf16[1024,768]{1,0:T(8,128)(2,1)S(1)} %copy-done.2, bf16[1024,4096]{1,0:T(8,128)(2,1)} %get-tuple-element.202, bf16[1024,4096]{1,0:T(8,128)(2,1)} %convert_select_fusion.1), kind=kOutput, calls=%fused_computation.9 | convolution fusion | flops 6462373888 | bytes 43515904 | tf_op jit(solution)/shard_map/dot_general | solution.py:503
  526.6 9.3 %convolution_convert_fusion.1 = bf16[8,4096]{1,0:T(8,128)(2,1)S(1)} fusion(f32[768,4096]{1,0:T(8,128)} %bitcast_add_fusion.1.full_ref, f32[8,768]{1,0:T(8,128)S(1)} %get-tuple-element.204), kind=kOutput, calls=%fused_computation.15 | convolution fusion | flops 302022656 | bytes 12673024 | tf_op jit(solution)/shard_map/dot_general | solution.py:512
  535.9 10.4 %convolution_convert_fusion = bf16[8,4096]{1,0:T(8,128)(2,1)S(1)} fusion(f32[4096,768]{1,0:T(8,128)S(1)} %copy-done, f32[8,768]{1,0:T(8,128)S(1)} %get-tuple-element.206), kind=kOutput, calls=%fused_computation.14 | convolution fusion | flops 302022656 | bytes 12673024 | tf_op jit(solution)/shard_map/dot_general | solution.py:513
  547.4 4.7 collective-permute-done.88
  552.1 3.3 collective-permute-start.89
  556.1 5.0 collective-permute-done.89
  563.0 26.1 %final_update.2 = (f32[768,4096]{1,0:T(8,128)}, f32[768,4096]{1,0:T(8,128)}, f32[768,4096]{1,0:T(8,128)}) custom-call(bf16[48,768]{1,0:T(8,128)(2,1)} %copy-done.32, bf16[48,4096]{1,0:T(8,128)(2,1)} %copy-done.21, f32[768,4096]{1,0:T(8,128)} %bitcast_add_fusion.1.full_ref, f32[768,4096]{1,0:T(8,128)} %mom_ref.2, f32[768,4096]{1,0:T(8,128)} %w_ref.2), custom_call_target="tpu_custom_call" | custom-call | flops 301989888 | bytes 75497472 | tf_op jit(solution)/shard_map/final_update/pallas_call | solution.py:283
  589.1 26.4 %final_update.3 = (f32[4096,768]{1,0:T(8,128)}, f32[4096,768]{1,0:T(8,128)}, f32[4096,768]{1,0:T(8,128)}) custom-call(bf16[48,768]{1,0:T(8,128)(2,1)} %copy-done.31, bf16[48,4096]{1,0:T(8,128)(2,1)} %copy-done.20, f32[4096,768]{1,0:T(8,128)} %bitcast_add_fusion.full_ref, f32[4096,768]{1,0:T(8,128)} %mom_ref.3, f32[4096,768]{1,0:T(8,128)} %w_ref.3), custom_call_target="tpu_custom_call" | custom-call | flops 301989888 | bytes 75497472 | tf_op jit(solution)/shard_map/final_update/pallas_call | solution.py:283
  (601 shorter events, 126.5 us)
Async XLA Ops:
  7.2 131.0 %all-gather.3.cloned.1.call-start = ((), (), s32[]{:S(2)}) async-start(), calls=%async_computation | async-start | bytes 15925248 | tf_op jit(solution)/shard_map/all_gather | solution.py:405
  13.6 33.8 %collective-permute-start.9 = (s32[128,288]{1,0:T(8,128)S(1)}, s32[128,288]{1,0:T(8,128)S(1)}, u32[]{:S(2)}, u32[]{:S(2)}) collective-permute-start(s32[128,288]{1,0:T(8,128)S(1)} %get-tuple-element.138), channel_id=1, source_target_pairs={{0,2},{1,3},{2,0},{3,1},{4,6},{5,7},{6,4},{7,5},{8,10},{9,11},{10,... | collective-permute-start | bytes 442376 | tf_op jit(solution)/shard_map/ppermute | solution.py:32
  16.6 32.5 %collective-permute-start.8 = (s32[128,288]{1,0:T(8,128)S(1)}, s32[128,288]{1,0:T(8,128)S(1)}, u32[]{:S(2)}, u32[]{:S(2)}) collective-permute-start(s32[128,288]{1,0:T(8,128)S(1)} %get-tuple-element.138), channel_id=1, source_target_pairs={{0,1},{1,0},{2,3},{3,2},{4,5},{5,4},{6,7},{7,6},{8,9},{9,8},{10,11... | collective-permute-start | bytes 442376 | tf_op jit(solution)/shard_map/ppermute | solution.py:32
  16.6 31.4 %collective-permute-start.11 = (s32[128,288]{1,0:T(8,128)S(1)}, s32[128,288]{1,0:T(8,128)S(1)}, u32[]{:S(2)}, u32[]{:S(2)}) collective-permute-start(s32[128,288]{1,0:T(8,128)S(1)} %get-tuple-element.138), channel_id=1, source_target_pairs={{0,4},{1,5},{2,6},{3,7},{4,0},{5,1},{6,2},{7,3},{8,12},{9,13},{10,... | collective-permute-start | bytes 442376 | tf_op jit(solution)/shard_map/ppermute | solution.py:32
  34.9 11.8 %collective-permute-start.20 = (f32[1,128]{1,0:T(1,128)S(1)}, f32[1,128]{1,0:T(1,128)S(1)}, u32[]{:S(2)}, u32[]{:S(2)}) collective-permute-start(f32[1,128]{1,0:T(1,128)S(1)} %add.719), channel_id=1, source_target_pairs={{0,16},{8,24},{16,0},{24,8},{1,17},{9,25},{17,1},{25,9},{2,18},{10... | collective-permute-start | bytes 1544 | tf_op jit(solution)/shard_map/ppermute | solution.py:32
  47.4 4.7 collective-permute-start.14
  47.9 4.7 collective-permute-start.13
  164.8 8.5 %collective-permute-start.1 = (bf16[128,768]{1,0:T(8,128)(2,1)S(1)}, bf16[128,768]{1,0:T(8,128)(2,1)S(1)}, u32[]{:S(2)}, u32[]{:S(2)}) collective-permute-start(bf16[128,768]{1,0:T(8,128)(2,1)S(1)} %get-tuple-element.125), channel_id=1, source_target_pairs={{0,2},{1,3},{2,0},{3,1},{4,6},{5,7},{6,4},{7,5},{8,10},{9,11},{10,... | collective-permute-start | bytes 589832 | tf_op jit(solution)/shard_map/ppermute | solution.py:32
  165.6 14.0 %collective-permute-start = (bf16[128,768]{1,0:T(8,128)(2,1)S(1)}, bf16[128,768]{1,0:T(8,128)(2,1)S(1)}, u32[]{:S(2)}, u32[]{:S(2)}) collective-permute-start(bf16[128,768]{1,0:T(8,128)(2,1)S(1)} %get-tuple-element.125), channel_id=1, source_target_pairs={{0,1},{1,0},{2,3},{3,2},{4,5},{5,4},{6,7},{7,6},{8,9},{9,8},{10,11... | collective-permute-start | bytes 589832 | tf_op jit(solution)/shard_map/ppermute | solution.py:32
  165.6 7.7 %collective-permute-start.3 = (bf16[128,768]{1,0:T(8,128)(2,1)S(1)}, bf16[128,768]{1,0:T(8,128)(2,1)S(1)}, u32[]{:S(2)}, u32[]{:S(2)}) collective-permute-start(bf16[128,768]{1,0:T(8,128)(2,1)S(1)} %get-tuple-element.125), channel_id=1, source_target_pairs={{0,4},{1,5},{2,6},{3,7},{4,0},{5,1},{6,2},{7,3},{8,12},{9,13},{10,... | collective-permute-start | bytes 589832 | tf_op jit(solution)/shard_map/ppermute | solution.py:32
  167.2 10.4 %collective-permute-start.47 = (bf16[128,768]{1,0:T(8,128)(2,1)S(1)}, bf16[128,768]{1,0:T(8,128)(2,1)S(1)}, u32[]{:S(2)}, u32[]{:S(2)}) collective-permute-start(bf16[128,768]{1,0:T(8,128)(2,1)S(1)} %get-tuple-element.83), channel_id=1, source_target_pairs={{0,4},{1,5},{2,6},{3,7},{4,0},{5,1},{6,2},{7,3},{8,12},{9,13},{10,... | collective-permute-start | bytes 589832 | tf_op jit(solution)/shard_map/ppermute | solution.py:32
  167.7 11.1 %collective-permute-start.45 = (bf16[128,768]{1,0:T(8,128)(2,1)S(1)}, bf16[128,768]{1,0:T(8,128)(2,1)S(1)}, u32[]{:S(2)}, u32[]{:S(2)}) collective-permute-start(bf16[128,768]{1,0:T(8,128)(2,1)S(1)} %get-tuple-element.83), channel_id=1, source_target_pairs={{0,2},{1,3},{2,0},{3,1},{4,6},{5,7},{6,4},{7,5},{8,10},{9,11},{10,... | collective-permute-start | bytes 589832 | tf_op jit(solution)/shard_map/ppermute | solution.py:32
  173.3 8.0 %collective-permute-start.44 = (bf16[128,768]{1,0:T(8,128)(2,1)S(1)}, bf16[128,768]{1,0:T(8,128)(2,1)S(1)}, u32[]{:S(2)}, u32[]{:S(2)}) collective-permute-start(bf16[128,768]{1,0:T(8,128)(2,1)S(1)} %get-tuple-element.83), channel_id=1, source_target_pairs={{0,1},{1,0},{2,3},{3,2},{4,5},{5,4},{6,7},{7,6},{8,9},{9,8},{10,11... | collective-permute-start | bytes 589832 | tf_op jit(solution)/shard_map/ppermute | solution.py:32
  173.3 8.1 %collective-permute-start.6 = (bf16[64,768]{1,0:T(8,128)(2,1)S(1)}, bf16[64,768]{1,0:T(8,128)(2,1)S(1)}, u32[]{:S(2)}, u32[]{:S(2)}) collective-permute-start(bf16[64,768]{1,0:T(8,128)(2,1)S(1)} %slice.730), channel_id=1, source_target_pairs={{0,4},{1,5},{2,6},{3,7},{4,0},{5,1},{6,2},{7,3},{8,12},{9,13},{10,... | collective-permute-start | bytes 294920 | tf_op jit(solution)/shard_map/ppermute | solution.py:32
  177.5 5.1 collective-permute-start.5
  178.8 4.9 collective-permute-start.49
  179.7 4.7 collective-permute-start.50
  185.1 39.4 %collective-permute-start.51 = (bf16[128,768]{1,0:T(8,128)(2,1)}, bf16[128,768]{1,0:T(8,128)(2,1)}, u32[]{:S(2)}, u32[]{:S(2)}) collective-permute-start(bf16[128,768]{1,0:T(8,128)(2,1)} %pad_maximum_fusion.7), channel_id=1, source_target_pairs={{0,1},{1,0},{2,3},{3,2},{4,5},{5,4},{6,7},{7,6},{8,9},{9,8},{10,11... | collective-permute-start | bytes 589832 | tf_op jit(solution)/shard_map/ppermute | solution.py:32
  259.8 12.1 %collective-permute-start.53 = (f32[4,128,768]{2,1,0:T(8,128)}, f32[4,128,768]{2,1,0:T(8,128)}, u32[]{:S(2)}, u32[]{:S(2)}) collective-permute-start(f32[4,128,768]{2,1,0:T(8,128)} %slice.648), channel_id=1, source_target_pairs={{0,1},{1,0},{2,3},{3,2},{4,5},{5,4},{6,7},{7,6},{8,9},{9,8},{10,11... | collective-permute-start | bytes 4718600 | tf_op jit(solution)/shard_map/ppermute | solution.py:32
  263.4 10.3 %collective-permute-start.62 = (f32[4,128,768]{2,1,0:T(8,128)S(1)}, f32[4,128,768]{2,1,0:T(8,128)S(1)}, u32[]{:S(2)}, u32[]{:S(2)}) collective-permute-start(f32[4,128,768]{2,1,0:T(8,128)S(1)} %slice.674), channel_id=1, source_target_pairs={{0,1},{1,0},{2,3},{3,2},{4,5},{5,4},{6,7},{7,6},{8,9},{9,8},{10,11... | collective-permute-start | bytes 4718600 | tf_op jit(solution)/shard_map/ppermute | solution.py:32
  267.6 6.6 %collective-permute-start.21 = (f32[4,128,768]{2,1,0:T(8,128)S(1)}, f32[4,128,768]{2,1,0:T(8,128)S(1)}, u32[]{:S(2)}, u32[]{:S(2)}) collective-permute-start(f32[4,128,768]{2,1,0:T(8,128)S(1)} %slice.594), channel_id=1, source_target_pairs={{0,1},{1,0},{2,3},{3,2},{4,5},{5,4},{6,7},{7,6},{8,9},{9,8},{10,11... | collective-permute-start | bytes 4718600 | tf_op jit(solution)/shard_map/ppermute | solution.py:32
  274.6 7.9 %collective-permute-start.59 = (bf16[2,128,384]{2,1,0:T(8,128)(2,1)S(1)}, bf16[2,128,384]{2,1,0:T(8,128)(2,1)S(1)}, u32[]{:S(2)}, u32[]{:S(2)}) collective-permute-start(bf16[2,128,384]{2,1,0:T(8,128)(2,1)S(1)} %pad_maximum_fusion.9), channel_id=1, source_target_pairs={{0,4},{1,5},{2,6},{3,7},{4,0},{5,1},{6,2},{7,3},{8,12},{9,13},{10,... | collective-permute-start | bytes 589832 | tf_op jit(solution)/shard_map/ppermute | solution.py:32
  275.2 16.1 %collective-permute-start.55 = (bf16[2,128,384]{2,1,0:T(8,128)(2,1)S(1)}, bf16[2,128,384]{2,1,0:T(8,128)(2,1)S(1)}, u32[]{:S(2)}, u32[]{:S(2)}) collective-permute-start(bf16[2,128,384]{2,1,0:T(8,128)(2,1)S(1)} %pad_maximum_fusion.8), channel_id=1, source_target_pairs={{0,2},{1,3},{2,0},{3,1},{4,6},{5,7},{6,4},{7,5},{8,10},{9,11},{10,... | collective-permute-start | bytes 589832 | tf_op jit(solution)/shard_map/ppermute | solution.py:32
  276.2 22.9 %collective-permute-start.65 = (bf16[2,128,384]{2,1,0:T(8,128)(2,1)S(1)}, bf16[2,128,384]{2,1,0:T(8,128)(2,1)S(1)}, u32[]{:S(2)}, u32[]{:S(2)}) collective-permute-start(bf16[2,128,384]{2,1,0:T(8,128)(2,1)S(1)} %pad_maximum_fusion.11), channel_id=1, source_target_pairs={{0,4},{1,5},{2,6},{3,7},{4,0},{5,1},{6,2},{7,3},{8,12},{9,13},{10,... | collective-permute-start | bytes 589832 | tf_op jit(solution)/shard_map/ppermute | solution.py:32
  277.8 68.3 %collective-permute-start.63 = (bf16[2,128,384]{2,1,0:T(8,128)(2,1)S(1)}, bf16[2,128,384]{2,1,0:T(8,128)(2,1)S(1)}, u32[]{:S(2)}, u32[]{:S(2)}) collective-permute-start(bf16[2,128,384]{2,1,0:T(8,128)(2,1)S(1)} %pad_maximum_fusion.10), channel_id=1, source_target_pairs={{0,2},{1,3},{2,0},{3,1},{4,6},{5,7},{6,4},{7,5},{8,10},{9,11},{10,... | collective-permute-start | bytes 589832 | tf_op jit(solution)/shard_map/ppermute | solution.py:32
  279.2 10.0 %collective-permute-start.24 = (bf16[2,128,384]{2,1,0:T(8,128)(2,1)S(1)}, bf16[2,128,384]{2,1,0:T(8,128)(2,1)S(1)}, u32[]{:S(2)}, u32[]{:S(2)}) collective-permute-start(bf16[2,128,384]{2,1,0:T(8,128)(2,1)S(1)} %pad_maximum_fusion.3), channel_id=1, source_target_pairs={{0,4},{1,5},{2,6},{3,7},{4,0},{5,1},{6,2},{7,3},{8,12},{9,13},{10,... | collective-permute-start | bytes 589832 | tf_op jit(solution)/shard_map/ppermute | solution.py:32
  282.5 7.5 %collective-permute-start.22 = (bf16[2,128,384]{2,1,0:T(8,128)(2,1)S(1)}, bf16[2,128,384]{2,1,0:T(8,128)(2,1)S(1)}, u32[]{:S(2)}, u32[]{:S(2)}) collective-permute-start(bf16[2,128,384]{2,1,0:T(8,128)(2,1)S(1)} %pad_maximum_fusion.2), channel_id=1, source_target_pairs={{0,2},{1,3},{2,0},{3,1},{4,6},{5,7},{6,4},{7,5},{8,10},{9,11},{10,... | collective-permute-start | bytes 589832 | tf_op jit(solution)/shard_map/ppermute | solution.py:32
  289.2 59.6 %collective-permute-start.61 = (bf16[1,128,384]{2,1,0:T(8,128)(2,1)}, bf16[1,128,384]{2,1,0:T(8,128)(2,1)S(1)}, u32[]{:S(2)}, u32[]{:S(2)}) collective-permute-start(bf16[1,128,384]{2,1,0:T(8,128)(2,1)} %fusion.123), channel_id=1, source_target_pairs={{0,2},{1,3},{2,0},{3,1},{4,6},{5,7},{6,4},{7,5},{8,10},{9,11},{10,... | collective-permute-start | bytes 294920 | tf_op jit(solution)/shard_map/ppermute | solution.py:32
  290.0 5.0 collective-permute-start.25
  291.4 4.7 collective-permute-start.23
  297.3 5.7 collective-permute-start.29
  297.9 6.2 collective-permute-start.27
  299.1 6.9 %collective-permute-start.26 = (bf16[128,768]{1,0:T(8,128)(2,1)S(1)}, bf16[128,768]{1,0:T(8,128)(2,1)S(1)}, u32[]{:S(2)}, u32[]{:S(2)}) collective-permute-start(bf16[128,768]{1,0:T(8,128)(2,1)S(1)} %get-tuple-element.77), channel_id=1, source_target_pairs={{0,1},{1,0},{2,3},{3,2},{4,5},{5,4},{6,7},{7,6},{8,9},{9,8},{10,11... | collective-permute-start | bytes 589832 | tf_op jit(solution)/shard_map/ppermute | solution.py:32
  303.0 4.7 collective-permute-start.31
  304.1 4.7 collective-permute-start.32
  306.0 4.4 collective-permute-start.28
  307.6 43.0 %collective-permute-start.57 = (bf16[1,128,384]{2,1,0:T(8,128)(2,1)}, bf16[1,128,384]{2,1,0:T(8,128)(2,1)S(1)}, u32[]{:S(2)}, u32[]{:S(2)}) collective-permute-start(bf16[1,128,384]{2,1,0:T(8,128)(2,1)} %fusion.121), channel_id=1, source_target_pairs={{0,4},{1,5},{2,6},{3,7},{4,0},{5,1},{6,2},{7,3},{8,12},{9,13},{10,... | collective-permute-start | bytes 294920 | tf_op jit(solution)/shard_map/ppermute | solution.py:32
  308.8 45.8 %collective-permute-start.66 = (bf16[1,128,384]{2,1,0:T(8,128)(2,1)}, bf16[1,128,384]{2,1,0:T(8,128)(2,1)S(1)}, u32[]{:S(2)}, u32[]{:S(2)}) collective-permute-start(bf16[1,128,384]{2,1,0:T(8,128)(2,1)} %fusion.127), channel_id=1, source_target_pairs={{0,2},{1,3},{2,0},{3,1},{4,6},{5,7},{6,4},{7,5},{8,10},{9,11},{10,... | collective-permute-start | bytes 294920 | tf_op jit(solution)/shard_map/ppermute | solution.py:32
  346.1 8.4 %collective-permute-start.64 = (bf16[1,128,384]{2,1,0:T(8,128)(2,1)S(1)}, bf16[1,128,384]{2,1,0:T(8,128)(2,1)S(1)}, u32[]{:S(2)}, u32[]{:S(2)}) collective-permute-start(bf16[1,128,384]{2,1,0:T(8,128)(2,1)S(1)} %fusion.125), channel_id=1, source_target_pairs={{0,4},{1,5},{2,6},{3,7},{4,0},{5,1},{6,2},{7,3},{8,12},{9,13},{10,... | collective-permute-start | bytes 294920 | tf_op jit(solution)/shard_map/ppermute | solution.py:32
  348.6 9.7 %collective-permute-start.35 = (f32[4,128,768]{2,1,0:T(8,128)S(1)}, f32[4,128,768]{2,1,0:T(8,128)S(1)}, u32[]{:S(2)}, u32[]{:S(2)}) collective-permute-start(f32[4,128,768]{2,1,0:T(8,128)S(1)} %slice.618), channel_id=1, source_target_pairs={{0,1},{1,0},{2,3},{3,2},{4,5},{5,4},{6,7},{7,6},{8,9},{9,8},{10,11... | collective-permute-start | bytes 4718600 | tf_op jit(solution)/shard_map/ppermute | solution.py:32
  358.8 5.7 collective-permute-start.41
  360.6 6.2 collective-permute-start.37
  364.6 4.7 collective-permute-start.43
  366.9 4.7 collective-permute-start.39
  374.2 6.1 collective-permute-start.78
  375.2 6.4 %collective-permute-start.76 = (bf16[128,768]{1,0:T(8,128)(2,1)S(1)}, bf16[128,768]{1,0:T(8,128)(2,1)S(1)}, u32[]{:S(2)}, u32[]{:S(2)}) collective-permute-start(bf16[128,768]{1,0:T(8,128)(2,1)S(1)} %get-tuple-element.67), channel_id=1, source_target_pairs={{0,2},{1,3},{2,0},{3,1},{4,6},{5,7},{6,4},{7,5},{8,10},{9,11},{10,... | collective-permute-start | bytes 589832 | tf_op jit(solution)/shard_map/ppermute | solution.py:32
  376.3 10.7 %collective-permute-start.75 = (bf16[128,768]{1,0:T(8,128)(2,1)S(1)}, bf16[128,768]{1,0:T(8,128)(2,1)S(1)}, u32[]{:S(2)}, u32[]{:S(2)}) collective-permute-start(bf16[128,768]{1,0:T(8,128)(2,1)S(1)} %get-tuple-element.67), channel_id=1, source_target_pairs={{0,1},{1,0},{2,3},{3,2},{4,5},{5,4},{6,7},{7,6},{8,9},{9,8},{10,11... | collective-permute-start | bytes 589832 | tf_op jit(solution)/shard_map/ppermute | solution.py:32
  376.3 7.8 %collective-permute-start.70 = (bf16[128,768]{1,0:T(8,128)(2,1)S(1)}, bf16[128,768]{1,0:T(8,128)(2,1)S(1)}, u32[]{:S(2)}, u32[]{:S(2)}) collective-permute-start(bf16[128,768]{1,0:T(8,128)(2,1)S(1)} %get-tuple-element.111), channel_id=1, source_target_pairs={{0,4},{1,5},{2,6},{3,7},{4,0},{5,1},{6,2},{7,3},{8,12},{9,13},{10,... | collective-permute-start | bytes 589832 | tf_op jit(solution)/shard_map/ppermute | solution.py:32
  377.2 8.5 %collective-permute-start.68 = (bf16[128,768]{1,0:T(8,128)(2,1)S(1)}, bf16[128,768]{1,0:T(8,128)(2,1)S(1)}, u32[]{:S(2)}, u32[]{:S(2)}) collective-permute-start(bf16[128,768]{1,0:T(8,128)(2,1)S(1)} %get-tuple-element.111), channel_id=1, source_target_pairs={{0,2},{1,3},{2,0},{3,1},{4,6},{5,7},{6,4},{7,5},{8,10},{9,11},{10,... | collective-permute-start | bytes 589832 | tf_op jit(solution)/shard_map/ppermute | solution.py:32
  380.3 9.1 %collective-permute-start.67 = (bf16[128,768]{1,0:T(8,128)(2,1)S(1)}, bf16[128,768]{1,0:T(8,128)(2,1)S(1)}, u32[]{:S(2)}, u32[]{:S(2)}) collective-permute-start(bf16[128,768]{1,0:T(8,128)(2,1)S(1)} %get-tuple-element.111), channel_id=1, source_target_pairs={{0,1},{1,0},{2,3},{3,2},{4,5},{5,4},{6,7},{7,6},{8,9},{9,8},{10,11... | collective-permute-start | bytes 589832 | tf_op jit(solution)/shard_map/ppermute | solution.py:32
  381.6 7.9 %collective-permute-start.80 = (bf16[64,768]{1,0:T(8,128)(2,1)S(1)}, bf16[64,768]{1,0:T(8,128)(2,1)S(1)}, u32[]{:S(2)}, u32[]{:S(2)}) collective-permute-start(bf16[64,768]{1,0:T(8,128)(2,1)S(1)} %slice.805), channel_id=1, source_target_pairs={{0,2},{1,3},{2,0},{3,1},{4,6},{5,7},{6,4},{7,5},{8,10},{9,11},{10,... | collective-permute-start | bytes 294920 | tf_op jit(solution)/shard_map/ppermute | solution.py:32
  384.1 6.0 collective-permute-start.81
  385.8 4.6 collective-permute-start.72
  387.0 4.7 collective-permute-start.73
  389.4 4.3 collective-permute-start.79
  390.1 5.7 collective-permute-start.71
  390.4 4.7 collective-permute-start.69
  391.7 13.3 %collective-permute-start.82 = (bf16[128,768]{1,0:T(8,128)(2,1)S(1)}, bf16[128,768]{1,0:T(8,128)(2,1)S(1)}, u32[]{:S(2)}, u32[]{:S(2)}) collective-permute-start(bf16[128,768]{1,0:T(8,128)(2,1)S(1)} %pad_maximum_fusion.13), channel_id=1, source_target_pairs={{0,1},{1,0},{2,3},{3,2},{4,5},{5,4},{6,7},{7,6},{8,9},{9,8},{10,11... | collective-permute-start | bytes 589832 | tf_op jit(solution)/shard_map/ppermute | solution.py:32
  458.3 4.4 collective-permute-start.84
  462.7 15.1 %collective-permute-start.85 = (f32[18,768]{1,0:T(8,128)S(1)}, f32[18,768]{1,0:T(8,128)S(1)}, u32[]{:S(2)}, u32[]{:S(2)}) collective-permute-start(f32[18,768]{1,0:T(8,128)S(1)} %add.808), channel_id=1, source_target_pairs={{0,4},{1,5},{2,6},{3,7},{4,0},{5,1},{6,2},{7,3},{8,12},{9,13},{10,... | collective-permute-start | bytes 165896 | tf_op jit(solution)/shard_map/ppermute | solution.py:32
  477.8 23.4 %collective-permute-start.86 = (f32[18,768]{1,0:T(8,128)S(1)}, f32[18,768]{1,0:T(8,128)S(1)}, u32[]{:S(2)}, u32[]{:S(2)}) collective-permute-start(f32[18,768]{1,0:T(8,128)S(1)} %add.809), channel_id=1, source_target_pairs={{0,8},{8,0},{16,24},{24,16},{1,9},{9,1},{17,25},{25,17},{2,10},{10... | collective-permute-start | bytes 165896 | tf_op jit(solution)/shard_map/ppermute | solution.py:32
  501.2 18.9 %collective-permute-start.87 = (f32[18,768]{1,0:T(8,128)S(1)}, f32[18,768]{1,0:T(8,128)S(1)}, u32[]{:S(2)}, u32[]{:S(2)}) collective-permute-start(f32[18,768]{1,0:T(8,128)S(1)} %add.810), channel_id=1, source_target_pairs={{0,16},{8,24},{16,0},{24,8},{1,17},{9,25},{17,1},{25,9},{2,18},{10... | collective-permute-start | bytes 165896 | tf_op jit(solution)/shard_map/ppermute | solution.py:32
  546.4 5.7 collective-permute-start.88
  552.1 9.0 %collective-permute-start.89 = (bf16[17,4096]{1,0:T(8,128)(2,1)S(1)}, bf16[17,4096]{1,0:T(8,128)(2,1)S(1)}, u32[]{:S(2)}, u32[]{:S(2)}) collective-permute-start(bf16[17,4096]{1,0:T(8,128)(2,1)S(1)} %add_convert_fusion.1), channel_id=1, source_target_pairs={{0,16},{8,24},{16,0},{24,8},{1,17},{9,25},{17,1},{25,9},{2,18},{10... | collective-permute-start | bytes 417800 | tf_op jit(solution)/shard_map/ppermute | solution.py:32
  (117 other events, 1278.4 us)
Sparse Core Ops, SparseCore 0:
  13.5 82.6 all-gather.2

commit v2 on v1

v2 whole, which is shorter than its diff:
```python
import functools
import math

import jax
import jax.numpy as jnp
from jax import lax
from jax.experimental import pallas as pl
from jax.experimental.pallas import tpu as pltpu
from jax.sharding import PartitionSpec as P

HEADS = 12

pack_base = 32768
aux_weight = 1.0 / 32.0
momentum_decay = 0.9
rate_enc = 3000.0
rate_dec = 3000.0
rate_benc = 10000.0
rate_bdec = 500.0
lanes = 128
vmem_most = 60 * 2**20
contract_cols = (((1,), (1,)), ((), ()))
contract_rows = (((0,), (0,)), ((), ()))
contract_plain = (((1,), (0,)), ((), ()))
f32 = jnp.float32
bf16 = jnp.bfloat16


def swap(values, axis, bit):
    count = lax.axis_size(axis)
    return lax.ppermute(values, axis, [(i, i ^ bit) for i in range(count)])


def bits_of(axis):
    count = lax.axis_size(axis)
    return [1 << k for k in range(count.bit_length() - 1)]


def even_order():
    count = lax.axis_size("lat")
    return [2, 6, 4, 0] if count == 8 else list(range(count - 2, -1, -2))


def gather_even(own):
    if lax.axis_size("lat") == 8:
        half = own.shape[0] // 2
        by_two, by_four = swap(own, "lat", 2), swap(own, "lat", 4)
        return jnp.concatenate(
            [by_two, swap(by_four[:half], "lat", 2), swap(by_two[half:], "lat", 4), by_four, own], axis=0
        )
    blocks = {0: own}
    for bit in bits_of("lat")[1:]:
        order = sorted(blocks)
        moved = swap(jnp.stack([blocks[j] for j in order]), "lat", bit)
        for at, j in enumerate(order):
            blocks[j ^ bit] = moved[at]
    return jnp.concatenate([blocks[j] for j in even_order()], axis=0)


def gather_tokens(own):
    even = gather_even(own)
    return even, swap(even, "lat", 1)


def scatter_paths():
    others = bits_of("lat")[1:]
    if len(others) == 2:
        return [(0, 2, others), (1, 2, others[::-1])]
    return [(0, 1, others)]


def take_blocks(values, part, parts):
    rows, width = values.shape[0] // len(even_order()), values.shape[1] // parts
    return {
        j: values[at * rows : (at + 1) * rows, part * width : (part + 1) * width]
        for at, j in enumerate(even_order())
    }


def scatter_sum(even, odd_moved):
    chip = even + odd_moved
    done = []
    for part, parts, order in scatter_paths():
        held = take_blocks(chip, part, parts)
        for bit in order:
            sent = [j for j in even_order() if j in held and j & bit]
            got = swap(jnp.concatenate([held[j] for j in sent], axis=0).astype(bf16), "lat", bit)
            rows = held[0].shape[0]
            for at, j in enumerate(sent):
                held[j ^ bit] = held[j ^ bit] + got[at * rows : (at + 1) * rows].astype(f32)
                del held[j]
        done.append(held[0])
    return jnp.concatenate(done, axis=1)


def merge(mean_a, lse_a, mean_b, lse_b):
    top = jnp.maximum(lse_a, lse_b)
    exp_a, exp_b = jnp.exp(lse_a - top), jnp.exp(lse_b - top)
    total = exp_a + exp_b
    mixed = mean_a.astype(f32) * (exp_a / total) + mean_b.astype(f32) * (exp_b / total)
    return mixed, top + jnp.log(total)


def scatter_mean(even, even_lse, odd_moved, odd_lse_moved):
    chip, chip_lse = merge(even, even_lse, odd_moved, odd_lse_moved)
    done = []
    for part, parts, order in scatter_paths():
        means, lses = take_blocks(chip, part, parts), take_blocks(chip_lse, 0, 1)
        held = {j: (means[j], lses[j]) for j in means}
        for bit in order:
            sent = [j for j in even_order() if j in held and j & bit]
            rows = held[0][0].shape[0]
            got = swap(jnp.concatenate([held[j][0] for j in sent], axis=0).astype(bf16), "lat", bit)
            got_lse = swap(jnp.concatenate([held[j][1] for j in sent], axis=0), "lat", bit)
            for at, j in enumerate(sent):
                span = slice(at * rows, (at + 1) * rows)
                held[j ^ bit] = merge(*held[j ^ bit], got[span], got_lse[span])
                del held[j]
        done.append(held[0])
    return jnp.concatenate([mean for mean, _ in done], axis=1), done[0][1]


def sum_round(values, axis, bits, sent_as=None):
    if sent_as is not None:
        values = values.astype(sent_as)
    if len(bits) == 2:
        one, two, both = (swap(values, axis, bit) for bit in (bits[0], bits[1], bits[0] | bits[1]))
        return (values.astype(f32) + one.astype(f32)) + (two.astype(f32) + both.astype(f32))
    for bit in bits:
        values = values.astype(f32) + swap(values, axis, bit).astype(f32)
    return values


untouched = pl.BlockSpec(memory_space=pl.ANY)
in_vmem = pl.BlockSpec(memory_space=pltpu.VMEM)


def dot(a, b, numbers):
    return lax.dot_general(a, b, numbers, preferred_element_type=f32)


def call(kernel, name, args, out_shape, grid=(), in_specs=None, out_specs=None, deps=(), cost=(0, 0), aliases=None, scratch=()):
    count, skipped = len(args), len(deps)

    def body(*refs):
        kernel(*refs[:count], *refs[count + skipped :])

    if in_specs is None:
        in_specs = [in_vmem] * count
        out_specs = jax.tree.map(lambda _: in_vmem, out_shape)
    flops, moved = cost
    return pl.pallas_call(
        body,
        out_shape=out_shape,
        grid=grid,
        in_specs=list(in_specs) + [untouched] * skipped,
        out_specs=out_specs,
        scratch_shapes=list(scratch),
        input_output_aliases=aliases or {},
        compiler_params=pltpu.CompilerParams(vmem_limit_bytes=vmem_most),
        cost_estimate=pl.CostEstimate(flops=flops, bytes_accessed=moved, transcendentals=0),
        name=name,
    )(*args, *deps)


def like(shape, dtype=f32):
    return jax.ShapeDtypeStruct(shape, dtype)


def clear_at_start(*refs):
    @pl.when(pl.program_id(0) == 0)
    def _():
        for ref in refs:
            ref[...] = jnp.zeros_like(ref)


def mask_kernel(tokens, hi_count, aux_count, ids_ref, dead_ref, own_ref, partner_ref, scratch):
    width = ids_ref.shape[1]
    hi_rows = lax.broadcasted_iota(jnp.int32, (2 * hi_count, width), 0)
    lo_rows = lax.broadcasted_iota(jnp.int32, (lanes, width), 0)
    is_aux = lax.broadcasted_iota(jnp.int32, (2 * hi_count, width), 1) < aux_count
    weight = jnp.where(is_aux, 2.0, 1.0)

    def one_token(t, carry):
        row = ids_ref[pl.ds(t, 1), :]
        hi_hot = jnp.where(hi_rows == (row >> 7), weight, 0.0).astype(bf16)
        lo_hot = jnp.where(lo_rows == (row & 127), 1.0, 0.0).astype(bf16)
        picked = lax.dot_general(hi_hot, lo_hot, contract_cols, preferred_element_type=f32)
        at = pl.multiple_of(t * 2 * hi_count, 2 * hi_count)
        scratch[pl.ds(at, 2 * hi_count), :] = picked
        return carry

    lax.fori_loop(0, tokens, one_token, 0, unroll=16)
    for hi in range(2 * hi_count):
        code = scratch[pl.ds(hi, tokens, stride=2 * hi_count), :]
        aux = jnp.where(code >= 2.0, 2.0, 0.0)
        code = (code - aux + aux * dead_ref[:, hi * lanes : (hi + 1) * lanes]).astype(bf16)
        if hi < hi_count:
            own_ref[:, hi * lanes : (hi + 1) * lanes] = code
        else:
            partner_ref[:, (hi - hi_count) * lanes : (hi - hi_count + 1) * lanes] = code


def build_mask(pair_ids, dead_pair, aux_count):
    rows, width = pair_ids.shape
    lat_dev = dead_pair.shape[1] // 2
    hi_count, tokens = lat_dev // lanes, 64
    out_block = pl.BlockSpec((tokens, lat_dev), lambda i: (i, 0))
    return pl.pallas_call(
        functools.partial(mask_kernel, tokens, hi_count, aux_count),
        out_shape=(jax.ShapeDtypeStruct((rows, lat_dev), bf16),) * 2,
        grid=(rows // tokens,),
        in_specs=[
            pl.BlockSpec((tokens, width), lambda i: (i, 0)),
            pl.BlockSpec((1, 2 * lat_dev), lambda i: (0, 0)),
        ],
        out_specs=(out_block, out_block),
        scratch_shapes=[pltpu.VMEM((tokens * 2 * hi_count, lanes), f32)],
        compiler_params=pltpu.CompilerParams(vmem_limit_bytes=vmem_most),
        cost_estimate=pl.CostEstimate(
            flops=16 * rows * 2 * lat_dev * width, bytes_accessed=4 * rows * lat_dev, transcendentals=0
        ),
        name="build_mask",
    )(pair_ids, dead_pair)


def split_three(values):
    first = values.astype(bf16)
    rest = values - first.astype(f32)
    second = rest.astype(bf16)
    return first, second, (rest - second.astype(f32)).astype(bf16)


def split_floats(values):
    return [piece.astype(f32) for piece in split_three(values)]


def high_low(values):
    high = values.astype(bf16)
    return high, (values - high.astype(f32)).astype(bf16)


def halves_kernel(by_two_ref, by_four_ref, first_ref, second_ref):
    half = by_two_ref.shape[0] // 2
    first_ref[...] = by_four_ref[:half, :]
    second_ref[...] = by_two_ref[half:, :]


def assemble_kernel(by_two_ref, first_ref, second_ref, by_four_ref, own_ref, even_ref):
    rows = own_ref.shape[0]
    even_ref[:rows, :] = by_two_ref[...]
    even_ref[rows : rows + rows // 2, :] = first_ref[...]
    even_ref[rows + rows // 2 : 2 * rows, :] = second_ref[...]
    even_ref[2 * rows : 3 * rows, :] = by_four_ref[...]
    even_ref[3 * rows :, :] = own_ref[...]


class Gather:
    def __init__(self, own):
        self.own, self.plain = own, lax.axis_size("lat") != 8
        if not self.plain:
            self.by_two, self.by_four = swap(own, "lat", 2), swap(own, "lat", 4)

    def middle(self, *deps):
        if not self.plain:
            rows, width = self.own.shape
            piece = like((rows // 2, width), self.own.dtype)
            first, second = call(halves_kernel, "halves", (self.by_two, self.by_four), (piece, piece), deps=deps)
            self.diag = swap(first, "lat", 2), swap(second, "lat", 4)

    def end(self, *deps):
        if self.plain:
            return gather_tokens(self.own)
        rows, width = self.own.shape
        even = call(
            assemble_kernel,
            "assemble",
            (self.by_two, *self.diag, self.by_four, self.own),
            like((4 * rows, width), self.own.dtype),
            deps=deps,
        )
        return even, swap(even, "lat", 1)


def reorder_kernel(blocks_ref, even_ref, odd_ref):
    me, rows = lax.axis_index("lat"), blocks_ref.shape[1]
    for at, j in enumerate(even_order()):
        even_ref[at * rows : (at + 1) * rows, :] = blocks_ref[me ^ j]
        odd_ref[at * rows : (at + 1) * rows, :] = blocks_ref[me ^ (j ^ 1)]


def gather_behind(own, *deps):
    blocks = lax.all_gather(own, "lat", axis=0)
    count, rows, width = blocks.shape
    half = like((count // 2 * rows, width), own.dtype)
    return call(reorder_kernel, "reorder", (blocks,), (half, half), deps=deps)


def weigh(lse_a, lse_b):
    top = jnp.maximum(lse_a, lse_b)
    exp_a, exp_b = jnp.exp(lse_a - top), jnp.exp(lse_b - top)
    total = exp_a + exp_b
    return exp_a / total, exp_b / total, top + jnp.log(total)


def joint(a, b, tail):
    if not tail:
        return a + b
    share_a, share_b, lse = weigh(a[:, -tail:], b[:, -tail:])
    return jnp.concatenate([a[:, :-tail] * share_a[:, :1] + b[:, :-tail] * share_b[:, :1], lse], axis=1)


def to_send(values, tail):
    if not tail:
        return values.astype(bf16)
    lane = lax.broadcasted_iota(jnp.int32, (values.shape[0], tail), 1)
    one, two, three = split_floats(values[:, -tail:])
    logs = jnp.where(lane < 32, one, jnp.where(lane < 64, two, three))
    return jnp.concatenate([values[:, :-tail], logs], axis=1).astype(bf16)


def received(ref, span, tail):
    values = ref[span, :].astype(f32)
    if not tail:
        return values
    logs = values[:, -tail:]
    lse = logs[:, :1] + logs[:, 32:33] + logs[:, 64:65]
    return jnp.concatenate([values[:, :-tail], jnp.broadcast_to(lse, logs.shape)], axis=1)


def chip_kernel(tail, even_ref, odd_ref, keep_a, send_a, keep_b, send_b):
    rows = even_ref.shape[0] // 4
    total = joint(even_ref[...], odd_ref[...], tail)
    half = (total.shape[1] - tail) // 2

    def columns(values, part):
        means = values[:, part * half : (part + 1) * half]
        return jnp.concatenate([means, values[:, -tail:]], axis=1) if tail else means

    send_a[...] = to_send(columns(total[: 2 * rows], 0), tail)
    keep_a[...] = columns(total[2 * rows :], 0)
    send_b[...] = to_send(columns(total[rows : 3 * rows], 1), tail)
    keep_b[:rows, :] = columns(total[:rows], 1)
    keep_b[rows:, :] = columns(total[3 * rows :], 1)


def hop_kernel(tail, keep_a, got_a, keep_b, got_b, next_a, send_a, next_b, send_b):
    rows = keep_a.shape[0] // 2
    early, late = slice(0, rows), slice(rows, 2 * rows)
    send_a[...] = to_send(joint(keep_a[early, :], received(got_a, late, tail), tail), tail)
    next_a[...] = joint(keep_a[late, :], received(got_a, early, tail), tail)
    send_b[...] = to_send(joint(keep_b[early, :], received(got_b, early, tail), tail), tail)
    next_b[...] = joint(keep_b[late, :], received(got_b, late, tail), tail)


def last_kernel(tail, keep_a, got_a, keep_b, got_b, total_ref):
    rows = keep_a.shape[0]
    for part, (keep, got) in enumerate(((keep_a, got_a), (keep_b, got_b))):
        total = joint(keep[...], received(got, slice(0, rows), tail), tail)
        half = total.shape[1] - tail
        total_ref[:, part * half : (part + 1) * half] = total[:, :half]
        if tail and part == 0:
            total_ref[:, 2 * half :] = total[:, half:]


class Scatter:
    def __init__(self, odd, tail=0):
        self.moved, self.tail, self.plain = swap(odd, "lat", 1), tail, lax.axis_size("lat") != 8

    def step(self, kernel, name, args, rows, width, deps):
        outs = (like((rows, width)), like((rows, width), bf16))
        self.state = call(functools.partial(kernel, self.tail), name, args, outs * 2, deps=deps)

    def chip(self, even, *deps):
        self.even = even
        if not self.plain:
            rows, width = even.shape
            self.width = (width - self.tail) // 2 + self.tail
            self.rows = rows // 4
            self.step(chip_kernel, "chip_sum", (even, self.moved), 2 * self.rows, self.width, deps)
            keep_a, send_a, keep_b, send_b = self.state
            self.pending = keep_a, swap(send_a, "lat", 2), keep_b, swap(send_b, "lat", 4)
            return send_a
        return even

    def hop(self, *deps):
        if self.plain:
            return self.even
        self.step(hop_kernel, "hop_sum", self.pending, self.rows, self.width, deps)
        keep_a, send_a, keep_b, send_b = self.state
        self.pending = keep_a, swap(send_a, "lat", 4), keep_b, swap(send_b, "lat", 2)
        return send_a

    def last(self, *deps):
        if self.plain:
            if not self.tail:
                return scatter_sum(self.even, self.moved)
            width = self.even.shape[1] - self.tail
            mean, lse = scatter_mean(
                self.even[:, :width], self.even[:, width : width + 1], self.moved[:, :width], self.moved[:, width : width + 1]
            )
            return jnp.concatenate([mean, jnp.broadcast_to(lse, (lse.shape[0], self.tail))], axis=1)
        width = 2 * (self.width - self.tail) + self.tail
        return call(
            functools.partial(last_kernel, self.tail), "last_sum", self.pending, like((self.rows, width)), deps=deps
        )


def head_kernel(chunk, chunks, normed_ref, table_ref, out_ref):
    normed = normed_ref[...]

    def logits_of(c):
        return dot(normed, table_ref[c * chunk : (c + 1) * chunk, :], contract_cols)

    def fold(values, op):
        folded = values[:, :lanes]
        for k in range(1, chunk // lanes):
            folded = op(folded, values[:, k * lanes : (k + 1) * lanes])
        return folded

    top = total = mean = None
    logits = logits_of(0)
    for c in range(chunks):
        later = logits_of(c + 1) if c + 1 < chunks else None
        chunk_top = jnp.max(fold(logits, jnp.maximum), axis=1, keepdims=True)
        new_top = chunk_top if top is None else jnp.maximum(top, chunk_top)
        grown = jnp.exp(logits - new_top).astype(bf16)
        chunk_total = fold(grown.astype(f32), jnp.add)
        chunk_mean = dot(grown, table_ref[c * chunk : (c + 1) * chunk, :], contract_plain)
        if top is None:
            total, mean = chunk_total, chunk_mean
        else:
            shrink = jnp.exp(top - new_top)
            total, mean = total * shrink + chunk_total, mean * shrink + chunk_mean
        top, logits = new_top, later
    total = jnp.sum(total, axis=1, keepdims=True)
    width = mean.shape[1]
    out_ref[:, :width] = mean / total
    out_ref[:, width:] = jnp.broadcast_to(top + jnp.log(total), (mean.shape[0], lanes))


def head_part(normed, table, *deps):
    rows, width = normed.shape
    entries = table.shape[0]
    tiles = entries // lanes
    chunk = lanes * max(d for d in range(1, 14) if tiles % d == 0)
    block = min(512, rows)
    return call(
        functools.partial(head_kernel, chunk, entries // chunk),
        "head_part",
        (normed, table),
        like((rows, width + lanes)),
        (rows // block,),
        [
            pl.BlockSpec((block, width), lambda i: (i, 0)),
            pl.BlockSpec(table.shape, lambda i: (0, 0), pipeline_mode=pl.Buffered(1)),
        ],
        pl.BlockSpec((block, width + lanes), lambda i: (i, 0)),
        deps,
        (6 * rows * entries * width, 2 * entries * width),
    )


def round_kernel(values_ref, out_ref):
    out_ref[...] = values_ref[...].astype(bf16)


def rounded(values, by_rows, *deps):
    latents = values.shape[0 if by_rows else 1]
    block = min(1024, latents)
    spec = row_block(block, values.shape[1]) if by_rows else column_block(values.shape[0], block)
    return call(
        round_kernel,
        "rounded",
        (values,),
        like(values.shape, bf16),
        (latents // block,),
        [spec],
        spec,
        deps,
        (0, 6 * values.size),
    )


def pieces_kernel(factor_ref, rows_ref, columns_ref):
    one, two, three = split_floats(factor_ref[...])
    rank, latents = one.shape
    rows_ref[...] = jnp.concatenate([one, two, three, jnp.zeros_like(one)], axis=0).astype(bf16)
    tall = jnp.concatenate([one, two, three, jnp.zeros((lanes - 3 * rank, latents), f32)], axis=0)
    columns_ref[...] = tall.T.astype(bf16)


def factor_pieces(factor, *deps):
    rank, latents = factor.shape
    block = min(1024, latents)
    return call(
        pieces_kernel,
        "factor_pieces",
        (factor,),
        (like((4 * rank, latents), bf16), like((latents, lanes), bf16)),
        (latents // block,),
        [column_block(rank, block)],
        (column_block(4 * rank, block), row_block(block, lanes)),
        deps,
        (0, 1024 * latents),
    )


def column_block(rows, block):
    return pl.BlockSpec((rows, block), lambda i: (0, i))


def row_block(block, width):
    return pl.BlockSpec((block, width), lambda i: (i, 0))


def whole_of(shape):
    return pl.BlockSpec(shape, lambda i: (0,) * len(shape))


def forward_kernel(inputs_ref, enc_ref, bias_ref, mask_ref, dec_ref, tops_ref, auxes_ref, part_ref):
    clear_at_start(part_ref)
    code = (dot(inputs_ref[...], enc_ref[...], contract_plain) + bias_ref[...]).astype(bf16)
    mask = mask_ref[...]
    nothing = jnp.zeros((), bf16)
    tops = jnp.where((mask == 1.0) | (mask == 3.0), code, nothing)
    tops_ref[...] = tops
    auxes_ref[...] = jnp.where(mask >= 2.0, code, nothing)
    part_ref[...] += dot(tops, dec_ref[...], contract_plain)


def forward(inputs, enc, bias, mask, dec, *deps):
    rows, width = inputs.shape
    latents = enc.shape[1]
    block = min(1024, latents)
    column = column_block(rows, block)
    return call(
        forward_kernel,
        "forward",
        (inputs, enc, bias, mask, dec),
        (like((rows, latents), bf16), like((rows, latents), bf16), like((rows, width))),
        (latents // block,),
        [whole_of((rows, width)), column_block(width, block), column_block(1, block), column, row_block(block, width)],
        (column, column, whole_of((rows, width))),
        deps,
        (4 * rows * latents * width, 2 * latents * (2 * width + 3 * rows)),
    )


def aux_forward_kernel(odd_ref, even_ref, dec_ref, out_ref, odd_sum, even_sum):
    clear_at_start(odd_sum, even_sum)
    odd_sum[...] += dot(odd_ref[...], dec_ref[...], contract_plain)
    even_sum[...] += dot(even_ref[...], dec_ref[...], contract_plain)

    @pl.when(pl.program_id(0) == pl.num_programs(0) - 1)
    def _():
        me, rows = lax.axis_index("lat"), out_ref.shape[1]
        for at, j in enumerate(even_order()):
            out_ref[me ^ j] = even_sum[at * rows : (at + 1) * rows, :]
            out_ref[me ^ (j ^ 1)] = odd_sum[at * rows : (at + 1) * rows, :]


def aux_forward(odd, even, dec, *deps):
    latents, width = dec.shape
    rows, count = odd.shape[0], lax.axis_size("lat")
    block = min(1024, latents)
    column, shape = column_block(rows, block), (count, 2 * rows // count, width)
    return call(
        aux_forward_kernel,
        "aux_forward",
        (odd, even, dec),
        like(shape),
        (latents // block,),
        [column, column, row_block(block, width)],
        whole_of(shape),
        deps,
        (4 * rows * latents * width, 2 * latents * (width + 2 * rows)),
        scratch=[pltpu.VMEM((rows, width), f32)] * 2,
    )


def aux_back_kernel(odd_ref, even_ref, dec_ref, odd_mask, even_mask, odd_out, even_out):
    dec = dec_ref[...]
    for grads, mask, out in ((odd_ref, odd_mask, odd_out), (even_ref, even_mask, even_out)):
        pulled = dot(grads[...], dec, contract_cols).astype(bf16)
        out[...] = jnp.where(mask[...] >= 2.0, pulled, jnp.zeros((), bf16))


def aux_back(odd, even, dec, odd_mask, even_mask, *deps):
    latents, width = dec.shape
    rows = odd.shape[0]
    block = min(1024, latents)
    column, whole = column_block(rows, block), whole_of((rows, width))
    return call(
        aux_back_kernel,
        "aux_back",
        (odd, even, dec, odd_mask, even_mask),
        (like((rows, latents), bf16),) * 2,
        (latents // block,),
        [whole, whole, row_block(block, width), column, column],
        (column, column),
        deps,
        (4 * rows * latents * width, 2 * latents * (width + 4 * rows)),
    )


def product_kernel(odd_ref, even_ref, factor_ref, odd_out, even_out):
    clear_at_start(odd_out, even_out)
    odd_out[...] += dot(odd_ref[...], factor_ref[...], contract_plain)
    even_out[...] += dot(even_ref[...], factor_ref[...], contract_plain)


def factor_products(odd, even, factor, *deps):
    rows, latents = odd.shape
    block = min(1024, latents)
    column, out = column_block(rows, block), whole_of((rows, lanes))
    return call(
        product_kernel,
        "factor_products",
        (odd, even, factor),
        (like((rows, lanes)),) * 2,
        (latents // block,),
        [column, column, row_block(block, lanes)],
        (out, out),
        deps,
        (4 * rows * latents * lanes, 4 * latents * rows),
    )


def add_left(ref, pieces, values, numbers):
    high, low = high_low(values)
    by_high, by_low = dot(pieces, high, numbers), dot(pieces, low, numbers)
    ref[...] += (by_high[:8] + by_high[8:16] + by_high[16:24]) + (by_low[:8] + by_low[8:16])


def err_left_kernel(pieces_ref, err_ref, out_ref):
    clear_at_start(out_ref)
    add_left(out_ref, pieces_ref[...], err_ref[...], contract_cols)


def err_left(pieces, err, *deps):
    width, latents = err.shape
    block = min(1024, latents)
    return call(
        err_left_kernel,
        "err_left",
        (pieces, err),
        like((8, width)),
        (latents // block,),
        [column_block(32, block), column_block(width, block)],
        whole_of((8, width)),
        deps,
        (128 * latents * width, 4 * latents * width),
    )


def part_dec_kernel(odd_codes, even_codes, odd_grads, even_grads, err_ref, pieces_ref, part_ref, left_ref):
    total = err_ref[...] + dot(odd_codes[...], odd_grads[...], contract_rows)
    total = total + dot(even_codes[...], even_grads[...], contract_rows)
    part_ref[...] = total
    clear_at_start(left_ref)
    add_left(left_ref, pieces_ref[...], total, contract_plain)


def part_dec(codes, grads, err, pieces, *deps):
    latents, width = err.shape
    rows = codes[0].shape[0]
    block = min(1024, latents)
    column, whole, big = column_block(rows, block), whole_of((rows, width)), row_block(block, width)
    return call(
        part_dec_kernel,
        "part_dec",
        (*codes, *grads, err, pieces),
        (like((latents, width)), like((8, width))),
        (latents // block,),
        [column, column, whole, whole, big, column_block(32, block)],
        (big, whole_of((8, width))),
        deps,
        (4 * rows * latents * width, latents * (8 * width + 4 * rows)),
    )


def add_dec_kernel(odd_codes, even_codes, odd_grads, even_grads, base_ref, out_ref):
    total = base_ref[...] + dot(odd_codes[...], odd_grads[...], contract_rows)
    out_ref[...] = total + dot(even_codes[...], even_grads[...], contract_rows)


def add_dec(codes, grads, base, part, parts, *deps):
    latents, width = base.shape
    rows = codes[0].shape[0]
    block = min(1024, latents // parts)
    steps = latents // parts // block
    column = pl.BlockSpec((rows, block), lambda i: (0, i + part * steps))
    big = pl.BlockSpec((block, width), lambda i: (i + part * steps, 0))
    whole = whole_of((rows, width))
    return call(
        add_dec_kernel,
        "add_dec",
        (*codes, *grads, base),
        like((latents, width)),
        (steps,),
        [column, column, whole, whole, big],
        big,
        deps,
        (4 * rows * latents * width // parts, latents * (8 * width + 4 * rows) // parts),
        aliases={4: 0},
    )


def form_enc_kernel(odd_inputs, even_inputs, odd_grads, even_grads, err_ref, out_ref):
    total = err_ref[...] + dot(odd_inputs[...], odd_grads[...], contract_rows)
    out_ref[...] = total + dot(even_inputs[...], even_grads[...], contract_rows)


def form_enc(inputs, grads, err, *deps):
    width, latents = err.shape
    rows = grads[0].shape[0]
    block = min(1024, latents)
    column, whole, big = column_block(rows, block), whole_of((rows, width)), column_block(width, block)
    return call(
        form_enc_kernel,
        "form_enc",
        (*inputs, *grads, err),
        like((width, latents)),
        (latents // block,),
        [whole, whole, column, column, big],
        big,
        deps,
        (4 * rows * latents * width, latents * (8 * width + 4 * rows)),
    )


def back_kernel(odd_ref, even_ref, dec_ref, enc_ref, odd_mask, even_mask, odd_aux, even_aux, factor_ref, *outs):
    odd_out, even_out, bias_ref, pull_ref, odd_sums, even_sums = outs
    dec, factor = dec_ref[...], factor_ref[...]
    clear_at_start(pull_ref, odd_sums, even_sums)
    nothing = jnp.zeros((), bf16)
    bias = None
    for grads, mask, aux, out, sums in (
        (odd_ref, odd_mask, odd_aux, odd_out, odd_sums),
        (even_ref, even_mask, even_aux, even_out, even_sums),
    ):
        pulled = dot(grads[...], dec, contract_cols).astype(bf16)
        mask = mask[...]
        total = jnp.where((mask == 1.0) | (mask == 3.0), pulled, nothing).astype(f32) + aux[...].astype(f32)
        column = jnp.sum(total, axis=0, keepdims=True)
        bias = column if bias is None else bias + column
        rounded = total.astype(bf16)
        out[...] = rounded
        sums[...] += dot(rounded, factor, contract_plain)
    bias_ref[...] = bias
    one, two, three = split_floats(bias)
    pieces = jnp.concatenate([one, two, three, jnp.zeros((13, bias.shape[1]), f32)], axis=0).astype(bf16)
    pull_ref[...] += dot(pieces, enc_ref[...], contract_cols)


def back_pass(odd, even, dec, enc, odd_mask, even_mask, odd_aux, even_aux, factor, *deps):
    latents, width = dec.shape
    rows = odd.shape[0]
    block = min(1024, latents)
    column, whole = column_block(rows, block), whole_of((rows, width))
    return call(
        back_kernel,
        "back_pass",
        (odd, even, dec, enc, odd_mask, even_mask, odd_aux, even_aux, factor),
        (
            like((rows, latents), bf16),
            like((rows, latents), bf16),
            like((1, latents)),
            like((16, width)),
            like((rows, lanes)),
            like((rows, lanes)),
        ),
        (latents // block,),
        [whole, whole, row_block(block, width), column_block(width, block)]
        + [column] * 4
        + [row_block(block, lanes)],
        (
            column,
            column,
            column_block(1, block),
            whole_of((16, width)),
            whole_of((rows, lanes)),
            whole_of((rows, lanes)),
        ),
        deps,
        (4 * rows * latents * (width + lanes), 2 * latents * (2 * width + 6 * rows)),
    )


def left_sums_kernel(
    rank,
    enc_odd,
    enc_even,
    odd_inputs,
    even_inputs,
    dec_odd,
    dec_even,
    odd_grads,
    even_grads,
    enc_base,
    dec_base,
    own_grads,
    pull_ref,
    loss_ref,
    out_ref,
):
    def against(products, inputs):
        total = None
        for piece in split_three(products[...]):
            wide = dot(piece, inputs[...], contract_rows)
            total = wide if total is None else total + wide
        return total[:rank] + total[rank : 2 * rank] + total[2 * rank : 3 * rank]

    out_ref[:rank, :] = enc_base[...] + against(enc_odd, odd_inputs) + against(enc_even, even_inputs)
    out_ref[rank : 2 * rank, :] = dec_base[...] + against(dec_odd, odd_grads) + against(dec_even, even_grads)
    bias = jnp.sum(own_grads[...].astype(f32), axis=0, keepdims=True)
    bias = bias - jnp.sum(pull_ref[...], axis=0, keepdims=True)
    index = lax.broadcasted_iota(jnp.int32, (8, bias.shape[1]), 0)
    out_ref[2 * rank :, :] = jnp.where(index == 0, bias, jnp.where(index == 1, loss_ref[...], 0.0))


def ortho_kernel(rank, left_ref, enc_ref, dec_ref):
    def spread(rows):
        index = lax.broadcasted_iota(jnp.int32, rows.shape, 0)
        for i in range(rank):
            unit = rows[i : i + 1, :]
            unit = unit * lax.rsqrt(jnp.sum(unit * unit, axis=1, keepdims=True))
            along = jnp.sum(rows * unit, axis=1, keepdims=True)
            rows = jnp.where(index == i, unit, jnp.where(index > i, rows - along * unit, rows))
        one, two, three = split_floats(rows)
        return jnp.concatenate([one, one, two, two, one, three], axis=0).astype(bf16)

    enc_ref[...] = spread(left_ref[:rank, :])
    dec_ref[...] = spread(left_ref[rank : 2 * rank, :])


def orthonormal(left, rank):
    shape = jax.ShapeDtypeStruct((6 * rank, left.shape[1]), bf16)
    return pl.pallas_call(
        functools.partial(ortho_kernel, rank), out_shape=(shape, shape), name="orthonormal"
    )(left)


def right_kernel(numbers, rank, left_ref, full_ref, out_ref):
    high, low = high_low(full_ref[...])
    left = left_ref[...]
    by_high, by_low = dot(left, high, numbers), dot(left, low, numbers)
    one, two, three = slice(0, rank), slice(2 * rank, 3 * rank), slice(5 * rank, 6 * rank)
    total = by_high[one] + by_high[two] + by_high[three] + by_low[one] + by_low[two]
    out_ref[...] = total.astype(out_ref.dtype)


def right_part(left, full, by_rows, dtype, *deps):
    latents, width = full.shape if by_rows else full.shape[::-1]
    rank = left.shape[0] // 6
    block = min(1024, latents)
    return call(
        functools.partial(right_kernel, contract_cols if by_rows else contract_plain, rank),
        "right_part",
        (left, full),
        like((rank, latents), dtype),
        (latents // block,),
        [whole_of(left.shape), row_block(block, width) if by_rows else column_block(width, block)],
        column_block(rank, block),
        deps,
        (24 * rank * latents * width, 4 * latents * width),
    )


def stack_kernel(right_ref, bias_ref, out_ref):
    index = lax.broadcasted_iota(jnp.int32, right_ref.shape, 0)
    bias = jnp.where(index == 0, bias_ref[...], 0.0)
    out_ref[...] = jnp.concatenate([right_ref[...], bias], axis=0).astype(bf16)


def pieces_of_right(right):
    one, two, three = split_floats(right)
    return jnp.concatenate([one, two, one, two, three, one], axis=0).astype(bf16)


def enc_final_kernel(rep_count, left_ref, right_ref, full_ref, mom_ref, w_ref, w_out, mom_out, err_out):
    approx = dot(left_ref[...], pieces_of_right(right_ref[:8, :]), contract_rows)
    err_out[...] = full_ref[...] - approx * (1.0 / rep_count)
    mom = momentum_decay * mom_ref[...] + approx
    mom_out[...] = mom
    w_out[...] = w_ref[...] - rate_enc * mom


def dec_final_kernel(rep_count, left_ref, right_ref, full_ref, mom_ref, w_ref, w_out, mom_out, err_out):
    approx = dot(pieces_of_right(right_ref[:8, :]), left_ref[...], contract_rows)
    err_out[...] = full_ref[...] - approx * (1.0 / rep_count)
    mom = momentum_decay * mom_ref[...] + approx
    mom_out[...] = mom
    step = w_ref[...] - rate_dec * mom
    w_out[...] = step * lax.rsqrt(jnp.sum(step * step, axis=1, keepdims=True) + 1e-06)


def final_update(kernel, by_rows, rep_count, left, right, full, mom, weight, *deps):
    latents, width = right.shape[1], left.shape[1]
    block = min(1024, latents)
    big = row_block(block, width) if by_rows else column_block(width, block)
    return call(
        functools.partial(kernel, rep_count),
        "final_update",
        (left, right, full, mom, weight),
        (like(full.shape),) * 3,
        (latents // block,),
        [whole_of(left.shape), column_block(right.shape[0], block), big, big, big],
        (big, big, big),
        deps,
        (2 * 48 * latents * width, 24 * latents * width),
    )


def layer_norm(values, gain_row, shift_row):
    center = values - jnp.mean(values, axis=-1, keepdims=True)
    spread = jnp.mean(center * center, axis=-1, keepdims=True)
    return center * lax.rsqrt(spread + 1e-05) * gain_row + shift_row


def frozen_block(residual, norm_params, biases, qkv, w_out, fc, w_proj):
    seq_len = residual.shape[0]
    model_width = residual.shape[1]
    hidden_units = w_proj.shape[0]
    head_dim = model_width // HEADS
    stream = residual.astype(f32)
    normed = layer_norm(stream, norm_params[0], norm_params[1]).astype(bf16)

    def times(values, parts, bias):
        width = parts[0].shape[1]
        return [
            jnp.dot(values, part, preferred_element_type=f32) + bias[k * width : (k + 1) * width]
            for k, part in enumerate(parts)
        ]

    queries, keys, values = [
        part.astype(bf16).reshape(seq_len, HEADS, head_dim)
        for part in times(normed, qkv, biases[: 3 * model_width])
    ]
    scores = jnp.einsum("qhd,khd->hqk", queries, keys, preferred_element_type=f32) / math.sqrt(head_dim)
    causal = jnp.arange(seq_len)[:, None] >= jnp.arange(seq_len)[None, :]
    scores = jnp.where(causal, scores, -1e30)
    weights = jax.nn.softmax(scores, axis=-1).astype(bf16)
    attended = jnp.einsum("hqk,khd->qhd", weights, values, preferred_element_type=f32)
    attended = attended.astype(bf16).reshape(seq_len, model_width)
    stream = (
        stream
        + jnp.dot(attended, w_out, preferred_element_type=f32)
        + biases[3 * model_width : 4 * model_width]
    )
    normed = layer_norm(stream, norm_params[2], norm_params[3]).astype(bf16)
    inner_in = times(normed, fc, biases[4 * model_width : 4 * model_width + hidden_units])
    activated = jnp.concatenate(
        [jax.nn.gelu(part, approximate=True).astype(bf16) for part in inner_in], axis=1
    )
    return (
        stream
        + jnp.dot(activated, w_proj, preferred_element_type=f32)
        + biases[4 * model_width + hidden_units :]
    )


def per_device(
    residual,
    valid_mask,
    top_idx,
    aux_idx,
    dead_flags,
    norm_params,
    biases,
    w_qkv,
    w_out,
    w_fc,
    w_proj,
    head_table,
    w_enc,
    encoder_bias_vec,
    w_dec,
    decoder_bias_vec,
    mom_enc,
    mom_benc,
    mom_dec,
    mom_bdec,
    q_enc,
    q_dec,
    err_enc,
    err_dec,
):
    rep_count = lax.axis_size("rep")
    lat_index = lax.axis_index("lat")
    model_width = residual.shape[1]
    hidden_units = w_fc.shape[1]
    lat_dev = w_enc.shape[1]
    top_count, aux_count = top_idx.shape[1], aux_idx.shape[1]
    rank = q_enc.shape[1]
    err_enc, err_dec = err_enc[0], err_dec[0]

    joined = lax.all_gather(jnp.concatenate([w_qkv, w_out, w_fc], axis=1), "lat", axis=0, tiled=True)
    proj_all = lax.all_gather(w_proj, "lat", axis=0, tiled=True)
    squares = [joined[:, k : k + model_width] for k in range(0, joined.shape[1], model_width)]

    half = aux_count // 2
    valid_float = valid_mask.astype(f32)
    packed = jnp.concatenate(
        [aux_idx[:, :half] * pack_base + aux_idx[:, half:], top_idx, valid_mask[:, None]], axis=1
    )
    gather = Gather(packed)
    enc_weight = rounded(w_enc, False, packed)
    gather.middle(enc_weight)
    dec_weight = rounded(w_dec, True, enc_weight)
    packed, _ = gather.end(dec_weight)
    picks = packed[:, half : half + top_count]
    ids = jnp.concatenate([packed[:, :half] // pack_base, packed[:, :half] % pack_base, picks], axis=1)
    own_base, partner_base = lat_index * lat_dev, (lat_index ^ 1) * lat_dev
    from_own, from_partner = ids - own_base, ids - partner_base
    ids = jnp.where(
        (from_own >= 0) & (from_own < lat_dev),
        from_own,
        jnp.where((from_partner >= 0) & (from_partner < lat_dev), from_partner + lat_dev, -1),
    )
    padding = -ids.shape[1] % lanes
    ids = jnp.concatenate([ids, jnp.full((ids.shape[0], padding), -1, jnp.int32)], axis=1)
    dead_pair = jnp.concatenate(
        [lax.dynamic_slice_in_dim(dead_flags, base, lat_dev) for base in (own_base, partner_base)]
    ).astype(f32)
    mask_even, mask_partner = build_mask(ids, dead_pair[None, :], aux_count)
    mask_odd = swap(mask_partner, "lat", 1)

    valid_total = jnp.full((1, lanes), jnp.sum(packed[:, half + top_count].astype(f32)))
    valid_total = sum_round(valid_total, "lat", [1])
    for bit in bits_of("rep"):
        valid_total = sum_round(valid_total, "rep", [bit])
    weight_own = (valid_float / valid_total[0, 0])[:, None]

    stream = frozen_block(
        residual, norm_params, biases, squares[:3], squares[3], squares[4:], proj_all
    )

    def final_norm(values):
        return layer_norm(values, norm_params[4], norm_params[5])

    gather = Gather((stream - decoder_bias_vec).astype(bf16))
    orig_normed = final_norm(stream)
    q_enc_rows, q_enc_columns = factor_pieces(q_enc.T, gather.own, valid_total)
    gather.middle(q_enc_rows)
    q_dec_rows, q_dec_columns = factor_pieces(q_dec.T, q_enc_rows)
    centered = gather.end(q_dec_rows)
    orig_blocks = orig_normed.astype(bf16)

    bias_row = encoder_bias_vec[None, :]
    tops_odd, auxes_odd, top_odd = forward(
        centered[1], enc_weight, bias_row, mask_odd, dec_weight
    )
    rebuilt = Scatter(top_odd)
    tops_even, auxes_even, top_even = forward(centered[0], enc_weight, bias_row, mask_even, dec_weight, top_odd)
    sent = rebuilt.chip(top_even)
    aux_part = aux_forward(auxes_odd, auxes_even, dec_weight, sent)
    auxiliary_rebuilt = lax.psum_scatter(aux_part, "lat", scatter_dimension=0, tiled=False)
    sent = rebuilt.hop(aux_part)
    orig_group = gather_behind(orig_blocks, aux_part)
    orig_odd = head_part(orig_group[1], head_table, sent)
    rebuilt_input = rebuilt.last(orig_odd) + decoder_bias_vec
    rec_float, norm_back = jax.vjp(final_norm, rebuilt_input)
    gather = Gather(rec_float.astype(bf16))
    orig_mean = Scatter(orig_odd, lanes)
    orig_even = head_part(orig_group[0], head_table, gather.own)
    gather.middle(orig_even)
    products_dec = factor_products(tops_odd, tops_even, q_dec_columns, orig_even)
    rec_group = gather.end(products_dec[0])
    sent = orig_mean.chip(orig_even, products_dec[0])

    resid_err = stream - rebuilt_input - auxiliary_rebuilt
    aux_pull = -(2.0 * aux_weight) * weight_own * resid_err
    aux_blocks = aux_pull.astype(bf16)

    rec_odd = head_part(rec_group[1], head_table, sent)
    rec_mean = Scatter(rec_odd, lanes)
    sent = orig_mean.hop(rec_odd)
    rec_even = head_part(rec_group[0], head_table, sent, rec_odd)
    sent = rec_mean.chip(rec_even)
    orig_mean = orig_mean.last(rec_even)
    aux_group = gather_behind(aux_blocks, rec_even)

    pre_odd, pre_even = aux_back(aux_group[1], aux_group[0], dec_weight, mask_odd, mask_even, sent)
    sent = rec_mean.hop(pre_odd)
    dec_part, left_dec = part_dec(
        (auxes_odd, auxes_even), (aux_group[1], aux_group[0]), err_dec, q_dec_rows, sent, pre_odd
    )
    rec_mean = rec_mean.last(dec_part)

    orig_lse, rec_lse = orig_mean[:, model_width], rec_mean[:, model_width]
    orig_mean, rec_mean = orig_mean[:, :model_width], rec_mean[:, :model_width]
    (grad_head,) = norm_back(weight_own * (rec_mean - orig_mean))
    grad_recon = (grad_head + aux_pull).astype(bf16)
    gather = Gather(grad_recon)
    gap = orig_normed.astype(bf16).astype(f32) - rec_float.astype(bf16).astype(f32)
    kl_own = jnp.sum(gap * orig_mean, axis=1) - orig_lse + rec_lse
    per_token = kl_own + aux_weight * jnp.sum(resid_err * resid_err, axis=1)
    loss_row = jnp.full((1, model_width), jnp.sum(valid_float * per_token))
    left_enc = err_left(q_enc_rows, err_enc, grad_recon)
    gather.middle(left_enc)
    recon_group = gather.end()

    pre_odd, pre_even, grad_benc, bias_pull, enc_odd, enc_even = back_pass(
        recon_group[1], recon_group[0], dec_weight, enc_weight, mask_odd, mask_even, pre_odd, pre_even, q_enc_columns
    )
    small = call(
        functools.partial(left_sums_kernel, rank),
        "left_sums",
        (
            enc_odd,
            enc_even,
            centered[1],
            centered[0],
            *products_dec,
            recon_group[1],
            recon_group[0],
            left_enc,
            left_dec,
            grad_recon,
            bias_pull,
            loss_row,
        ),
        like((2 * rank + 8, model_width)),
    )
    codes, grads = (tops_odd, tops_even), (recon_group[1], recon_group[0])
    full_dec = add_dec(codes, grads, dec_part, 0, 2, small)
    small = sum_round(small, "lat", [1])
    full_dec = add_dec(codes, grads, full_dec, 1, 2, small)
    small = sum_round(small, "lat", bits_of("lat")[1:])
    full_enc = form_enc((centered[1], centered[0]), (pre_odd, pre_even), err_enc, small, full_dec)
    small = sum_round(small, "rep", bits_of("rep"))
    grad_bdec, loss_sum = small[2 * rank], small[2 * rank + 1, 0]

    ortho_enc, ortho_dec = orthonormal(small[: 2 * rank], rank)
    right_enc = right_part(ortho_enc, full_enc, False, bf16)
    right_dec = right_part(ortho_dec, full_dec, True, f32, right_enc)
    right_enc = sum_round(right_enc, "rep", bits_of("rep"), sent_as=bf16)
    right_dec = call(
        stack_kernel, "stack", (right_dec, grad_benc), like((2 * rank, lat_dev), bf16), deps=(right_enc,)
    )
    right_dec = sum_round(right_dec, "rep", bits_of("rep"), sent_as=bf16)
    grad_benc = right_dec[rank]

    w_enc_new, mom_enc_new, err_enc_new = final_update(
        enc_final_kernel, False, rep_count, ortho_enc, right_enc, full_enc, mom_enc, w_enc
    )
    w_dec_new, mom_dec_new, err_dec_new = final_update(
        dec_final_kernel, True, rep_count, ortho_dec, right_dec, full_dec, mom_dec, w_dec, w_enc_new
    )
    mom_benc_new = momentum_decay * mom_benc + grad_benc
    mom_bdec_new = momentum_decay * mom_bdec + grad_bdec
    b_enc_new = encoder_bias_vec - rate_benc * mom_benc_new
    b_dec_new = decoder_bias_vec - rate_bdec * mom_bdec_new
    return (
        loss_sum,
        valid_total[0, 0],
        w_enc_new,
        b_enc_new,
        w_dec_new,
        b_dec_new,
        mom_enc_new,
        mom_benc_new,
        mom_dec_new,
        mom_bdec_new,
        right_enc.T,
        right_dec[:rank].T,
        err_enc_new[None],
        err_dec_new[None],
    )


def solution(mesh):
    in_specs = (
        P(("rep", "lat"), None),
        P(("rep", "lat")),
        P(("rep", "lat"), None),
        P(("rep", "lat"), None),
        P(),
        P(),
        P(),
        P("lat", None),
        P("lat", None),
        P("lat", None),
        P("lat", None),
        P("lat", None),
        P(None, "lat"),
        P("lat"),
        P("lat", None),
        P(),
        P(None, "lat"),
        P("lat"),
        P("lat", None),
        P(),
        P("lat", None),
        P("lat", None),
        P("rep", None, "lat"),
        P("rep", "lat", None),
    )
    out_specs = (
        P(),
        P(),
        P(None, "lat"),
        P("lat"),
        P("lat", None),
        P(),
        P(None, "lat"),
        P("lat"),
        P("lat", None),
        P(),
        P("lat", None),
        P("lat", None),
        P("rep", None, "lat"),
        P("rep", "lat", None),
    )
    return jax.shard_map(
        per_device, mesh=mesh, in_specs=in_specs, out_specs=out_specs, check_vma=False
    )
```

time: 627 us -> 575 us (0.917)
  Pallas kernels: 193 us -> 392 us
  matrix products: 184 us -> 17.6 us
  waiting for transfers between devices: 69.3 us -> 31.9 us
  local copies, waits for them, and re-layouts: 46.3 us -> 25.5 us
  other arithmetic: 41.7 us -> 23.2 us
  starting transfers between devices: 72 us -> 65.1 us
    pallas_call x4 -> x45, Pallas kernels: 112 us -> 340 us  [the longest x44 337 us: call(): pl.pallas_call(body, out_shape=out_shape, grid=grid, in_specs=list(in_spe...]
    dot_general x21 -> x0, matrix products: 171 us -> none  [the longest x1 22.2 us: per_device(): lax.dot_general(topk_code, recon_group, contract_rows, preferred_element_...]
    ppermute x90 -> x51, waiting for transfers between devices: 69.3 us -> 21.4 us  [swap(): return lax.ppermute(values, axis, [(i, i ^ bit) for i in range(count)])]
    pallas_call x1, Pallas kernels: 81 us -> 52 us  [build_mask(): pl.pallas_call(functools.partial(mask_kernel, tokens, hi_count, aux_count...]
    ppermute x90 -> x51, starting transfers between devices: 72 us -> 52.7 us  [swap(): return lax.ppermute(values, axis, [(i, i ^ bit) for i in range(count)])]
    slice x26 -> x6, local copies, waits for them, and re-layouts: 16.3 us -> 1.69 us  [the longest x2 1.05 us: per_device(): orig_lse, rec_lse = (orig_mean[:, model_width], rec_mean[:, model_width])]
    reduce_scatter x0 -> x1, starting transfers between devices: none -> 12.3 us  [per_device(): lax.psum_scatter(aux_part, 'lat', scatter_dimension=0, tiled=False)]
    convert_element_type x19 -> x4, other arithmetic: 13.7 us -> 2.34 us  [the longest x1 0.83 us: per_device(): orig_blocks = orig_normed.astype(bf16)]
  transfers between devices with their start and end apart: 91 -> 56, of which waited for: 40 -> 12; matrix products, arithmetic and copies ran while one was open for 24% -> 7% of each run, Pallas kernels for 18% -> 56%
where the time goes in v2:
time: 575 us; the launch traced here: 570 us
  Pallas kernels  392 us (68%)
  starting transfers between devices  65.1 us (11%)
  waiting for transfers between devices  31.9 us (6%)
  local copies, waits for them, and re-layouts  25.5 us (4%)
  other arithmetic  23.2 us (4%)
  matrix products  17.6 us (3%)
  between operations  14.9 us (3%)
    pallas_call x44, Pallas kernels, call(): pl.pallas_call(body, out_shape=out_shape, grid=grid, in_specs=list(in_spe...  337 us
    ppermute x51, starting transfers between devices, swap(): return lax.ppermute(values, axis, [(i, i ^ bit) for i in range(count)])  52.7 us
    pallas_call x1, Pallas kernels, build_mask(): pl.pallas_call(functools.partial(mask_kernel, tokens, hi_count, aux_count...  52 us
    ppermute x51, waiting for transfers between devices, swap(): return lax.ppermute(values, axis, [(i, i ^ bit) for i in range(count)])  21.4 us
    unnamed x125, local copies, waits for them, and re-layouts  18.1 us
    reduce_scatter x1, starting transfers between devices, per_device(): lax.psum_scatter(aux_part, 'lat', scatter_dimension=0, tiled=False)  12.3 us
    dot_general x7, matrix products, times(): jnp.dot(values, part, preferred_element_type=f32)  11.5 us
  transfers between devices with their start and end apart: 56, of which 12 were waited for; matrix products, arithmetic and copies ran while one was open for 7% of the time, Pallas kernels for 56%

profile of v2, /device:TPU:0, one launch (start us, length us, event | category | flops | bytes accessed | tf_op | source)
XLA Modules:
  0.0 569.8 jit_solution(11461791761167882347)
XLA Ops:
  7.3 2.4 pad_maximum_fusion
  10.1 3.0 collective-permute-start
  16.5 7.8 %rounded.2.refs_2_.refs_1_.refs_3_ = bf16[768,4096]{1,0:T(8,128)(2,1)} custom-call(f32[768,4096]{1,0:T(8,128)} %refs_4_.2, s32[128,289]{1,0:T(8,128)} %copy-done.7), custom_call_target="tpu_custom_call" | custom-call | bytes 18874368 | tf_op jit(solution)/shard_map/rounded/pallas_call | solution.py:152
  24.3 7.3 %rounded.3.refs_5_.refs_4_.refs_2_ = bf16[4096,768]{1,0:T(8,128)(2,1)} custom-call(f32[4096,768]{1,0:T(8,128)} %refs_4_.3, bf16[768,4096]{1,0:T(8,128)(2,1)} %rounded.2.refs_2_.refs_1_.refs_3_), custom_call_target="tpu_custom_call" | custom-call | bytes 18874368 | tf_op jit(solution)/shard_map/rounded/pallas_call | solution.py:152
  33.1 1.7 halves.4
  35.3 4.3 collective-permute-done.2.refs_1_
  40.9 2.1 assemble.4
  44.6 1.7 fusion.88
  49.9 52.0 %build_mask.1 = (bf16[512,4096]{1,0:T(8,128)(2,1)}, bf16[512,4096]{1,0:T(8,128)(2,1)}) custom-call(s32[512,640]{1,0:T(8,128)} %concatenate.33.ids_ref, f32[1,8192]{1,0:T(1,128)} %add_convert_fusion.4.dead_ref), custom_call_target="tpu_custom_call" | custom-call | flops 42949672960 | bytes 8388608 | tf_op jit(solution)/shard_map/build_mask/pallas_call | solution.py:209
  108.3 1.7 fusion.14
  111.3 1.7 fusion.101
  113.3 1.6 fusion.46
  116.7 1.6 fusion.70
  118.3 1.6 fusion.82
  120.0 3.2 fusion.102
  126.8 2.9 collective-permute-start.6
  131.8 3.2 factor_pieces.2
  135.8 1.7 halves.5
  139.7 3.2 factor_pieces.3
  144.5 2.1 assemble.5.refs_0_.refs_3_.refs_1_
  146.7 12.3 %reduce-scatter.2.cloned.1.call-start = ((), (), s32[]{:S(2)}) async-start(), calls=%async_computation.3 | async-start | bytes 3538944 | tf_op jit(solution)/shard_map/reduce_scatter | solution.py:1059
  159.9 12.4 %forward.2 = (bf16[512,4096]{1,0:T(8,128)(2,1)}, bf16[512,4096]{1,0:T(8,128)(2,1)}, f32[512,768]{1,0:T(8,128)}) custom-call(bf16[512,768]{1,0:T(8,128)(2,1)} %copy-done.4, bf16[768,4096]{1,0:T(8,128)(2,1)} %rounded.2.refs_2_.refs_1_.refs_3_, f32[1,4096]{1,0:T(1,128)} %bitcast.57, bf16[512,4096]{1,0:T(8,128)(2,1)} %collective-permute-done.12.refs_3_.refs_4_, ...), custom_call_target="tpu_custom_call" | custom-call | flops 6442450944 | bytes 25165824 | tf_op jit(solution)/shard_map/forward/pallas_call | solution.py:152
  172.9 12.4 %forward.3 = (bf16[512,4096]{1,0:T(8,128)(2,1)}, bf16[512,4096]{1,0:T(8,128)(2,1)}, f32[512,768]{1,0:T(8,128)}) custom-call(bf16[512,768]{1,0:T(8,128)(2,1)} %assemble.5.refs_0_.refs_3_.refs_1_, bf16[768,4096]{1,0:T(8,128)(2,1)} %rounded.2.refs_2_.refs_1_.refs_3_, f32[1,4096]{1,0:T(1,128)} %bitcast.58, ...), custom_call_target="tpu_custom_call" | custom-call | flops 6442450944 | bytes 25165824 | tf_op jit(solution)/shard_map/forward/pallas_call | solution.py:152
  186.5 3.0 chip_sum.3
  189.4 11.6 %aux_forward.1.refs_4_.refs_1_ = f32[8,128,768]{2,1,0:T(8,128)} custom-call(bf16[512,4096]{1,0:T(8,128)(2,1)} %get-tuple-element.96.refs_0_, bf16[512,4096]{1,0:T(8,128)(2,1)} %get-tuple-element.97.refs_1_, bf16[4096,768]{1,0:T(8,128)(2,1)} %rounded.3.refs_5_.refs_4_.refs_2_, bf16[256,384]{1,0:T(8,128)(2,1)} %get-tuple-element.93.refs_3_), custom_call_target="tpu_custom_call" | custom-call | flops 6442450944 | bytes 14680064 | tf_op jit(solution)/shard_map/aux_forward/pallas_call | solution.py:152
  204.1 2.7 reorder.2
  206.9 2.0 collective-permute-done.14.refs_1_
  209.8 2.2 hop_sum.3
  214.0 17.3 %head_part.4.refs_4_ = f32[512,896]{1,0:T(8,128)} custom-call(bf16[512,768]{1,0:T(8,128)(2,1)} %get-tuple-element.102.refs_0_, bf16[6656,768]{1,0:T(8,128)(2,1)} %refs_1_.7, bf16[128,384]{1,0:T(8,128)(2,1)} %get-tuple-element.99.refs_2_), custom_call_target="tpu_custom_call" | custom-call | flops 15703474176 | bytes 10223616 | tf_op jit(solution)/shard_map/head_part/pallas_call | solution.py:152
  232.0 1.9 last_sum.3
  236.3 10.4 %reduce-scatter.2.cloned.1.call-done = f32[1,128,768]{2,1,0:T(8,128)} async-done(((f32[8,128,768]{2,1,0:T(8,128)}), f32[1,128,768]{2,1,0:T(8,128)}) %reduce-scatter.2.cloned.1.call-update) | async-done | bytes 393232 | tf_op jit(solution)/shard_map/reduce_scatter | solution.py:1059
  250.0 17.7 %head_part.5.refs_2_.refs_3_.refs_0_ = f32[512,896]{1,0:T(8,128)} custom-call(bf16[512,768]{1,0:T(8,128)(2,1)} %get-tuple-element.103.refs_0_, bf16[6656,768]{1,0:T(8,128)(2,1)} %refs_1_.7, bf16[128,768]{1,0:T(8,128)(2,1)} %copy-done.8), custom_call_target="tpu_custom_call" | custom-call | flops 15703474176 | bytes 10223616 | tf_op jit(solution)/shard_map/head_part/pallas_call | solution.py:152
  269.1 1.7 halves.6
  272.8 6.4 %factor_products.1 = (f32[512,128]{1,0:T(8,128)}, f32[512,128]{1,0:T(8,128)}) custom-call(bf16[512,4096]{1,0:T(8,128)(2,1)} %get-tuple-element.106.refs_0_, bf16[512,4096]{1,0:T(8,128)(2,1)} %get-tuple-element.107.refs_1_, bf16[4096,128]{1,0:T(8,128)(2,1)} %get-tuple-element.108.refs_2_, f32[512,896]{1,0:T(8,128)} %head_part.5.refs_2_.refs_3_.refs_0_), custom_call_target="tpu_custom_call" | custom-call | flops 1073741824 | bytes 8388608 | tf_op jit(solution)/shard_map/factor_products/pallas_call | solution.py:152
  280.0 2.2 assemble.6.refs_0_
  284.3 3.5 chip_sum.4
  287.8 17.6 %head_part.6.refs_4_.refs_3_ = f32[512,896]{1,0:T(8,128)} custom-call(bf16[512,768]{1,0:T(8,128)(2,1)} %collective-permute-done.25.refs_0_, bf16[6656,768]{1,0:T(8,128)(2,1)} %refs_1_.7, bf16[256,512]{1,0:T(8,128)(2,1)} %get-tuple-element.111.refs_2_), custom_call_target="tpu_custom_call" | custom-call | flops 15703474176 | bytes 10223616 | tf_op jit(solution)/shard_map/head_part/pallas_call | solution.py:152
  307.9 6.3 %collective-permute-done.23.refs_1_ = bf16[256,512]{1,0:T(8,128)(2,1)S(1)} collective-permute-done((bf16[256,512]{1,0:T(8,128)(2,1)S(1)}, bf16[256,512]{1,0:T(8,128)(2,1)S(1)}, u32[]{:S(2)}, u32[]{:S(2)}) %collective-permute-start.23) | collective-permute-done | bytes 262176 | tf_op jit(solution)/shard_map/ppermute | solution.py:31
  316.0 2.8 hop_sum.4
  320.8 17.6 %head_part.7.refs_0_.refs_1_.refs_4_ = f32[512,896]{1,0:T(8,128)} custom-call(bf16[512,768]{1,0:T(8,128)(2,1)} %assemble.6.refs_0_, bf16[6656,768]{1,0:T(8,128)(2,1)} %refs_1_.7, bf16[128,512]{1,0:T(8,128)(2,1)} %get-tuple-element.114.refs_2_, f32[512,896]{1,0:T(8,128)} %head_part.6.refs_4_.refs_3_), custom_call_target="tpu_custom_call" | custom-call | flops 15703474176 | bytes 10223616 | tf_op jit(solution)/shard_map/head_part/pallas_call | solution.py:152
  339.1 2.2 last_sum.5
  341.3 2.7 reorder.3
  345.2 3.6 chip_sum.5
  350.8 12.5 %aux_back.1 = (bf16[512,4096]{1,0:T(8,128)(2,1)}, bf16[512,4096]{1,0:T(8,128)(2,1)}) custom-call(bf16[512,768]{1,0:T(8,128)(2,1)} %get-tuple-element.119.refs_0_.refs_2_, bf16[512,768]{1,0:T(8,128)(2,1)} %get-tuple-element.120.refs_1_.refs_3_, bf16[4096,768]{1,0:T(8,128)(2,1)} %rounded.3.refs_5_.refs_4_.refs_2_, ...), custom_call_target="tpu_custom_call" | custom-call | flops 6442450944 | bytes 23068672 | tf_op jit(solution)/shard_map/aux_back/pallas_call | solution.py:152
  364.1 2.8 hop_sum.5
  368.9 16.7 %part_dec.1 = (f32[4096,768]{1,0:T(8,128)}, f32[8,768]{1,0:T(8,128)}) custom-call(bf16[512,4096]{1,0:T(8,128)(2,1)} %get-tuple-element.96.refs_0_, bf16[512,4096]{1,0:T(8,128)(2,1)} %get-tuple-element.97.refs_1_, bf16[512,768]{1,0:T(8,128)(2,1)} %get-tuple-element.119.refs_0_.refs_2_, bf16[512,768]{1,0:T(8,128)(2,1)} %get-tuple-element.120.refs_1_.refs_3_, ...), custom_call_target="tpu_custom_call" | custom-call | flops 6442450944 | bytes 33554432 | tf_op jit(solution)/shard_map/part_dec/pallas_call | solution.py:152
  386.3 2.3 last_sum.4
  393.5 7.8 %err_left.1.refs_2_.refs_8_ = f32[8,768]{1,0:T(8,128)} custom-call(bf16[32,4096]{1,0:T(8,128)(2,1)} %get-tuple-element.84.refs_2_.refs_1_.refs_0_, f32[768,4096]{1,0:T(8,128)} %bitcast.40, bf16[128,768]{1,0:T(8,128)(2,1)} %copy-done.3), custom_call_target="tpu_custom_call" | custom-call | flops 402653184 | bytes 12582912 | tf_op jit(solution)/shard_map/err_left/pallas_call | solution.py:152
  402.6 1.7 halves.7
  406.4 2.8 collective-permute-done.35.refs_1_
  410.5 2.2 assemble.7.refs_1_.refs_7_.refs_3_
  416.0 18.0 %back_pass.1 = (bf16[512,4096]{1,0:T(8,128)(2,1)}, bf16[512,4096]{1,0:T(8,128)(2,1)}, f32[1,4096]{1,0:T(1,128)}, f32[16,768]{1,0:T(8,128)}, f32[512,128]{1,0:T(8,128)}, /*index=5*/f32[512,128]{1,0:T(8,128)}) custom-call(bf16[512,768]{1,0:T(8,128)(2,1)} %copy-done.1, bf16[512,768]{1,0:T(8,128)(2,1)} %assemble.7.refs_1_.refs_7_.refs_3_, ...), custom_call_target="tpu_custom_call" | custom-call | flops 7516192768 | bytes 37748736 | tf_op jit(solution)/shard_map/back_pass/pallas_call | solution.py:152
  435.3 4.3 left_sums.1.refs_5_
  439.7 8.6 %add_dec.2.refs_4_ = f32[4096,768]{1,0:T(8,128)} custom-call(bf16[512,4096]{1,0:T(8,128)(2,1)} %get-tuple-element.106.refs_0_, bf16[512,4096]{1,0:T(8,128)(2,1)} %get-tuple-element.107.refs_1_, bf16[512,768]{1,0:T(8,128)(2,1)} %copy-done.1, bf16[512,768]{1,0:T(8,128)(2,1)} %assemble.7.refs_1_.refs_7_.refs_3_, ...), custom_call_target="tpu_custom_call", output_to_operand_aliasing={{}: (4, {})} | custom-call | flops 3221225472 | bytes 16777216 | tf_op jit(solution)/shard_map/add_dec/pallas_call | solution.py:152
  452.0 8.9 %add_dec.3.refs_6_.refs_1_.refs_2_ = f32[4096,768]{1,0:T(8,128)} custom-call(bf16[512,4096]{1,0:T(8,128)(2,1)} %get-tuple-element.106.refs_0_, bf16[512,4096]{1,0:T(8,128)(2,1)} %get-tuple-element.107.refs_1_, bf16[512,768]{1,0:T(8,128)(2,1)} %copy-done.1, bf16[512,768]{1,0:T(8,128)(2,1)} %assemble.7.refs_1_.refs_7_.refs_3_, ...), custom_call_target="tpu_custom_call", output_to_operand_aliasing={{}: (4, {})} | custom-call | flops 3221225472 | bytes 16777216 | tf_op jit(solution)/shard_map/add_dec/pallas_call | solution.py:152
  463.3 2.4 collective-permute-start.43
  466.2 15.2 %form_enc.1.refs_1_.refs_2_ = f32[768,4096]{1,0:T(8,128)} custom-call(bf16[512,768]{1,0:T(8,128)(2,1)} %copy-done.4, bf16[512,768]{1,0:T(8,128)(2,1)} %assemble.5.refs_0_.refs_3_.refs_1_, bf16[512,4096]{1,0:T(8,128)(2,1)} %get-tuple-element.140.refs_2_, bf16[512,4096]{1,0:T(8,128)(2,1)} %get-tuple-element.141.refs_3_, f32[768,4096]{1,0:T(8,128)} %bitcast.41, ...), custom_call_target="tpu_custom_call" | custom-call | flops 6442450944 | bytes 33554432 | tf_op jit(solution)/shard_map/form_enc/pallas_call | solution.py:152
  483.0 2.8 orthonormal.1
  485.8 7.0 %right_part.2.refs_2_ = bf16[8,4096]{1,0:T(8,128)(2,1)} custom-call(bf16[48,768]{1,0:T(8,128)(2,1)} %get-tuple-element.139.refs_0_, f32[768,4096]{1,0:T(8,128)} %form_enc.1.refs_1_.refs_2_), custom_call_target="tpu_custom_call" | custom-call | flops 603979776 | bytes 12582912 | tf_op jit(solution)/shard_map/right_part/pallas_call | solution.py:152
  493.4 3.3 collective-permute-start.46
  497.3 7.7 %right_part.3.refs_0_ = f32[8,4096]{1,0:T(8,128)} custom-call(bf16[48,768]{1,0:T(8,128)(2,1)} %get-tuple-element.143.refs_0_, f32[4096,768]{1,0:T(8,128)} %add_dec.3.refs_6_.refs_1_.refs_2_, bf16[8,4096]{1,0:T(8,128)(2,1)} %right_part.2.refs_2_), custom_call_target="tpu_custom_call" | custom-call | flops 603979776 | bytes 12582912 | tf_op jit(solution)/shard_map/right_part/pallas_call | solution.py:152
  507.4 3.8 collective-permute-start.49
  512.8 24.5 %final_update.2 = (f32[768,4096]{1,0:T(8,128)}, f32[768,4096]{1,0:T(8,128)}, f32[768,4096]{1,0:T(8,128)}) custom-call(bf16[48,768]{1,0:T(8,128)(2,1)} %get-tuple-element.139.refs_0_, f32[8,4096]{1,0:T(8,128)} %add_add_fusion.2.refs_1_.refs_2_, f32[768,4096]{1,0:T(8,128)} %form_enc.1.refs_1_.refs_2_, f32[768,4096]{1,0:T(8,128)} %refs_3_.2, f32[768,4096]{1,0:T(8,128)} %refs_4_.2), custom_call_target="tpu_custom_call" | custom-call | flops 301989888 | bytes 75497472 | tf_op jit(solution)/shard_map/final_update/pallas_call | solution.py:152
  538.2 24.3 %final_update.3 = (f32[4096,768]{1,0:T(8,128)}, f32[4096,768]{1,0:T(8,128)}, f32[4096,768]{1,0:T(8,128)}) custom-call(bf16[48,768]{1,0:T(8,128)(2,1)} %get-tuple-element.143.refs_0_, f32[16,4096]{1,0:T(8,128)} %copy-done.13, f32[4096,768]{1,0:T(8,128)} %add_dec.3.refs_6_.refs_1_.refs_2_, f32[4096,768]{1,0:T(8,128)} %refs_3_.3, f32[4096,768]{1,0:T(8,128)} %refs_4_.3, ...), custom_call_target="tpu_custom_call" | custom-call | flops 301989888 | bytes 75497472 | tf_op jit(solution)/shard_map/final_update/pallas_call | solution.py:152
  (299 shorter events, 95.8 us)
Async XLA Ops:
  7.2 97.5 %all-gather.7.cloned.1.call-start = ((), (), s32[]{:S(2)}) async-start(), calls=%async_computation.1 | async-start | bytes 10616832 | tf_op jit(solution)/shard_map/all_gather | solution.py:999
  9.7 110.3 %all-gather.9.cloned.1.call-start = ((), (), s32[]{:S(2)}) async-start(), calls=%async_computation.2 | async-start | bytes 5308416 | tf_op jit(solution)/shard_map/all_gather | solution.py:1000
  10.1 21.6 %collective-permute-start = (s32[128,289]{1,0:T(8,128)S(1)}, s32[128,289]{1,0:T(8,128)S(1)}, u32[]{:S(2)}, u32[]{:S(2)}) collective-permute-start(s32[128,289]{1,0:T(8,128)S(1)} %pad_add_fusion.1.refs_1_.refs_4_), channel_id=1, source_target_pairs={{0,2},{1,3},{2,0},{3,1},{4,6},{5,7},{6,4},{7,5},{8,10},{9,11},{10,... | collective-permute-start | bytes 443912 | tf_op jit(solution)/shard_map/ppermute | solution.py:31
  13.1 18.6 %collective-permute-start.1 = (s32[128,289]{1,0:T(8,128)S(1)}, s32[128,289]{1,0:T(8,128)S(1)}, u32[]{:S(2)}, u32[]{:S(2)}) collective-permute-start(s32[128,289]{1,0:T(8,128)S(1)} %pad_add_fusion.1.refs_1_.refs_4_), channel_id=1, source_target_pairs={{0,4},{1,5},{2,6},{3,7},{4,0},{5,1},{6,2},{7,3},{8,12},{9,13},{10,... | collective-permute-start | bytes 443912 | tf_op jit(solution)/shard_map/ppermute | solution.py:31
  14.7 189.4 %all-gather.11.cloned.1.call-start = ((), (), s32[]{:S(2)}) async-start(), calls=%async_computation.4 | async-start | bytes 1769472 | tf_op jit(solution)/shard_map/all_gather | solution.py:293
  34.8 4.8 collective-permute-start.2
  35.3 4.8 collective-permute-start.3
  47.0 55.4 %collective-permute-start.4 = (f32[1,128]{1,0:T(1,128)S(1)}, f32[1,128]{1,0:T(1,128)S(1)}, u32[]{:S(2)}, u32[]{:S(2)}) collective-permute-start(f32[1,128]{1,0:T(1,128)S(1)} %broadcast_in_dim.29), channel_id=1, source_target_pairs={{0,1},{1,0},{2,3},{3,2},{4,5},{5,4},{6,7},{7,6},{8,9},{9,8},{10,11... | collective-permute-start | bytes 1544 | tf_op jit(solution)/shard_map/ppermute | solution.py:31
  101.9 57.1 %collective-permute-start.12 = (bf16[512,4096]{1,0:T(8,128)(2,1)}, bf16[512,4096]{1,0:T(8,128)(2,1)}, u32[]{:S(2)}, u32[]{:S(2)}) collective-permute-start(bf16[512,4096]{1,0:T(8,128)(2,1)} %get-tuple-element.89), channel_id=1, source_target_pairs={{0,1},{1,0},{2,3},{3,2},{4,5},{5,4},{6,7},{7,6},{8,9},{9,8},{10,11... | collective-permute-start | bytes 12582920 | tf_op jit(solution)/shard_map/ppermute | solution.py:31
  103.0 23.1 %collective-permute-start.5 = (f32[1,128]{1,0:T(1,128)S(1)}, f32[1,128]{1,0:T(1,128)S(1)}, u32[]{:S(2)}, u32[]{:S(2)}) collective-permute-start(f32[1,128]{1,0:T(1,128)S(1)} %broadcast_add_fusion), channel_id=1, source_target_pairs={{0,8},{8,0},{16,24},{24,16},{1,9},{9,1},{17,25},{25,17},{2,10},{10... | collective-permute-start | bytes 1544 | tf_op jit(solution)/shard_map/ppermute | solution.py:31
  124.3 10.7 %collective-permute-start.7 = (bf16[128,768]{1,0:T(8,128)(2,1)S(1)}, bf16[128,768]{1,0:T(8,128)(2,1)S(1)}, u32[]{:S(2)}, u32[]{:S(2)}) collective-permute-start(bf16[128,768]{1,0:T(8,128)(2,1)S(1)} %get-tuple-element.172.refs_1_.refs_4_), channel_id=1, source_target_pairs={{0,2},{1,3},{2,0},{3,1},{4,6},{5,7},{6,4},{7,5},{8,10},{9,11},{10,... | collective-permute-start | bytes 589832 | tf_op jit(solution)/shard_map/ppermute | solution.py:31
  125.7 9.4 %collective-permute-start.8 = (bf16[128,768]{1,0:T(8,128)(2,1)S(1)}, bf16[128,768]{1,0:T(8,128)(2,1)S(1)}, u32[]{:S(2)}, u32[]{:S(2)}) collective-permute-start(bf16[128,768]{1,0:T(8,128)(2,1)S(1)} %get-tuple-element.172.refs_1_.refs_4_), channel_id=1, source_target_pairs={{0,4},{1,5},{2,6},{3,7},{4,0},{5,1},{6,2},{7,3},{8,12},{9,13},{10,... | collective-permute-start | bytes 589832 | tf_op jit(solution)/shard_map/ppermute | solution.py:31
  126.8 4.5 collective-permute-start.6
  137.5 5.4 collective-permute-start.10
  139.0 4.8 collective-permute-start.9
  146.7 12.3 %collective-permute-start.11 = (bf16[512,768]{1,0:T(8,128)(2,1)}, bf16[512,768]{1,0:T(8,128)(2,1)S(1)}, u32[]{:S(2)}, u32[]{:S(2)}) collective-permute-start(bf16[512,768]{1,0:T(8,128)(2,1)} %assemble.5.refs_0_.refs_3_.refs_1_), channel_id=1, source_target_pairs={{0,1},{1,0},{2,3},{3,2},{4,5},{5,4},{6,7},{7,6},{8,9},{9,8},{10,11... | collective-permute-start | bytes 2359304 | tf_op jit(solution)/shard_map/ppermute | solution.py:31
  146.7 99.9 %reduce-scatter.2.cloned.1.call-start = ((), (), s32[]{:S(2)}) async-start(), calls=%async_computation.3 | async-start | bytes 3538944 | tf_op jit(solution)/shard_map/reduce_scatter | solution.py:1059
  172.3 13.0 %collective-permute-start.13 = (f32[512,768]{1,0:T(8,128)}, f32[512,768]{1,0:T(8,128)S(1)}, u32[]{:S(2)}, u32[]{:S(2)}) collective-permute-start(f32[512,768]{1,0:T(8,128)} %get-tuple-element.90.refs_5_), channel_id=1, source_target_pairs={{0,1},{1,0},{2,3},{3,2},{4,5},{5,4},{6,7},{7,6},{8,9},{9,8},{10,11... | collective-permute-start | bytes 4718600 | tf_op jit(solution)/shard_map/ppermute | solution.py:31
  201.1 140.2 %all-gather.13.cloned.1.call-start = ((), (), s32[]{:S(2)}) async-start(), calls=%async_computation.5 | async-start | bytes 1769472 | tf_op jit(solution)/shard_map/all_gather | solution.py:293
  202.0 6.8 %collective-permute-start.14 = (bf16[256,384]{1,0:T(8,128)(2,1)S(1)}, bf16[256,384]{1,0:T(8,128)(2,1)S(1)}, u32[]{:S(2)}, u32[]{:S(2)}) collective-permute-start(bf16[256,384]{1,0:T(8,128)(2,1)S(1)} %copy-done.61), channel_id=1, source_target_pairs={{0,2},{1,3},{2,0},{3,1},{4,6},{5,7},{6,4},{7,5},{8,10},{9,11},{10,... | collective-permute-start | bytes 589832 | tf_op jit(solution)/shard_map/ppermute | solution.py:31
  202.6 6.6 %collective-permute-start.15 = (bf16[256,384]{1,0:T(8,128)(2,1)S(1)}, bf16[256,384]{1,0:T(8,128)(2,1)S(1)}, u32[]{:S(2)}, u32[]{:S(2)}) collective-permute-start(bf16[256,384]{1,0:T(8,128)(2,1)S(1)} %copy-done.60), channel_id=1, source_target_pairs={{0,4},{1,5},{2,6},{3,7},{4,0},{5,1},{6,2},{7,3},{8,12},{9,13},{10,... | collective-permute-start | bytes 589832 | tf_op jit(solution)/shard_map/ppermute | solution.py:31
  212.0 19.3 %collective-permute-start.16 = (bf16[128,384]{1,0:T(8,128)(2,1)}, bf16[128,384]{1,0:T(8,128)(2,1)S(1)}, u32[]{:S(2)}, u32[]{:S(2)}) collective-permute-start(bf16[128,384]{1,0:T(8,128)(2,1)} %get-tuple-element.99.refs_2_), channel_id=1, source_target_pairs={{0,4},{1,5},{2,6},{3,7},{4,0},{5,1},{6,2},{7,3},{8,12},{9,13},{10,... | collective-permute-start | bytes 294920 | tf_op jit(solution)/shard_map/ppermute | solution.py:31
  213.6 17.8 %collective-permute-start.17 = (bf16[128,384]{1,0:T(8,128)(2,1)}, bf16[128,384]{1,0:T(8,128)(2,1)S(1)}, u32[]{:S(2)}, u32[]{:S(2)}) collective-permute-start(bf16[128,384]{1,0:T(8,128)(2,1)} %get-tuple-element.101), channel_id=1, source_target_pairs={{0,2},{1,3},{2,0},{3,1},{4,6},{5,7},{6,4},{7,5},{8,10},{9,11},{10,... | collective-permute-start | bytes 294920 | tf_op jit(solution)/shard_map/ppermute | solution.py:31
  231.3 51.7 %collective-permute-start.22 = (f32[512,896]{1,0:T(8,128)}, f32[512,896]{1,0:T(8,128)S(1)}, u32[]{:S(2)}, u32[]{:S(2)}) collective-permute-start(f32[512,896]{1,0:T(8,128)} %head_part.4.refs_4_), channel_id=1, source_target_pairs={{0,1},{1,0},{2,3},{3,2},{4,5},{5,4},{6,7},{7,6},{8,9},{9,8},{10,11... | collective-permute-start | bytes 5505032 | tf_op jit(solution)/shard_map/ppermute | solution.py:31
  247.9 19.8 %collective-permute-start.18 = (bf16[128,768]{1,0:T(8,128)(2,1)S(1)}, bf16[128,768]{1,0:T(8,128)(2,1)S(1)}, u32[]{:S(2)}, u32[]{:S(2)}) collective-permute-start(bf16[128,768]{1,0:T(8,128)(2,1)S(1)} %get-tuple-element.170.refs_2_.refs_4_), channel_id=1, source_target_pairs={{0,2},{1,3},{2,0},{3,1},{4,6},{5,7},{6,4},{7,5},{8,10},{9,11},{10,... | collective-permute-start | bytes 589832 | tf_op jit(solution)/shard_map/ppermute | solution.py:31
  249.4 18.3 %collective-permute-start.19 = (bf16[128,768]{1,0:T(8,128)(2,1)S(1)}, bf16[128,768]{1,0:T(8,128)(2,1)S(1)}, u32[]{:S(2)}, u32[]{:S(2)}) collective-permute-start(bf16[128,768]{1,0:T(8,128)(2,1)S(1)} %get-tuple-element.170.refs_2_.refs_4_), channel_id=1, source_target_pairs={{0,4},{1,5},{2,6},{3,7},{4,0},{5,1},{6,2},{7,3},{8,12},{9,13},{10,... | collective-permute-start | bytes 589832 | tf_op jit(solution)/shard_map/ppermute | solution.py:31
  270.8 8.5 %collective-permute-start.20 = (bf16[64,768]{1,0:T(8,128)(2,1)}, bf16[64,768]{1,0:T(8,128)(2,1)S(1)}, u32[]{:S(2)}, u32[]{:S(2)}) collective-permute-start(bf16[64,768]{1,0:T(8,128)(2,1)} %get-tuple-element.104), channel_id=1, source_target_pairs={{0,2},{1,3},{2,0},{3,1},{4,6},{5,7},{6,4},{7,5},{8,10},{9,11},{10,... | collective-permute-start | bytes 294920 | tf_op jit(solution)/shard_map/ppermute | solution.py:31
  272.3 7.1 %collective-permute-start.21 = (bf16[64,768]{1,0:T(8,128)(2,1)}, bf16[64,768]{1,0:T(8,128)(2,1)S(1)}, u32[]{:S(2)}, u32[]{:S(2)}) collective-permute-start(bf16[64,768]{1,0:T(8,128)(2,1)} %get-tuple-element.105), channel_id=1, source_target_pairs={{0,4},{1,5},{2,6},{3,7},{4,0},{5,1},{6,2},{7,3},{8,12},{9,13},{10,... | collective-permute-start | bytes 294920 | tf_op jit(solution)/shard_map/ppermute | solution.py:31
  272.8 9.4 %copy-start.57 = (f32[1,128]{1,0:T(1,128)S(1)}, f32[1,128]{1,0:T(1,128)}, u32[]{:S(2)}) copy-start(f32[1,128]{1,0:T(1,128)} %add.267.refs_2_) | copy-start | bytes 1540
  282.2 5.6 collective-permute-start.25
  287.8 18.1 %copy-start.59 = (bf16[256,512]{1,0:T(8,128)(2,1)S(1)}, bf16[256,512]{1,0:T(8,128)(2,1)}, u32[]{:S(2)}) copy-start(bf16[256,512]{1,0:T(8,128)(2,1)} %get-tuple-element.111.refs_2_) | copy-start | bytes 786436
  287.8 19.5 %copy-start.58 = (bf16[256,512]{1,0:T(8,128)(2,1)S(1)}, bf16[256,512]{1,0:T(8,128)(2,1)}, u32[]{:S(2)}) copy-start(bf16[256,512]{1,0:T(8,128)(2,1)} %get-tuple-element.113) | copy-start | bytes 786436
  305.4 38.5 %collective-permute-start.26 = (f32[512,896]{1,0:T(8,128)}, f32[512,896]{1,0:T(8,128)S(1)}, u32[]{:S(2)}, u32[]{:S(2)}) collective-permute-start(f32[512,896]{1,0:T(8,128)} %head_part.6.refs_4_.refs_3_), channel_id=1, source_target_pairs={{0,1},{1,0},{2,3},{3,2},{4,5},{5,4},{6,7},{7,6},{8,9},{9,8},{10,11... | collective-permute-start | bytes 5505032 | tf_op jit(solution)/shard_map/ppermute | solution.py:31
  305.9 8.2 %collective-permute-start.23 = (bf16[256,512]{1,0:T(8,128)(2,1)S(1)}, bf16[256,512]{1,0:T(8,128)(2,1)S(1)}, u32[]{:S(2)}, u32[]{:S(2)}) collective-permute-start(bf16[256,512]{1,0:T(8,128)(2,1)S(1)} %copy-done.59), channel_id=1, source_target_pairs={{0,2},{1,3},{2,0},{3,1},{4,6},{5,7},{6,4},{7,5},{8,10},{9,11},{10,... | collective-permute-start | bytes 786440 | tf_op jit(solution)/shard_map/ppermute | solution.py:31
  307.4 7.9 %collective-permute-start.24 = (bf16[256,512]{1,0:T(8,128)(2,1)S(1)}, bf16[256,512]{1,0:T(8,128)(2,1)S(1)}, u32[]{:S(2)}, u32[]{:S(2)}) collective-permute-start(bf16[256,512]{1,0:T(8,128)(2,1)S(1)} %copy-done.58), channel_id=1, source_target_pairs={{0,4},{1,5},{2,6},{3,7},{4,0},{5,1},{6,2},{7,3},{8,12},{9,13},{10,... | collective-permute-start | bytes 786440 | tf_op jit(solution)/shard_map/ppermute | solution.py:31
  318.8 19.6 %collective-permute-start.31 = (bf16[128,512]{1,0:T(8,128)(2,1)}, bf16[128,512]{1,0:T(8,128)(2,1)S(1)}, u32[]{:S(2)}, u32[]{:S(2)}) collective-permute-start(bf16[128,512]{1,0:T(8,128)(2,1)} %get-tuple-element.114.refs_2_), channel_id=1, source_target_pairs={{0,4},{1,5},{2,6},{3,7},{4,0},{5,1},{6,2},{7,3},{8,12},{9,13},{10,... | collective-permute-start | bytes 393224 | tf_op jit(solution)/shard_map/ppermute | solution.py:31
  319.3 19.1 %collective-permute-start.32 = (bf16[128,512]{1,0:T(8,128)(2,1)}, bf16[128,512]{1,0:T(8,128)(2,1)S(1)}, u32[]{:S(2)}, u32[]{:S(2)}) collective-permute-start(bf16[128,512]{1,0:T(8,128)(2,1)} %get-tuple-element.129), channel_id=1, source_target_pairs={{0,2},{1,3},{2,0},{3,1},{4,6},{5,7},{6,4},{7,5},{8,10},{9,11},{10,... | collective-permute-start | bytes 393224 | tf_op jit(solution)/shard_map/ppermute | solution.py:31
  348.7 14.5 %collective-permute-start.27 = (bf16[256,512]{1,0:T(8,128)(2,1)}, bf16[256,512]{1,0:T(8,128)(2,1)S(1)}, u32[]{:S(2)}, u32[]{:S(2)}) collective-permute-start(bf16[256,512]{1,0:T(8,128)(2,1)} %get-tuple-element.116.refs_5_), channel_id=1, source_target_pairs={{0,2},{1,3},{2,0},{3,1},{4,6},{5,7},{6,4},{7,5},{8,10},{9,11},{10,... | collective-permute-start | bytes 786440 | tf_op jit(solution)/shard_map/ppermute | solution.py:31
  349.2 14.0 %collective-permute-start.28 = (bf16[256,512]{1,0:T(8,128)(2,1)}, bf16[256,512]{1,0:T(8,128)(2,1)S(1)}, u32[]{:S(2)}, u32[]{:S(2)}) collective-permute-start(bf16[256,512]{1,0:T(8,128)(2,1)} %get-tuple-element.118), channel_id=1, source_target_pairs={{0,4},{1,5},{2,6},{3,7},{4,0},{5,1},{6,2},{7,3},{8,12},{9,13},{10,... | collective-permute-start | bytes 786440 | tf_op jit(solution)/shard_map/ppermute | solution.py:31
  366.8 18.8 %collective-permute-start.29 = (bf16[128,512]{1,0:T(8,128)(2,1)}, bf16[128,512]{1,0:T(8,128)(2,1)S(1)}, u32[]{:S(2)}, u32[]{:S(2)}) collective-permute-start(bf16[128,512]{1,0:T(8,128)(2,1)} %get-tuple-element.123.refs_6_), channel_id=1, source_target_pairs={{0,4},{1,5},{2,6},{3,7},{4,0},{5,1},{6,2},{7,3},{8,12},{9,13},{10,... | collective-permute-start | bytes 393224 | tf_op jit(solution)/shard_map/ppermute | solution.py:31
  367.3 18.3 %collective-permute-start.30 = (bf16[128,512]{1,0:T(8,128)(2,1)}, bf16[128,512]{1,0:T(8,128)(2,1)S(1)}, u32[]{:S(2)}, u32[]{:S(2)}) collective-permute-start(bf16[128,512]{1,0:T(8,128)(2,1)} %get-tuple-element.125), channel_id=1, source_target_pairs={{0,2},{1,3},{2,0},{3,1},{4,6},{5,7},{6,4},{7,5},{8,10},{9,11},{10,... | collective-permute-start | bytes 393224 | tf_op jit(solution)/shard_map/ppermute | solution.py:31
  391.4 9.9 %collective-permute-start.33 = (bf16[128,768]{1,0:T(8,128)(2,1)S(1)}, bf16[128,768]{1,0:T(8,128)(2,1)S(1)}, u32[]{:S(2)}, u32[]{:S(2)}) collective-permute-start(bf16[128,768]{1,0:T(8,128)(2,1)S(1)} %add_convert_fusion.refs_2_.refs_4_.refs_10_), channel_id=1, source_target_pairs={{0,2},{1,3},{2,0},{3,1},{4,6},{5,7},{6,4},{7,5},{8,10},{9,11},{10,... | collective-permute-start | bytes 589832 | tf_op jit(solution)/shard_map/ppermute | solution.py:31
  391.9 9.3 %collective-permute-start.34 = (bf16[128,768]{1,0:T(8,128)(2,1)S(1)}, bf16[128,768]{1,0:T(8,128)(2,1)S(1)}, u32[]{:S(2)}, u32[]{:S(2)}) collective-permute-start(bf16[128,768]{1,0:T(8,128)(2,1)S(1)} %add_convert_fusion.refs_2_.refs_4_.refs_10_), channel_id=1, source_target_pairs={{0,4},{1,5},{2,6},{3,7},{4,0},{5,1},{6,2},{7,3},{8,12},{9,13},{10,... | collective-permute-start | bytes 589832 | tf_op jit(solution)/shard_map/ppermute | solution.py:31
  404.3 4.8 collective-permute-start.35
  404.9 4.8 collective-permute-start.36
  412.6 2.5 collective-permute-start.37
  439.6 8.8 %copy-start.25 = (f32[24,768]{1,0:T(8,128)S(1)}, f32[24,768]{1,0:T(8,128)}, u32[]{:S(2)}) copy-start(f32[24,768]{1,0:T(8,128)} %left_sums.1.refs_5_) | copy-start | bytes 221188
  439.6 8.8 %collective-permute-start.38 = (f32[24,768]{1,0:T(8,128)}, f32[24,768]{1,0:T(8,128)S(1)}, u32[]{:S(2)}, u32[]{:S(2)}) collective-permute-start(f32[24,768]{1,0:T(8,128)} %left_sums.1.refs_5_), channel_id=1, source_target_pairs={{0,1},{1,0},{2,3},{3,2},{4,5},{5,4},{6,7},{7,6},{8,9},{9,8},{10,11... | collective-permute-start | bytes 221192 | tf_op jit(solution)/shard_map/ppermute | solution.py:31
  448.4 12.5 %collective-permute-start.39 = (f32[24,768]{1,0:T(8,128)S(1)}, f32[24,768]{1,0:T(8,128)S(1)}, u32[]{:S(2)}, u32[]{:S(2)}) collective-permute-start(f32[24,768]{1,0:T(8,128)S(1)} %add.318.refs_5_), channel_id=1, source_target_pairs={{0,2},{1,3},{2,0},{3,1},{4,6},{5,7},{6,4},{7,5},{8,10},{9,11},{10,... | collective-permute-start | bytes 221192 | tf_op jit(solution)/shard_map/ppermute | solution.py:31
  449.9 11.0 %collective-permute-start.40 = (f32[24,768]{1,0:T(8,128)S(1)}, f32[24,768]{1,0:T(8,128)S(1)}, u32[]{:S(2)}, u32[]{:S(2)}) collective-permute-start(f32[24,768]{1,0:T(8,128)S(1)} %add.318.refs_5_), channel_id=1, source_target_pairs={{0,4},{1,5},{2,6},{3,7},{4,0},{5,1},{6,2},{7,3},{8,12},{9,13},{10,... | collective-permute-start | bytes 221192 | tf_op jit(solution)/shard_map/ppermute | solution.py:31
  450.5 10.3 %collective-permute-start.41 = (f32[24,768]{1,0:T(8,128)S(1)}, f32[24,768]{1,0:T(8,128)S(1)}, u32[]{:S(2)}, u32[]{:S(2)}) collective-permute-start(f32[24,768]{1,0:T(8,128)S(1)} %add.318.refs_5_), channel_id=1, source_target_pairs={{0,6},{1,7},{2,4},{3,5},{4,2},{5,3},{6,0},{7,1},{8,14},{9,15},{10,... | collective-permute-start | bytes 221192 | tf_op jit(solution)/shard_map/ppermute | solution.py:31
  461.8 19.7 %collective-permute-start.42 = (f32[24,768]{1,0:T(8,128)S(1)}, f32[24,768]{1,0:T(8,128)S(1)}, u32[]{:S(2)}, u32[]{:S(2)}) collective-permute-start(f32[24,768]{1,0:T(8,128)S(1)} %add_add_fusion.4.refs_5_), channel_id=1, source_target_pairs={{0,8},{8,0},{16,24},{24,16},{1,9},{9,1},{17,25},{25,17},{2,10},{10... | collective-permute-start | bytes 221192 | tf_op jit(solution)/shard_map/ppermute | solution.py:31
  463.3 18.2 %collective-permute-start.43 = (f32[24,768]{1,0:T(8,128)S(1)}, f32[24,768]{1,0:T(8,128)S(1)}, u32[]{:S(2)}, u32[]{:S(2)}) collective-permute-start(f32[24,768]{1,0:T(8,128)S(1)} %add_add_fusion.4.refs_5_), channel_id=1, source_target_pairs={{0,16},{8,24},{16,0},{24,8},{1,17},{9,25},{17,1},{25,9},{2,18},{10... | collective-permute-start | bytes 221192 | tf_op jit(solution)/shard_map/ppermute | solution.py:31
  465.8 15.7 %collective-permute-start.44 = (f32[24,768]{1,0:T(8,128)S(1)}, f32[24,768]{1,0:T(8,128)S(1)}, u32[]{:S(2)}, u32[]{:S(2)}) collective-permute-start(f32[24,768]{1,0:T(8,128)S(1)} %add_add_fusion.4.refs_5_), channel_id=1, source_target_pairs={{0,24},{8,16},{16,8},{24,0},{1,25},{9,17},{17,9},{25,1},{2,26},{10... | collective-permute-start | bytes 221192 | tf_op jit(solution)/shard_map/ppermute | solution.py:31
  492.8 12.2 %collective-permute-start.45 = (bf16[8,4096]{1,0:T(8,128)(2,1)}, bf16[8,4096]{1,0:T(8,128)(2,1)S(1)}, u32[]{:S(2)}, u32[]{:S(2)}) collective-permute-start(bf16[8,4096]{1,0:T(8,128)(2,1)} %right_part.2.refs_2_), channel_id=1, source_target_pairs={{0,8},{8,0},{16,24},{24,16},{1,9},{9,1},{17,25},{25,17},{2,10},{10... | collective-permute-start | bytes 196616 | tf_op jit(solution)/shard_map/ppermute | solution.py:31
  493.4 11.6 %collective-permute-start.46 = (bf16[8,4096]{1,0:T(8,128)(2,1)}, bf16[8,4096]{1,0:T(8,128)(2,1)S(1)}, u32[]{:S(2)}, u32[]{:S(2)}) collective-permute-start(bf16[8,4096]{1,0:T(8,128)(2,1)} %right_part.2.refs_2_), channel_id=1, source_target_pairs={{0,16},{8,24},{16,0},{24,8},{1,17},{9,25},{17,1},{25,9},{2,18},{10... | collective-permute-start | bytes 196616 | tf_op jit(solution)/shard_map/ppermute | solution.py:31
  496.7 8.3 %collective-permute-start.47 = (bf16[8,4096]{1,0:T(8,128)(2,1)}, bf16[8,4096]{1,0:T(8,128)(2,1)S(1)}, u32[]{:S(2)}, u32[]{:S(2)}) collective-permute-start(bf16[8,4096]{1,0:T(8,128)(2,1)} %right_part.2.refs_2_), channel_id=1, source_target_pairs={{0,24},{8,16},{16,8},{24,0},{1,25},{9,17},{17,9},{25,1},{2,26},{10... | collective-permute-start | bytes 196616 | tf_op jit(solution)/shard_map/ppermute | solution.py:31
  497.3 14.4 %copy-start.56 = (f32[768]{0:T(1024)S(1)}, f32[768]{0:T(1024)}, u32[]{:S(2)}) copy-start(f32[768]{0:T(1024)} %param.43) | copy-start | bytes 9220
  507.3 30.0 %collective-permute-start.48 = (bf16[16,4096]{1,0:T(8,128)(2,1)}, bf16[16,4096]{1,0:T(8,128)(2,1)S(1)}, u32[]{:S(2)}, u32[]{:S(2)}) collective-permute-start(bf16[16,4096]{1,0:T(8,128)(2,1)} %stack.1), channel_id=1, source_target_pairs={{0,8},{8,0},{16,24},{24,16},{1,9},{9,1},{17,25},{25,17},{2,10},{10... | collective-permute-start | bytes 393224 | tf_op jit(solution)/shard_map/ppermute | solution.py:31
  507.4 29.9 %collective-permute-start.49 = (bf16[16,4096]{1,0:T(8,128)(2,1)}, bf16[16,4096]{1,0:T(8,128)(2,1)S(1)}, u32[]{:S(2)}, u32[]{:S(2)}) collective-permute-start(bf16[16,4096]{1,0:T(8,128)(2,1)} %stack.1), channel_id=1, source_target_pairs={{0,16},{8,24},{16,0},{24,8},{1,17},{9,25},{17,1},{25,9},{2,18},{10... | collective-permute-start | bytes 393224 | tf_op jit(solution)/shard_map/ppermute | solution.py:31
  511.2 26.1 %collective-permute-start.50 = (bf16[16,4096]{1,0:T(8,128)(2,1)}, bf16[16,4096]{1,0:T(8,128)(2,1)S(1)}, u32[]{:S(2)}, u32[]{:S(2)}) collective-permute-start(bf16[16,4096]{1,0:T(8,128)(2,1)} %stack.1), channel_id=1, source_target_pairs={{0,24},{8,16},{16,8},{24,0},{1,25},{9,17},{17,9},{25,1},{2,26},{10... | collective-permute-start | bytes 393224 | tf_op jit(solution)/shard_map/ppermute | solution.py:31
  512.8 24.5 %copy-start.27 = (bf16[16,4096]{1,0:T(8,128)(2,1)S(1)}, bf16[16,4096]{1,0:T(8,128)(2,1)}, u32[]{:S(2)}) copy-start(bf16[16,4096]{1,0:T(8,128)(2,1)} %stack.1) | copy-start | bytes 393220
  538.2 24.3 %copy-start.52 = (f32[4096]{0:T(1024)S(1)}, f32[4096]{0:T(1024)}, u32[]{:S(2)}) copy-start(f32[4096]{0:T(1024)} %param.37) | copy-start | bytes 49156
  538.2 24.3 %copy-start.53 = (f32[4096]{0:T(1024)S(1)}, f32[4096]{0:T(1024)}, u32[]{:S(2)}) copy-start(f32[4096]{0:T(1024)} %param.41) | copy-start | bytes 49156
  (55 other events, 110.8 us)
Sparse Core Ops, SparseCore 0:
  10.5 61.5 all-gather.6
  74.0 38.9 all-gather.8
  146.8 24.3 all-gather.10
  201.2 45.3 reduce-scatter.1
  283.1 26.7 all-gather.12

commit v3 on v2

--- a/solution.py
+++ b/solution.py
@@ -9,6 +9,7 @@
 from jax.sharding import PartitionSpec as P
 
 HEADS = 12
+HEAD_PARTS = (3, 13)
 
 pack_base = 32768
 aux_weight = 1.0 / 32.0
@@ -174,23 +175,51 @@
             ref[...] = jnp.zeros_like(ref)
 
 
-def mask_kernel(tokens, hi_count, aux_count, ids_ref, dead_ref, own_ref, partner_ref, scratch):
-    width = ids_ref.shape[1]
-    hi_rows = lax.broadcasted_iota(jnp.int32, (2 * hi_count, width), 0)
-    lo_rows = lax.broadcasted_iota(jnp.int32, (lanes, width), 0)
-    is_aux = lax.broadcasted_iota(jnp.int32, (2 * hi_count, width), 1) < aux_count
-    weight = jnp.where(is_aux, 2.0, 1.0)
-
-    def one_token(t, carry):
-        row = ids_ref[pl.ds(t, 1), :]
-        hi_hot = jnp.where(hi_rows == (row >> 7), weight, 0.0).astype(bf16)
-        lo_hot = jnp.where(lo_rows == (row & 127), 1.0, 0.0).astype(bf16)
-        picked = lax.dot_general(hi_hot, lo_hot, contract_cols, preferred_element_type=f32)
-        at = pl.multiple_of(t * 2 * hi_count, 2 * hi_count)
-        scratch[pl.ds(at, 2 * hi_count), :] = picked
+def mask_kernel(tokens, hi_count, aux_count, top_count, *refs):
+    packed = refs[0][...]
+    dead_ref, own_ref, partner_ref, valid_ref, ids_ref, top_ref, scratch = refs[1], *refs[-6:]
+    me, lat_dev = lax.axis_index("lat"), hi_count * lanes
+    half, rows = aux_count // 2, 2 * hi_count
+
+    def placed(ids):
+        from_own, from_partner = ids - me * lat_dev, ids - (me ^ 1) * lat_dev
+        return jnp.where(
+            (from_own >= 0) & (from_own < lat_dev),
+            from_own,
+            jnp.where((from_partner >= 0) & (from_partner < lat_dev), from_partner + lat_dev, -(2**20)),
+        )
+
+    ids_ref[:, :half] = placed(packed[:, :half] >> 15)
+    ids_ref[:, half:] = placed(packed[:, :half] & (pack_base - 1))
+    joint_count = lanes // top_count
+    tops = packed[:, half:]
+    lane = lax.broadcasted_iota(jnp.int32, tops.shape, 1)
+    repeated = tops
+    for k in range(1, joint_count):
+        repeated = jnp.where(lane // top_count == k, pltpu.roll(tops, k * top_count, 1), repeated)
+    top_ref[...] = placed(repeated) + (lane // top_count) * (rows * lanes)
+    counted = jnp.where(lane == top_count, -1 - tops, 0).astype(f32)
+    valid = jnp.sum(jnp.sum(counted, axis=0, keepdims=True), axis=1, keepdims=True)
+    clear_at_start(valid_ref)
+    valid_ref[...] += jnp.broadcast_to(valid, valid_ref.shape)
+
+    def hot(count, width, index):
+        return jnp.where(lax.broadcasted_iota(jnp.int32, (count, width), 0) == index, 1.0, 0.0).astype(bf16)
+
+    def some_tokens(group, carry):
+        base = group * joint_count
+        for k in range(joint_count):
+            row = ids_ref[pl.ds(base + k, 1), :]
+            picked = dot(hot(rows, aux_count, row >> 7), hot(lanes, aux_count, row & 127), contract_cols)
+            scratch[pl.ds(pl.multiple_of((base + k) * rows, rows), rows), :] = 2.0 * picked
+        joint_row = top_ref[pl.ds(base, 1), :]
+        for k in range(1, joint_count):
+            joint_row = jnp.where(lane[:1] // top_count == k, top_ref[pl.ds(base + k, 1), :], joint_row)
+        picked = dot(hot(joint_count * rows, lanes, joint_row >> 7), hot(lanes, lanes, joint_row & 127), contract_cols)
+        scratch[pl.ds(pl.multiple_of(base * rows, rows), joint_count * rows), :] += picked
         return carry
 
-    lax.fori_loop(0, tokens, one_token, 0, unroll=16)
+    lax.fori_loop(0, tokens // joint_count, some_tokens, 0, unroll=4)
     for hi in range(2 * hi_count):
         code = scratch[pl.ds(hi, tokens, stride=2 * hi_count), :]
         aux = jnp.where(code >= 2.0, 2.0, 0.0)
@@ -201,27 +230,40 @@
             partner_ref[:, (hi - hi_count) * lanes : (hi - hi_count + 1) * lanes] = code
 
 
-def build_mask(pair_ids, dead_pair, aux_count):
-    rows, width = pair_ids.shape
+def build_mask(packed, dead_pair, aux_count, top_count, rows, first, so_far=(), deps=()):
+    width = packed.shape[1]
     lat_dev = dead_pair.shape[1] // 2
     hi_count, tokens = lat_dev // lanes, 64
-    out_block = pl.BlockSpec((tokens, lat_dev), lambda i: (i, 0))
-    return pl.pallas_call(
-        functools.partial(mask_kernel, tokens, hi_count, aux_count),
-        out_shape=(jax.ShapeDtypeStruct((rows, lat_dev), bf16),) * 2,
-        grid=(rows // tokens,),
-        in_specs=[
-            pl.BlockSpec((tokens, width), lambda i: (i, 0)),
-            pl.BlockSpec((1, 2 * lat_dev), lambda i: (0, 0)),
+    steps = packed.shape[0] // tokens
+    out_block = pl.BlockSpec((tokens, lat_dev), lambda i: (i + first // tokens, 0))
+    *masks, valid = call(
+        functools.partial(mask_kernel, tokens, hi_count, aux_count, top_count),
+        "build_mask",
+        (packed, dead_pair, *so_far),
+        (like((rows, lat_dev), bf16), like((rows, lat_dev), bf16), like((1, lanes))),
+        (steps,),
+        [row_block(tokens, width), whole_of((1, 2 * lat_dev))] + [untouched] * len(so_far),
+        (out_block, out_block, whole_of((1, lanes))),
+        deps,
+        (16 * steps * tokens * 2 * lat_dev * aux_count, 4 * steps * tokens * lat_dev),
+        aliases={2 + k: k for k in range(len(so_far))},
+        scratch=[
+            pltpu.VMEM((tokens, aux_count), jnp.int32),
+            pltpu.VMEM((tokens, lanes), jnp.int32),
+            pltpu.VMEM((tokens * 2 * hi_count, lanes), f32),
         ],
-        out_specs=(out_block, out_block),
-        scratch_shapes=[pltpu.VMEM((tokens * 2 * hi_count, lanes), f32)],
-        compiler_params=pltpu.CompilerParams(vmem_limit_bytes=vmem_most),
-        cost_estimate=pl.CostEstimate(
-            flops=16 * rows * 2 * lat_dev * width, bytes_accessed=4 * rows * lat_dev, transcendentals=0
-        ),
-        name="build_mask",
-    )(pair_ids, dead_pair)
+    )
+    return masks, valid
+
+
+def pass_kernel(in_ref, out_ref):
+    pass
+
+
+def pass_after(value, *deps):
+    return call(
+        pass_kernel, "pass_after", (value,), like(value.shape, value.dtype), (), [untouched], untouched, deps, aliases={0: 0}
+    )
 
 
 def split_three(values):
@@ -235,50 +277,48 @@
     return [piece.astype(f32) for piece in split_three(values)]
 
 
+def residual_kernel(weight, stream_ref, rebuilt_ref, aux_ref, weight_ref, pull_ref, rounded_ref, square_ref):
+    err = stream_ref[...] - rebuilt_ref[...] - aux_ref[...]
+    pull = -(2.0 * weight) * weight_ref[...] * err
+    pull_ref[...] = pull
+    rounded_ref[...] = pull.astype(bf16)
+    square_ref[...] = jnp.sum(err * err, axis=1, keepdims=True)
+
+
+def residual_pull(stream, rebuilt, aux, weight_own, *deps):
+    shape = stream.shape
+    return call(
+        functools.partial(residual_kernel, aux_weight),
+        "residual_pull",
+        (stream, rebuilt, aux, weight_own),
+        (like(shape), like(shape, bf16), like((shape[0], 1))),
+        deps=deps,
+    )
+
+
 def high_low(values):
     high = values.astype(bf16)
     return high, (values - high.astype(f32)).astype(bf16)
 
 
-def halves_kernel(by_two_ref, by_four_ref, first_ref, second_ref):
-    half = by_two_ref.shape[0] // 2
-    first_ref[...] = by_four_ref[:half, :]
-    second_ref[...] = by_two_ref[half:, :]
-
-
-def assemble_kernel(by_two_ref, first_ref, second_ref, by_four_ref, own_ref, even_ref):
-    rows = own_ref.shape[0]
-    even_ref[:rows, :] = by_two_ref[...]
-    even_ref[rows : rows + rows // 2, :] = first_ref[...]
-    even_ref[rows + rows // 2 : 2 * rows, :] = second_ref[...]
-    even_ref[2 * rows : 3 * rows, :] = by_four_ref[...]
-    even_ref[3 * rows :, :] = own_ref[...]
+def assemble_kernel(*refs):
+    *blocks, even_ref = refs
+    rows = blocks[0].shape[0]
+    for at, block in enumerate(blocks):
+        even_ref[at * rows : (at + 1) * rows, :] = block[...]
 
 
 class Gather:
     def __init__(self, own):
         self.own, self.plain = own, lax.axis_size("lat") != 8
         if not self.plain:
-            self.by_two, self.by_four = swap(own, "lat", 2), swap(own, "lat", 4)
-
-    def middle(self, *deps):
-        if not self.plain:
-            rows, width = self.own.shape
-            piece = like((rows // 2, width), self.own.dtype)
-            first, second = call(halves_kernel, "halves", (self.by_two, self.by_four), (piece, piece), deps=deps)
-            self.diag = swap(first, "lat", 2), swap(second, "lat", 4)
+            self.blocks = [swap(own, "lat", j) if j else own for j in even_order()]
 
     def end(self, *deps):
         if self.plain:
             return gather_tokens(self.own)
         rows, width = self.own.shape
-        even = call(
-            assemble_kernel,
-            "assemble",
-            (self.by_two, *self.diag, self.by_four, self.own),
-            like((4 * rows, width), self.own.dtype),
-            deps=deps,
-        )
+        even = call(assemble_kernel, "assemble", self.blocks, like((4 * rows, width), self.own.dtype), deps=deps)
         return even, swap(even, "lat", 1)
 
 
@@ -296,18 +336,15 @@
     return call(reorder_kernel, "reorder", (blocks,), (half, half), deps=deps)
 
 
-def weigh(lse_a, lse_b):
-    top = jnp.maximum(lse_a, lse_b)
-    exp_a, exp_b = jnp.exp(lse_a - top), jnp.exp(lse_b - top)
-    total = exp_a + exp_b
-    return exp_a / total, exp_b / total, top + jnp.log(total)
-
-
-def joint(a, b, tail):
+def joint(parts, tail):
     if not tail:
-        return a + b
-    share_a, share_b, lse = weigh(a[:, -tail:], b[:, -tail:])
-    return jnp.concatenate([a[:, :-tail] * share_a[:, :1] + b[:, :-tail] * share_b[:, :1], lse], axis=1)
+        return sum(parts[1:], parts[0])
+    lses = [part[:, -tail:] for part in parts]
+    top = functools.reduce(jnp.maximum, lses)
+    weights = [jnp.exp(lse - top) for lse in lses]
+    total = sum(weights[1:], weights[0])
+    means = [part[:, :-tail] * (weight / total)[:, :1] for part, weight in zip(parts, weights)]
+    return jnp.concatenate([sum(means[1:], means[0]), top + jnp.log(total)], axis=1)
 
 
 def to_send(values, tail):
@@ -319,8 +356,8 @@
     return jnp.concatenate([values[:, :-tail], logs], axis=1).astype(bf16)
 
 
-def received(ref, span, tail):
-    values = ref[span, :].astype(f32)
+def received(ref, tail):
+    values = ref[...].astype(f32)
     if not tail:
         return values
     logs = values[:, -tail:]
@@ -328,68 +365,34 @@
     return jnp.concatenate([values[:, :-tail], jnp.broadcast_to(lse, logs.shape)], axis=1)
 
 
-def chip_kernel(tail, even_ref, odd_ref, keep_a, send_a, keep_b, send_b):
-    rows = even_ref.shape[0] // 4
-    total = joint(even_ref[...], odd_ref[...], tail)
-    half = (total.shape[1] - tail) // 2
-
-    def columns(values, part):
-        means = values[:, part * half : (part + 1) * half]
-        return jnp.concatenate([means, values[:, -tail:]], axis=1) if tail else means
-
-    send_a[...] = to_send(columns(total[: 2 * rows], 0), tail)
-    keep_a[...] = columns(total[2 * rows :], 0)
-    send_b[...] = to_send(columns(total[rows : 3 * rows], 1), tail)
-    keep_b[:rows, :] = columns(total[:rows], 1)
-    keep_b[rows:, :] = columns(total[3 * rows :], 1)
-
-
-def hop_kernel(tail, keep_a, got_a, keep_b, got_b, next_a, send_a, next_b, send_b):
-    rows = keep_a.shape[0] // 2
-    early, late = slice(0, rows), slice(rows, 2 * rows)
-    send_a[...] = to_send(joint(keep_a[early, :], received(got_a, late, tail), tail), tail)
-    next_a[...] = joint(keep_a[late, :], received(got_a, early, tail), tail)
-    send_b[...] = to_send(joint(keep_b[early, :], received(got_b, early, tail), tail), tail)
-    next_b[...] = joint(keep_b[late, :], received(got_b, late, tail), tail)
-
-
-def last_kernel(tail, keep_a, got_a, keep_b, got_b, total_ref):
-    rows = keep_a.shape[0]
-    for part, (keep, got) in enumerate(((keep_a, got_a), (keep_b, got_b))):
-        total = joint(keep[...], received(got, slice(0, rows), tail), tail)
-        half = total.shape[1] - tail
-        total_ref[:, part * half : (part + 1) * half] = total[:, :half]
-        if tail and part == 0:
-            total_ref[:, 2 * half :] = total[:, half:]
+def chip_kernel(tail, even_ref, odd_ref, *outs):
+    rows = outs[0].shape[0]
+    for at, out in enumerate(outs):
+        span = slice(at * rows, (at + 1) * rows)
+        total = joint([even_ref[span, :], odd_ref[span, :]], tail)
+        out[...] = total if at == len(outs) - 1 else to_send(total, tail)
+
+
+def last_kernel(tail, *refs):
+    *got, keep, total_ref = refs
+    total_ref[...] = joint([keep[...]] + [received(ref, tail) for ref in got], tail)
 
 
 class Scatter:
     def __init__(self, odd, tail=0):
         self.moved, self.tail, self.plain = swap(odd, "lat", 1), tail, lax.axis_size("lat") != 8
 
-    def step(self, kernel, name, args, rows, width, deps):
-        outs = (like((rows, width)), like((rows, width), bf16))
-        self.state = call(functools.partial(kernel, self.tail), name, args, outs * 2, deps=deps)
-
     def chip(self, even, *deps):
         self.even = even
-        if not self.plain:
-            rows, width = even.shape
-            self.width = (width - self.tail) // 2 + self.tail
-            self.rows = rows // 4
-            self.step(chip_kernel, "chip_sum", (even, self.moved), 2 * self.rows, self.width, deps)
-            keep_a, send_a, keep_b, send_b = self.state
-            self.pending = keep_a, swap(send_a, "lat", 2), keep_b, swap(send_b, "lat", 4)
-            return send_a
-        return even
-
-    def hop(self, *deps):
         if self.plain:
-            return self.even
-        self.step(hop_kernel, "hop_sum", self.pending, self.rows, self.width, deps)
-        keep_a, send_a, keep_b, send_b = self.state
-        self.pending = keep_a, swap(send_a, "lat", 4), keep_b, swap(send_b, "lat", 2)
-        return send_a
+            return even
+        rows, width = even.shape[0] // 4, even.shape[1]
+        shapes = [like((rows, width), bf16)] * 3 + [like((rows, width))]
+        *sends, keep = call(
+            functools.partial(chip_kernel, self.tail), "chip_sum", (even, self.moved), shapes, deps=deps
+        )
+        self.pending = [swap(send, "lat", j) for send, j in zip(sends, even_order())] + [keep]
+        return keep
 
     def last(self, *deps):
         if self.plain:
@@ -400,22 +403,34 @@
                 self.even[:, :width], self.even[:, width : width + 1], self.moved[:, :width], self.moved[:, width : width + 1]
             )
             return jnp.concatenate([mean, jnp.broadcast_to(lse, (lse.shape[0], self.tail))], axis=1)
-        width = 2 * (self.width - self.tail) + self.tail
         return call(
-            functools.partial(last_kernel, self.tail), "last_sum", self.pending, like((self.rows, width)), deps=deps
+            functools.partial(last_kernel, self.tail), "last_sum", self.pending, like(self.pending[-1].shape), deps=deps
         )
 
 
-def head_kernel(chunk, chunks, normed_ref, table_ref, out_ref):
+def head_kernel(cuts, steps, normed_ref, table_hbm, out_ref, table_ref, sems):
+    def piece(c):
+        span = pl.ds(cuts[c], cuts[c + 1] - cuts[c])
+        return pltpu.make_async_copy(table_hbm.at[span, :], table_ref.at[span, :], sems.at[c])
+
+    def at_start(action):
+        if steps == 1:
+            action()
+        else:
+            pl.when(pl.program_id(0) == 0)(action)
+
+    chunks = len(cuts) - 1
+    at_start(lambda: [piece(c).start() for c in range(chunks)] and None)
     normed = normed_ref[...]
 
     def logits_of(c):
-        return dot(normed, table_ref[c * chunk : (c + 1) * chunk, :], contract_cols)
+        at_start(lambda: piece(c).wait())
+        return dot(normed, table_ref[cuts[c] : cuts[c + 1], :], contract_cols)
 
     def fold(values, op):
         folded = values[:, :lanes]
-        for k in range(1, chunk // lanes):
-            folded = op(folded, values[:, k * lanes : (k + 1) * lanes])
+        for k in range(lanes, values.shape[1], lanes):
+            folded = op(folded, values[:, k : k + lanes])
         return folded
 
     top = total = mean = None
@@ -426,7 +441,7 @@
         new_top = chunk_top if top is None else jnp.maximum(top, chunk_top)
         grown = jnp.exp(logits - new_top).astype(bf16)
         chunk_total = fold(grown.astype(f32), jnp.add)
-        chunk_mean = dot(grown, table_ref[c * chunk : (c + 1) * chunk, :], contract_plain)
+        chunk_mean = dot(grown, table_ref[cuts[c] : cuts[c + 1], :], contract_plain)
         if top is None:
             total, mean = chunk_total, chunk_mean
         else:
@@ -439,25 +454,29 @@
     out_ref[:, width:] = jnp.broadcast_to(top + jnp.log(total), (mean.shape[0], lanes))
 
 
+def head_cuts(entries):
+    unit = 256 if entries % 256 == 0 else lanes
+    tiles = entries // unit
+    ends = sorted({max(1, tiles * part // 26) for part in HEAD_PARTS} | {tiles})
+    return [0] + [unit * end for end in ends]
+
+
 def head_part(normed, table, *deps):
     rows, width = normed.shape
     entries = table.shape[0]
-    tiles = entries // lanes
-    chunk = lanes * max(d for d in range(1, 14) if tiles % d == 0)
     block = min(512, rows)
-    return call(
-        functools.partial(head_kernel, chunk, entries // chunk),
+    cuts = head_cuts(entries)
+    return call(
+        functools.partial(head_kernel, cuts, rows // block),
         "head_part",
         (normed, table),
         like((rows, width + lanes)),
         (rows // block,),
-        [
-            pl.BlockSpec((block, width), lambda i: (i, 0)),
-            pl.BlockSpec(table.shape, lambda i: (0, 0), pipeline_mode=pl.Buffered(1)),
-        ],
+        [pl.BlockSpec((block, width), lambda i: (i, 0)), untouched],
         pl.BlockSpec((block, width + lanes), lambda i: (i, 0)),
         deps,
         (6 * rows * entries * width, 2 * entries * width),
+        scratch=[pltpu.VMEM(table.shape, bf16), pltpu.SemaphoreType.DMA((len(cuts) - 1,))],
     )
 
 
@@ -817,7 +836,7 @@
     bias = jnp.sum(own_grads[...].astype(f32), axis=0, keepdims=True)
     bias = bias - jnp.sum(pull_ref[...], axis=0, keepdims=True)
     index = lax.broadcasted_iota(jnp.int32, (8, bias.shape[1]), 0)
-    out_ref[2 * rank :, :] = jnp.where(index == 0, bias, jnp.where(index == 1, loss_ref[...], 0.0))
+    out_ref[2 * rank :, :] = jnp.where(index == 0, bias, jnp.where(index == 1, jnp.sum(loss_ref[...], axis=1, keepdims=True), 0.0))
 
 
 def ortho_kernel(rank, left_ref, enc_ref, dec_ref):
@@ -910,6 +929,124 @@
         (big, big, big),
         deps,
         (2 * 48 * latents * width, 24 * latents * width),
+    )
+
+
+def stack_weights_kernel(qkv_ref, out_ref, fc_ref, proj_ref, top_ref, bottom_ref):
+    share, width = out_ref.shape
+    squares = [qkv_ref[:, k * width : (k + 1) * width] for k in range(3)] + [out_ref[...]]
+    squares += [fc_ref[:, k * width : (k + 1) * width] for k in range(fc_ref.shape[1] // width)]
+    half = top_ref.shape[0] // share
+    for k, square in enumerate(squares):
+        if k < half:
+            top_ref[k * share : (k + 1) * share, :] = square
+        else:
+            bottom_ref[(k - half) * share : (k - half + 1) * share, :] = square
+    bottom_ref[(len(squares) - half) * share :, :] = proj_ref[...]
+
+
+def stack_weights(w_qkv, w_out, w_fc, w_proj):
+    share, width = w_out.shape
+    rows = share * (4 + w_fc.shape[1] // width) + w_proj.shape[0]
+    half = like((rows // 2, width), bf16)
+    return call(stack_weights_kernel, "stack_weights", (w_qkv, w_out, w_fc, w_proj), (half, half))
+
+
+def frozen_kernel(share, *refs):
+    residual_ref, norm_ref, bias_ref, dec_bias_ref = refs[:4]
+    count = refs[-2].shape[0]
+    pieces = refs[4 : 4 + 2 * count]
+    stream_out, centered_out, orig_out, weights, sems = refs[4 + 2 * count :]
+    me = lax.axis_index("lat")
+    total_rows, width = weights.shape[1:]
+    hidden = (total_rows // share - 8) * share * count
+    cuts = [0, 3 * share, total_rows // 2, total_rows]
+    copies = [[] for _ in cuts[1:]]
+    for j in range(count):
+        for k in range(len(cuts) - 1):
+            rows = cuts[k + 1] - cuts[k]
+            piece, inner = (pieces[2 * j], cuts[k]) if k < len(cuts) - 2 else (pieces[2 * j + 1], 0)
+            copies[k].append(
+                pltpu.make_async_copy(
+                    piece.at[pl.ds(inner, rows), :],
+                    weights.at[me ^ j, pl.ds(cuts[k], rows), :],
+                    sems.at[k, j],
+                )
+            )
+    for group in copies:
+        for copy in group:
+            copy.start()
+
+    def square(k):
+        return weights[:, k * share : (k + 1) * share, :].reshape(width, width)
+
+    def norm(values, row):
+        return layer_norm(values, norm_ref[row : row + 1, :], norm_ref[row + 1 : row + 2, :])
+
+    def bias(k, count=1):
+        return bias_ref[:, k * width : (k + count) * width]
+
+    stream = residual_ref[...].astype(f32)
+    normed = norm(stream, 0).astype(bf16)
+    for copy in copies[0]:
+        copy.wait()
+    queries, keys, values = [
+        (dot(normed, square(k), contract_plain) + bias(k)).astype(bf16) for k in range(3)
+    ]
+    seq_len = stream.shape[0]
+    early = lax.broadcasted_iota(jnp.int32, (seq_len, lanes), 1) < width // HEADS
+    causal = lax.broadcasted_iota(jnp.int32, (seq_len, seq_len), 0) >= lax.broadcasted_iota(
+        jnp.int32, (seq_len, seq_len), 1
+    )
+    nothing = jnp.zeros((), bf16)
+    attended = []
+    for k in range(0, width, lanes):
+        pair_q, pair_k, pair_v = (part[:, k : k + lanes] for part in (queries, keys, values))
+        outs = []
+        for is_early in (True, False):
+            head_q = jnp.where(early == is_early, pair_q, nothing)
+            scores = dot(head_q, pair_k, contract_cols) / math.sqrt(width // HEADS)
+            scores = jnp.where(causal, scores, -1e30)
+            grown = jnp.exp(scores - jnp.max(scores, axis=1, keepdims=True))
+            share_of = (grown / jnp.sum(grown, axis=1, keepdims=True)).astype(bf16)
+            outs.append(dot(share_of, pair_v, contract_plain))
+        attended.append(jnp.where(early, outs[0], outs[1]).astype(bf16))
+    attended = jnp.concatenate(attended, axis=1)
+    for copy in copies[1]:
+        copy.wait()
+    stream = stream + dot(attended, square(3), contract_plain) + bias(3)
+    normed = norm(stream, 2).astype(bf16)
+    for copy in copies[2]:
+        copy.wait()
+    out = None
+    for k in range(hidden // width):
+        inner = dot(normed, square(4 + k), contract_plain) + bias(4 + k)
+        activated = jax.nn.gelu(inner, approximate=True).astype(bf16)
+        per = width // (hidden // weights.shape[0])
+        block = weights[k * per : (k + 1) * per, 8 * share :, :].reshape(width, width)
+        part = dot(activated, block, contract_plain)
+        out = part if out is None else out + part
+    stream = stream + out + bias(4 + hidden // width)
+    stream_out[...] = stream
+    centered_out[...] = (stream - dec_bias_ref[...]).astype(bf16)
+    orig_out[...] = norm(stream, 4).astype(bf16)
+
+
+def frozen_whole(residual, norm_params, biases, dec_bias, pieces, share, *deps):
+    rows, width = residual.shape
+    total = 2 * pieces[0].shape[0]
+    count = len(pieces) // 2
+    return call(
+        functools.partial(frozen_kernel, share),
+        "frozen_block",
+        (residual, norm_params, biases[None, :], dec_bias[None, :], *pieces),
+        (like((rows, width)), like((rows, width), bf16), like((rows, width), bf16)),
+        (),
+        [in_vmem] * 4 + [untouched] * len(pieces),
+        (in_vmem,) * 3,
+        deps,
+        (2 * rows * count * total * width, 2 * count * total * width),
+        scratch=[pltpu.VMEM((count, total, width), bf16), pltpu.SemaphoreType.DMA((3, count))],
     )
 
 
@@ -996,114 +1133,140 @@
     rank = q_enc.shape[1]
     err_enc, err_dec = err_enc[0], err_dec[0]
 
-    joined = lax.all_gather(jnp.concatenate([w_qkv, w_out, w_fc], axis=1), "lat", axis=0, tiled=True)
-    proj_all = lax.all_gather(w_proj, "lat", axis=0, tiled=True)
-    squares = [joined[:, k : k + model_width] for k in range(0, joined.shape[1], model_width)]
-
     half = aux_count // 2
     valid_float = valid_mask.astype(f32)
     packed = jnp.concatenate(
-        [aux_idx[:, :half] * pack_base + aux_idx[:, half:], top_idx, valid_mask[:, None]], axis=1
-    )
-    gather = Gather(packed)
-    enc_weight = rounded(w_enc, False, packed)
-    gather.middle(enc_weight)
-    dec_weight = rounded(w_dec, True, enc_weight)
-    packed, _ = gather.end(dec_weight)
-    picks = packed[:, half : half + top_count]
-    ids = jnp.concatenate([packed[:, :half] // pack_base, packed[:, :half] % pack_base, picks], axis=1)
-    own_base, partner_base = lat_index * lat_dev, (lat_index ^ 1) * lat_dev
-    from_own, from_partner = ids - own_base, ids - partner_base
-    ids = jnp.where(
-        (from_own >= 0) & (from_own < lat_dev),
-        from_own,
-        jnp.where((from_partner >= 0) & (from_partner < lat_dev), from_partner + lat_dev, -1),
-    )
-    padding = -ids.shape[1] % lanes
-    ids = jnp.concatenate([ids, jnp.full((ids.shape[0], padding), -1, jnp.int32)], axis=1)
+        [
+            aux_idx[:, :half] * pack_base + aux_idx[:, half:],
+            top_idx,
+            jnp.broadcast_to(-1 - valid_mask[:, None], (valid_mask.shape[0], lanes - top_count)),
+        ],
+        axis=1,
+    )
     dead_pair = jnp.concatenate(
-        [lax.dynamic_slice_in_dim(dead_flags, base, lat_dev) for base in (own_base, partner_base)]
-    ).astype(f32)
-    mask_even, mask_partner = build_mask(ids, dead_pair[None, :], aux_count)
-    mask_odd = swap(mask_partner, "lat", 1)
-
-    valid_total = jnp.full((1, lanes), jnp.sum(packed[:, half + top_count].astype(f32)))
+        [
+            lax.dynamic_slice_in_dim(dead_flags, base * lat_dev, lat_dev)
+            for base in (lat_index, lat_index ^ 1)
+        ]
+    ).astype(f32)[None, :]
+    share = w_qkv.shape[0]
+    by_piece = lax.axis_size("lat") == 8 and share % 16 == 0
+    if by_piece:
+        top, bottom = stack_weights(w_qkv, w_out, w_fc, w_proj)
+        picks = Gather(packed)
+        four_top, two_bottom = swap(top, "lat", 4), swap(bottom, "lat", 2)
+        two_top, four_bottom = swap(top, "lat", 2), swap(bottom, "lat", 4)
+        rows = packed.shape[0]
+        masks, valid_0 = build_mask(packed, dead_pair, aux_count, top_count, 4 * rows, 3 * rows, deps=(top,))
+        by_two, by_six, by_four, _ = picks.blocks
+        masks, valid_1 = build_mask(
+            by_two, dead_pair, aux_count, top_count, 4 * rows, 0, masks, deps=(by_six, by_four)
+        )
+        four_top, two_bottom = pass_after(four_top, masks[0]), pass_after(two_bottom, masks[0])
+        six_top, six_bottom = swap(four_top, "lat", 2), swap(two_bottom, "lat", 4)
+        masks, valid_2 = build_mask(by_four, dead_pair, aux_count, top_count, 4 * rows, 2 * rows, masks)
+        masks, valid_3 = build_mask(by_six, dead_pair, aux_count, top_count, 4 * rows, rows, masks)
+        valid_total = valid_0 + valid_1 + valid_2 + valid_3
+        even_pieces = [(top, bottom), (two_top, two_bottom), (four_top, four_bottom)]
+        even_pieces.append((pass_after(six_top, masks[0]), pass_after(six_bottom, masks[0])))
+        pieces = [
+            piece
+            for pair in even_pieces
+            for piece in (*pair, *(swap(half_piece, "lat", 1) for half_piece in pair))
+        ]
+    else:
+        joined = lax.all_gather(jnp.concatenate([w_qkv, w_out, w_fc], axis=1), "lat", axis=0, tiled=True)
+        proj_all = lax.all_gather(w_proj, "lat", axis=0, tiled=True)
+        squares = [joined[:, k : k + model_width] for k in range(0, joined.shape[1], model_width)]
+        packed = gather_even(packed)
+        masks, valid_total = build_mask(packed, dead_pair, aux_count, top_count, packed.shape[0], 0)
+    mask_even, mask_partner = masks
     valid_total = sum_round(valid_total, "lat", [1])
-    for bit in bits_of("rep"):
-        valid_total = sum_round(valid_total, "rep", [bit])
-    weight_own = (valid_float / valid_total[0, 0])[:, None]
-
-    stream = frozen_block(
-        residual, norm_params, biases, squares[:3], squares[3], squares[4:], proj_all
-    )
-
     def final_norm(values):
         return layer_norm(values, norm_params[4], norm_params[5])
 
-    gather = Gather((stream - decoder_bias_vec).astype(bf16))
-    orig_normed = final_norm(stream)
-    q_enc_rows, q_enc_columns = factor_pieces(q_enc.T, gather.own, valid_total)
-    gather.middle(q_enc_rows)
+    if by_piece:
+        stream, centered_own, orig_blocks = frozen_whole(
+            residual,
+            norm_params,
+            biases,
+            decoder_bias_vec,
+            pieces,
+            share,
+            masks[0],
+            valid_total,
+        )
+        mask_partner = pass_after(mask_partner, centered_own)
+    else:
+        stream = frozen_block(residual, norm_params, biases, squares[:3], squares[3], squares[4:], proj_all)
+        centered_own = (stream - decoder_bias_vec).astype(bf16)
+        orig_blocks = final_norm(stream).astype(bf16)
+    gather = Gather(centered_own)
+    enc_weight = rounded(w_enc, False, centered_own)
+    mask_odd = swap(mask_partner, "lat", 1)
+    valid_total = sum_round(pass_after(valid_total, centered_own), "rep", bits_of("rep"))
+    weight_own = (valid_float / valid_total[0, 0])[:, None]
+    dec_weight = rounded(w_dec, True, enc_weight, valid_total)
+    centered = gather.end(dec_weight)
+    q_enc_rows, q_enc_columns = factor_pieces(q_enc.T, dec_weight)
     q_dec_rows, q_dec_columns = factor_pieces(q_dec.T, q_enc_rows)
-    centered = gather.end(q_dec_rows)
-    orig_blocks = orig_normed.astype(bf16)
 
     bias_row = encoder_bias_vec[None, :]
     tops_odd, auxes_odd, top_odd = forward(
-        centered[1], enc_weight, bias_row, mask_odd, dec_weight
+        centered[1], enc_weight, bias_row, mask_odd, dec_weight, q_dec_rows
     )
     rebuilt = Scatter(top_odd)
     tops_even, auxes_even, top_even = forward(centered[0], enc_weight, bias_row, mask_even, dec_weight, top_odd)
     sent = rebuilt.chip(top_even)
     aux_part = aux_forward(auxes_odd, auxes_even, dec_weight, sent)
     auxiliary_rebuilt = lax.psum_scatter(aux_part, "lat", scatter_dimension=0, tiled=False)
-    sent = rebuilt.hop(aux_part)
     orig_group = gather_behind(orig_blocks, aux_part)
-    orig_odd = head_part(orig_group[1], head_table, sent)
-    rebuilt_input = rebuilt.last(orig_odd) + decoder_bias_vec
+    rebuilt_input = rebuilt.last(orig_group[0]) + decoder_bias_vec
     rec_float, norm_back = jax.vjp(final_norm, rebuilt_input)
     gather = Gather(rec_float.astype(bf16))
-    orig_mean = Scatter(orig_odd, lanes)
-    orig_even = head_part(orig_group[0], head_table, gather.own)
-    gather.middle(orig_even)
-    products_dec = factor_products(tops_odd, tops_even, q_dec_columns, orig_even)
-    rec_group = gather.end(products_dec[0])
-    sent = orig_mean.chip(orig_even, products_dec[0])
-
-    resid_err = stream - rebuilt_input - auxiliary_rebuilt
-    aux_pull = -(2.0 * aux_weight) * weight_own * resid_err
-    aux_blocks = aux_pull.astype(bf16)
-
+    orig_odd = head_part(orig_group[1], head_table, gather.own)
+    rec_group = gather.end(orig_odd)
+    orig_mean = Scatter(pass_after(orig_odd, rec_group[0]), lanes)
+    orig_even = head_part(orig_group[0], head_table, rec_group[0])
+    sent = orig_mean.chip(orig_even)
     rec_odd = head_part(rec_group[1], head_table, sent)
+    orig_mean = orig_mean.last(rec_odd)
+    rec_odd = pass_after(rec_odd, orig_mean)
     rec_mean = Scatter(rec_odd, lanes)
-    sent = orig_mean.hop(rec_odd)
-    rec_even = head_part(rec_group[0], head_table, sent, rec_odd)
+    aux_pull, aux_blocks, err_square = residual_pull(
+        stream, rebuilt_input, auxiliary_rebuilt, weight_own, orig_mean
+    )
+    rec_even = head_part(rec_group[0], head_table, aux_blocks)
     sent = rec_mean.chip(rec_even)
-    orig_mean = orig_mean.last(rec_even)
-    aux_group = gather_behind(aux_blocks, rec_even)
-
-    pre_odd, pre_even = aux_back(aux_group[1], aux_group[0], dec_weight, mask_odd, mask_even, sent)
-    sent = rec_mean.hop(pre_odd)
-    dec_part, left_dec = part_dec(
-        (auxes_odd, auxes_even), (aux_group[1], aux_group[0]), err_dec, q_dec_rows, sent, pre_odd
-    )
-    rec_mean = rec_mean.last(dec_part)
+
+    products_dec = factor_products(tops_odd, tops_even, q_dec_columns, sent)
+    left_enc = err_left(q_enc_rows, err_enc, products_dec[0])
+    rec_mean = rec_mean.last(left_enc)
 
     orig_lse, rec_lse = orig_mean[:, model_width], rec_mean[:, model_width]
     orig_mean, rec_mean = orig_mean[:, :model_width], rec_mean[:, :model_width]
     (grad_head,) = norm_back(weight_own * (rec_mean - orig_mean))
     grad_recon = (grad_head + aux_pull).astype(bf16)
     gather = Gather(grad_recon)
-    gap = orig_normed.astype(bf16).astype(f32) - rec_float.astype(bf16).astype(f32)
+    aux_group = gather_behind(aux_blocks, grad_recon)
+    pre_odd, pre_even = aux_back(aux_group[1], aux_group[0], dec_weight, mask_odd, mask_even)
+    recon_group = gather.end(pre_odd)
+    dec_part, left_dec = part_dec((auxes_odd, auxes_even), (aux_group[1], aux_group[0]), err_dec, q_dec_rows, recon_group[0])
+    gap = orig_blocks.astype(f32) - rec_float.astype(bf16).astype(f32)
     kl_own = jnp.sum(gap * orig_mean, axis=1) - orig_lse + rec_lse
-    per_token = kl_own + aux_weight * jnp.sum(resid_err * resid_err, axis=1)
-    loss_row = jnp.full((1, model_width), jnp.sum(valid_float * per_token))
-    left_enc = err_left(q_enc_rows, err_enc, grad_recon)
-    gather.middle(left_enc)
-    recon_group = gather.end()
+    loss_tokens = (valid_float * (kl_own + aux_weight * err_square[:, 0]))[None, :]
 
     pre_odd, pre_even, grad_benc, bias_pull, enc_odd, enc_even = back_pass(
-        recon_group[1], recon_group[0], dec_weight, enc_weight, mask_odd, mask_even, pre_odd, pre_even, q_enc_columns
+        recon_group[1],
+        recon_group[0],
+        dec_weight,
+        enc_weight,
+        mask_odd,
+        mask_even,
+        pre_odd,
+        pre_even,
+        q_enc_columns,
+        dec_part,
     )
     small = call(
         functools.partial(left_sums_kernel, rank),
@@ -1120,7 +1283,7 @@
             left_dec,
             grad_recon,
             bias_pull,
-            loss_row,
+            loss_tokens,
         ),
         like((2 * rank + 8, model_width)),
     )

time: 575 us -> 527 us (0.917)
  waiting for transfers between devices: 31.9 us -> 11.1 us
  matrix products: 17.6 us -> 0 us
  other arithmetic: 23.2 us -> 12.8 us
  starting transfers between devices: 65.1 us -> 57.6 us
    pallas_call x1 -> x0, Pallas kernels: 52 us -> none  [build_mask(): pl.pallas_call(functools.partial(mask_kernel, tokens, hi_count, aux_count...]
    pallas_call x44 -> x51, Pallas kernels: 337 us -> 388 us  [call(): pl.pallas_call(body, out_shape=out_shape, grid=grid, in_specs=list(in_spe...]
    dot_general x11 -> x0, matrix products: 17.1 us -> none  [the longest x7 11.5 us: times(): jnp.dot(values, part, preferred_element_type=f32)]
    reduce_scatter x1, starting transfers between devices: 12.3 us -> 0.04 us  [per_device(): lax.psum_scatter(aux_part, 'lat', scatter_dimension=0, tiled=False)]
    reduce_scatter x1, waiting for transfers between devices: 10.4 us -> 0.02 us  [per_device(): lax.psum_scatter(aux_part, 'lat', scatter_dimension=0, tiled=False)]
    ppermute x51 -> x59, waiting for transfers between devices: 21.4 us -> 11 us  [swap(): return lax.ppermute(values, axis, [(i, i ^ bit) for i in range(count)])]
    ppermute x51 -> x59, starting transfers between devices: 52.7 us -> 57.3 us  [swap(): return lax.ppermute(values, axis, [(i, i ^ bit) for i in range(count)])]
    unnamed x125 -> x139, local copies, waits for them, and re-layouts: 18.1 us -> 21.9 us
  transfers between devices with their start and end apart: 56 -> 62, of which waited for: 12 -> 7; matrix products, arithmetic and copies ran while one was open for 7% -> 3% of each run, Pallas kernels for 56% -> 62%
where the time goes in v3:
time: 527 us; the launch traced here: 517 us
  Pallas kernels  391 us (74%)
  starting transfers between devices  57.6 us (11%)
  local copies, waits for them, and re-layouts  29.3 us (6%)
  between operations  15.1 us (3%)
  other arithmetic  12.8 us (2%)
  waiting for transfers between devices  11.1 us (2%)
    pallas_call x51, Pallas kernels, call(): pl.pallas_call(body, out_shape=out_shape, grid=grid, in_specs=list(in_spe...  388 us
    ppermute x59, starting transfers between devices, swap(): return lax.ppermute(values, axis, [(i, i ^ bit) for i in range(count)])  57.3 us
    unnamed x139, local copies, waits for them, and re-layouts  21.9 us
    ppermute x59, waiting for transfers between devices, swap(): return lax.ppermute(values, axis, [(i, i ^ bit) for i in range(count)])  11 us
  transfers between devices with their start and end apart: 62, of which 7 were waited for; matrix products, arithmetic and copies ran while one was open for 3% of the time, Pallas kernels for 62%

profile of v3, /device:TPU:0, one launch (start us, length us, event | category | flops | bytes accessed | tf_op | source)
XLA Modules:
  0.0 517.1 jit_solution(18094086243579515816)
XLA Ops:
  9.9 4.0 collective-permute-start.1
  14.5 2.7 stack_weights.1
  17.2 1.9 collective-permute-start.10
  19.1 1.5 collective-permute-start.7
  22.0 12.7 %build_mask.4 = (bf16[512,4096]{1,0:T(8,128)(2,1)}, bf16[512,4096]{1,0:T(8,128)(2,1)}, f32[1,128]{1,0:T(1,128)}) custom-call(s32[128,384]{1,0:T(8,128)} %copy-done.42, f32[1,8192]{1,0:T(1,128)} %add_convert_fusion.2.refs_1_, bf16[576,768]{1,0:T(8,128)(2,1)} %get-tuple-element.80.refs_2_.refs_4_), custom_call_target="tpu_custom_call" | custom-call | flops 8589934592 | bytes 2097152 | tf_op jit(solution)/shard_map/build_mask/pallas_call | solution.py:153
  36.0 12.7 %build_mask.5 = (bf16[512,4096]{1,0:T(8,128)(2,1)}, bf16[512,4096]{1,0:T(8,128)(2,1)}, f32[1,128]{1,0:T(1,128)}) custom-call(s32[128,384]{1,0:T(8,128)} %copy-done.68, f32[1,8192]{1,0:T(1,128)} %add_convert_fusion.2.refs_1_, bf16[512,4096]{1,0:T(8,128)(2,1)} %get-tuple-element.82.refs_2_, ...), custom_call_target="tpu_custom_call", output_to_operand_aliasing={{0}: (2, {}), {1}: (3, {})} | custom-call | flops 8589934592 | bytes 2097152 | tf_op jit(solution)/shard_map/build_mask/pallas_call | solution.py:153
  49.7 1.9 collective-permute-start.11
  52.6 12.8 %build_mask.6 = (bf16[512,4096]{1,0:T(8,128)(2,1)}, bf16[512,4096]{1,0:T(8,128)(2,1)}, f32[1,128]{1,0:T(1,128)}) custom-call(s32[128,384]{1,0:T(8,128)} %copy-done.67, f32[1,8192]{1,0:T(1,128)} %add_convert_fusion.2.refs_1_, bf16[512,4096]{1,0:T(8,128)(2,1)} %get-tuple-element.85.refs_2_.refs_1_, ...), custom_call_target="tpu_custom_call", output_to_operand_aliasing={{0}: (2, {}), {1}: (3, {})} | custom-call | flops 8589934592 | bytes 2097152 | tf_op jit(solution)/shard_map/build_mask/pallas_call | solution.py:153
  65.4 1.6 collective-permute-start.14
  66.9 5.5 %collective-permute-done.15.refs_0_ = bf16[576,768]{1,0:T(8,128)(2,1)S(1)} collective-permute-done((bf16[576,768]{1,0:T(8,128)(2,1)}, bf16[576,768]{1,0:T(8,128)(2,1)S(1)}, u32[]{:S(2)}, u32[]{:S(2)}) %collective-permute-start.15) | collective-permute-done | bytes 884768 | tf_op jit(solution)/shard_map/ppermute | solution.py:32
  72.4 13.4 %build_mask.7 = (bf16[512,4096]{1,0:T(8,128)(2,1)}, bf16[512,4096]{1,0:T(8,128)(2,1)}, f32[1,128]{1,0:T(1,128)}) custom-call(s32[128,384]{1,0:T(8,128)} %copy-done.66, f32[1,8192]{1,0:T(1,128)} %add_convert_fusion.2.refs_1_, bf16[512,4096]{1,0:T(8,128)(2,1)} %get-tuple-element.88.refs_2_, ...), custom_call_target="tpu_custom_call", output_to_operand_aliasing={{0}: (2, {}), {1}: (3, {})} | custom-call | flops 8589934592 | bytes 2097152 | tf_op jit(solution)/shard_map/build_mask/pallas_call | solution.py:153
  94.4 1.6 collective-permute-done.13.refs_15_
  98.8 10.5 %frozen_block.1 = (f32[128,768]{1,0:T(8,128)}, bf16[128,768]{1,0:T(8,128)(2,1)}, bf16[128,768]{1,0:T(8,128)(2,1)}) custom-call(bf16[128,768]{1,0:T(8,128)(2,1)} %refs_0_.5, f32[6,768]{1,0:T(8,128)} %refs_1_.7, f32[1,6912]{1,0:T(1,128)} %broadcast_in_dim.38.refs_2_, f32[1,768]{1,0:T(1,128)} %broadcast_in_dim.39.refs_3_, ...), custom_call_target="tpu_custom_call" | custom-call | flops 1811939328 | bytes 14155776 | tf_op jit(solution)/shard_map/frozen_block/pallas_call | solution.py:153
  109.6 1.6 collective-permute-start.18
  111.2 2.6 collective-permute-start.19
  114.0 1.5 collective-permute-start.21
  115.5 7.3 %rounded.2.refs_1_.refs_3_ = bf16[768,4096]{1,0:T(8,128)(2,1)} custom-call(f32[768,4096]{1,0:T(8,128)} %refs_4_.2, bf16[128,768]{1,0:T(8,128)(2,1)} %get-tuple-element.93.refs_1_.refs_3_), custom_call_target="tpu_custom_call" | custom-call | bytes 18874368 | tf_op jit(solution)/shard_map/rounded/pallas_call | solution.py:153
  123.0 1.7 collective-permute-start.23
  125.3 7.3 %rounded.3.refs_4_.refs_1_.refs_2_ = bf16[4096,768]{1,0:T(8,128)(2,1)} custom-call(f32[4096,768]{1,0:T(8,128)} %refs_4_.3, bf16[768,4096]{1,0:T(8,128)(2,1)} %rounded.2.refs_1_.refs_3_, f32[1,128]{1,0:T(1,128)} %add_add_fusion.5.refs_2_), custom_call_target="tpu_custom_call" | custom-call | bytes 18874368 | tf_op jit(solution)/shard_map/rounded/pallas_call | solution.py:153
  134.0 2.2 assemble.3.refs_0_.refs_3_.refs_1_
  136.3 3.2 factor_pieces.2
  139.5 3.2 factor_pieces.3
  143.6 12.5 %forward.2 = (bf16[512,4096]{1,0:T(8,128)(2,1)}, bf16[512,4096]{1,0:T(8,128)(2,1)}, f32[512,768]{1,0:T(8,128)}) custom-call(bf16[512,768]{1,0:T(8,128)(2,1)} %copy-done.14, bf16[768,4096]{1,0:T(8,128)(2,1)} %rounded.2.refs_1_.refs_3_, f32[1,4096]{1,0:T(1,128)} %bitcast.34, bf16[512,4096]{1,0:T(8,128)(2,1)} %collective-permute-done.25.refs_3_.refs_4_, ...), custom_call_target="tpu_custom_call" | custom-call | flops 6442450944 | bytes 25165824 | tf_op jit(solution)/shard_map/forward/pallas_call | solution.py:153
  157.5 12.5 %forward.3 = (bf16[512,4096]{1,0:T(8,128)(2,1)}, bf16[512,4096]{1,0:T(8,128)(2,1)}, f32[512,768]{1,0:T(8,128)}) custom-call(bf16[512,768]{1,0:T(8,128)(2,1)} %assemble.3.refs_0_.refs_3_.refs_1_, bf16[768,4096]{1,0:T(8,128)(2,1)} %rounded.2.refs_1_.refs_3_, f32[1,4096]{1,0:T(1,128)} %bitcast.35, ...), custom_call_target="tpu_custom_call" | custom-call | flops 6442450944 | bytes 25165824 | tf_op jit(solution)/shard_map/forward/pallas_call | solution.py:153
  171.2 2.9 chip_sum.3
  174.0 1.5 collective-permute-start.27
  177.5 11.7 %aux_forward.1.refs_1_ = f32[8,128,768]{2,1,0:T(8,128)} custom-call(bf16[512,4096]{1,0:T(8,128)(2,1)} %get-tuple-element.104.refs_0_, bf16[512,4096]{1,0:T(8,128)(2,1)} %get-tuple-element.105.refs_1_, bf16[4096,768]{1,0:T(8,128)(2,1)} %rounded.3.refs_4_.refs_1_.refs_2_, f32[128,768]{1,0:T(8,128)} %get-tuple-element.102.refs_3_), custom_call_target="tpu_custom_call" | custom-call | flops 6442450944 | bytes 14680064 | tf_op jit(solution)/shard_map/aux_forward/pallas_call | solution.py:153
  189.5 2.7 reorder.2
  193.0 2.1 last_sum.3
  196.6 1.6 collective-permute-start.30
  200.2 17.9 %head_part.4.refs_4_.refs_0_ = f32[512,896]{1,0:T(8,128)} custom-call(bf16[512,768]{1,0:T(8,128)(2,1)} %get-tuple-element.107.refs_0_, bf16[6656,768]{1,0:T(8,128)(2,1)} %refs_1_.11, bf16[128,768]{1,0:T(8,128)(2,1)} %copy-done.26), custom_call_target="tpu_custom_call" | custom-call | flops 15703474176 | bytes 10223616 | tf_op jit(solution)/shard_map/head_part/pallas_call | solution.py:153
  219.6 2.2 assemble.4.refs_2_.refs_1_.refs_0_
  222.9 17.8 %head_part.5.refs_0_ = f32[512,896]{1,0:T(8,128)} custom-call(bf16[512,768]{1,0:T(8,128)(2,1)} %get-tuple-element.106.refs_4_.refs_0_, bf16[6656,768]{1,0:T(8,128)(2,1)} %refs_1_.11, bf16[512,768]{1,0:T(8,128)(2,1)} %assemble.4.refs_2_.refs_1_.refs_0_), custom_call_target="tpu_custom_call" | custom-call | flops 15703474176 | bytes 10223616 | tf_op jit(solution)/shard_map/head_part/pallas_call | solution.py:153
  241.9 3.3 chip_sum.4
  245.2 1.6 collective-permute-start.34
  249.6 18.1 %head_part.6.refs_4_.refs_0_ = f32[512,896]{1,0:T(8,128)} custom-call(bf16[512,768]{1,0:T(8,128)(2,1)} %copy-done.65, bf16[6656,768]{1,0:T(8,128)(2,1)} %refs_1_.11, f32[128,896]{1,0:T(8,128)} %get-tuple-element.112.refs_2_.refs_3_), custom_call_target="tpu_custom_call" | custom-call | flops 15703474176 | bytes 10223616 | tf_op jit(solution)/shard_map/head_part/pallas_call | solution.py:153
  269.3 2.6 last_sum.4.refs_4_.refs_1_
  273.7 2.2 residual_pull.1
  276.0 17.9 %head_part.7.refs_0_ = f32[512,896]{1,0:T(8,128)} custom-call(bf16[512,768]{1,0:T(8,128)(2,1)} %assemble.4.refs_2_.refs_1_.refs_0_, bf16[6656,768]{1,0:T(8,128)(2,1)} %refs_1_.11, bf16[128,768]{1,0:T(8,128)(2,1)} %get-tuple-element.113.refs_2_), custom_call_target="tpu_custom_call" | custom-call | flops 15703474176 | bytes 10223616 | tf_op jit(solution)/shard_map/head_part/pallas_call | solution.py:153
  295.1 3.3 chip_sum.5
  298.4 1.6 collective-permute-start.39
  301.9 6.5 %factor_products.1 = (f32[512,128]{1,0:T(8,128)}, f32[512,128]{1,0:T(8,128)}) custom-call(bf16[512,4096]{1,0:T(8,128)(2,1)} %get-tuple-element.118.refs_0_, bf16[512,4096]{1,0:T(8,128)(2,1)} %get-tuple-element.119.refs_1_, bf16[4096,128]{1,0:T(8,128)(2,1)} %get-tuple-element.120.refs_2_, f32[128,896]{1,0:T(8,128)} %get-tuple-element.117.refs_3_), custom_call_target="tpu_custom_call" | custom-call | flops 1073741824 | bytes 8388608 | tf_op jit(solution)/shard_map/factor_products/pallas_call | solution.py:153
  308.4 7.9 %err_left.1.refs_4_.refs_8_ = f32[8,768]{1,0:T(8,128)} custom-call(bf16[32,4096]{1,0:T(8,128)(2,1)} %get-tuple-element.95.refs_1_.refs_0_, f32[768,4096]{1,0:T(8,128)} %bitcast.23, f32[512,128]{1,0:T(8,128)} %get-tuple-element.121.refs_2_.refs_4_), custom_call_target="tpu_custom_call" | custom-call | flops 402653184 | bytes 12582912 | tf_op jit(solution)/shard_map/err_left/pallas_call | solution.py:153
  317.9 2.7 last_sum.5
  323.4 1.6 collective-permute-start.42
  327.9 2.7 reorder.3
  330.6 12.1 %aux_back.1 = (bf16[512,4096]{1,0:T(8,128)(2,1)}, bf16[512,4096]{1,0:T(8,128)(2,1)}) custom-call(bf16[512,768]{1,0:T(8,128)(2,1)} %get-tuple-element.123.refs_0_.refs_2_, bf16[512,768]{1,0:T(8,128)(2,1)} %get-tuple-element.124.refs_1_.refs_3_, bf16[4096,768]{1,0:T(8,128)(2,1)} %rounded.3.refs_4_.refs_1_.refs_2_, ...), custom_call_target="tpu_custom_call" | custom-call | flops 6442450944 | bytes 23068672 | tf_op jit(solution)/shard_map/aux_back/pallas_call | solution.py:153
  343.5 2.2 assemble.5.refs_6_.refs_1_.refs_7_.refs_3_
  346.2 16.7 %part_dec.1 = (f32[4096,768]{1,0:T(8,128)}, f32[8,768]{1,0:T(8,128)}) custom-call(bf16[512,4096]{1,0:T(8,128)(2,1)} %get-tuple-element.104.refs_0_, bf16[512,4096]{1,0:T(8,128)(2,1)} %get-tuple-element.105.refs_1_, bf16[512,768]{1,0:T(8,128)(2,1)} %get-tuple-element.123.refs_0_.refs_2_, bf16[512,768]{1,0:T(8,128)(2,1)} %get-tuple-element.124.refs_1_.refs_3_, ...), custom_call_target="tpu_custom_call" | custom-call | flops 6442450944 | bytes 33554432 | tf_op jit(solution)/shard_map/part_dec/pallas_call | solution.py:153
  363.9 18.0 %back_pass.1 = (bf16[512,4096]{1,0:T(8,128)(2,1)}, bf16[512,4096]{1,0:T(8,128)(2,1)}, f32[1,4096]{1,0:T(1,128)}, f32[16,768]{1,0:T(8,128)}, f32[512,128]{1,0:T(8,128)}, /*index=5*/f32[512,128]{1,0:T(8,128)}) custom-call(bf16[512,768]{1,0:T(8,128)(2,1)} %copy-done.2, bf16[512,768]{1,0:T(8,128)(2,1)} %assemble.5.refs_6_.refs_1_.refs_7_.refs_3_, ...), custom_call_target="tpu_custom_call" | custom-call | flops 7516192768 | bytes 37748736 | tf_op jit(solution)/shard_map/back_pass/pallas_call | solution.py:153
  381.9 4.3 left_sums.1.refs_5_
  386.7 8.8 %add_dec.2.refs_4_ = f32[4096,768]{1,0:T(8,128)} custom-call(bf16[512,4096]{1,0:T(8,128)(2,1)} %get-tuple-element.118.refs_0_, bf16[512,4096]{1,0:T(8,128)(2,1)} %get-tuple-element.119.refs_1_, bf16[512,768]{1,0:T(8,128)(2,1)} %copy-done.2, bf16[512,768]{1,0:T(8,128)(2,1)} %assemble.5.refs_6_.refs_1_.refs_7_.refs_3_, ...), custom_call_target="tpu_custom_call", output_to_operand_aliasing={{}: (4, {})} | custom-call | flops 3221225472 | bytes 16777216 | tf_op jit(solution)/shard_map/add_dec/pallas_call | solution.py:153
  395.6 1.6 collective-permute-start.47
  399.2 8.7 %add_dec.3.refs_6_.refs_1_.refs_2_ = f32[4096,768]{1,0:T(8,128)} custom-call(bf16[512,4096]{1,0:T(8,128)(2,1)} %get-tuple-element.118.refs_0_, bf16[512,4096]{1,0:T(8,128)(2,1)} %get-tuple-element.119.refs_1_, bf16[512,768]{1,0:T(8,128)(2,1)} %copy-done.2, bf16[512,768]{1,0:T(8,128)(2,1)} %assemble.5.refs_6_.refs_1_.refs_7_.refs_3_, ...), custom_call_target="tpu_custom_call", output_to_operand_aliasing={{}: (4, {})} | custom-call | flops 3221225472 | bytes 16777216 | tf_op jit(solution)/shard_map/add_dec/pallas_call | solution.py:153
  409.8 3.2 collective-permute-start.51
  413.2 15.2 %form_enc.1.refs_1_.refs_2_ = f32[768,4096]{1,0:T(8,128)} custom-call(bf16[512,768]{1,0:T(8,128)(2,1)} %copy-done.14, bf16[512,768]{1,0:T(8,128)(2,1)} %assemble.3.refs_0_.refs_3_.refs_1_, bf16[512,4096]{1,0:T(8,128)(2,1)} %get-tuple-element.136.refs_2_, bf16[512,4096]{1,0:T(8,128)(2,1)} %get-tuple-element.137.refs_3_, f32[768,4096]{1,0:T(8,128)} %bitcast.24, ...), custom_call_target="tpu_custom_call" | custom-call | flops 6442450944 | bytes 33554432 | tf_op jit(solution)/shard_map/form_enc/pallas_call | solution.py:153
  430.0 2.8 orthonormal.1
  432.8 7.0 %right_part.2.refs_2_ = bf16[8,4096]{1,0:T(8,128)(2,1)} custom-call(bf16[48,768]{1,0:T(8,128)(2,1)} %get-tuple-element.135.refs_0_, f32[768,4096]{1,0:T(8,128)} %form_enc.1.refs_1_.refs_2_), custom_call_target="tpu_custom_call" | custom-call | flops 603979776 | bytes 12582912 | tf_op jit(solution)/shard_map/right_part/pallas_call | solution.py:153
  440.2 3.8 collective-permute-start.54
  444.3 7.8 %right_part.3.refs_0_ = f32[8,4096]{1,0:T(8,128)} custom-call(bf16[48,768]{1,0:T(8,128)(2,1)} %get-tuple-element.139.refs_0_, f32[4096,768]{1,0:T(8,128)} %add_dec.3.refs_6_.refs_1_.refs_2_, bf16[8,4096]{1,0:T(8,128)(2,1)} %right_part.2.refs_2_), custom_call_target="tpu_custom_call" | custom-call | flops 603979776 | bytes 12582912 | tf_op jit(solution)/shard_map/right_part/pallas_call | solution.py:153
  452.8 1.6 stack.1
  454.7 3.8 collective-permute-start.57
  459.8 24.5 %final_update.2 = (f32[768,4096]{1,0:T(8,128)}, f32[768,4096]{1,0:T(8,128)}, f32[768,4096]{1,0:T(8,128)}) custom-call(bf16[48,768]{1,0:T(8,128)(2,1)} %get-tuple-element.135.refs_0_, f32[8,4096]{1,0:T(8,128)} %add_add_fusion.2.refs_1_.refs_2_, f32[768,4096]{1,0:T(8,128)} %form_enc.1.refs_1_.refs_2_, f32[768,4096]{1,0:T(8,128)} %refs_3_.4, f32[768,4096]{1,0:T(8,128)} %refs_4_.2), custom_call_target="tpu_custom_call" | custom-call | flops 301989888 | bytes 75497472 | tf_op jit(solution)/shard_map/final_update/pallas_call | solution.py:153
  485.2 24.3 %final_update.3 = (f32[4096,768]{1,0:T(8,128)}, f32[4096,768]{1,0:T(8,128)}, f32[4096,768]{1,0:T(8,128)}) custom-call(bf16[48,768]{1,0:T(8,128)(2,1)} %get-tuple-element.139.refs_0_, f32[16,4096]{1,0:T(8,128)} %copy-done.18, f32[4096,768]{1,0:T(8,128)} %add_dec.3.refs_6_.refs_1_.refs_2_, f32[4096,768]{1,0:T(8,128)} %refs_3_.5, f32[4096,768]{1,0:T(8,128)} %refs_4_.3, ...), custom_call_target="tpu_custom_call" | custom-call | flops 301989888 | bytes 75497472 | tf_op jit(solution)/shard_map/final_update/pallas_call | solution.py:153
  (295 shorter events, 65.2 us)
Async XLA Ops:
  7.2 182.3 %all-gather.5.cloned.1.call-start = ((), (), s32[]{:S(2)}) async-start(), calls=%async_computation.2 | async-start | bytes 1769472 | tf_op jit(solution)/shard_map/all_gather | solution.py:333
  9.9 24.8 %collective-permute-start.1 = (s32[128,384]{1,0:T(8,128)S(1)}, s32[128,384]{1,0:T(8,128)S(1)}, u32[]{:S(2)}, u32[]{:S(2)}) collective-permute-start(s32[128,384]{1,0:T(8,128)S(1)} %pad_add_fusion.refs_0_), channel_id=1, source_target_pairs={{0,6},{1,7},{2,4},{3,5},{4,2},{5,3},{6,0},{7,1},{8,14},{9,15},{10,... | collective-permute-start | bytes 589832 | tf_op jit(solution)/shard_map/ppermute | solution.py:32
  13.8 21.4 %collective-permute-start.2 = (s32[128,384]{1,0:T(8,128)S(1)}, s32[128,384]{1,0:T(8,128)S(1)}, u32[]{:S(2)}, u32[]{:S(2)}) collective-permute-start(s32[128,384]{1,0:T(8,128)S(1)} %pad_add_fusion.refs_0_), channel_id=1, source_target_pairs={{0,4},{1,5},{2,6},{3,7},{4,0},{5,1},{6,2},{7,3},{8,12},{9,13},{10,... | collective-permute-start | bytes 589832 | tf_op jit(solution)/shard_map/ppermute | solution.py:32
  14.3 20.9 %collective-permute-start = (s32[128,384]{1,0:T(8,128)S(1)}, s32[128,384]{1,0:T(8,128)S(1)}, u32[]{:S(2)}, u32[]{:S(2)}) collective-permute-start(s32[128,384]{1,0:T(8,128)S(1)} %pad_add_fusion.refs_0_), channel_id=1, source_target_pairs={{0,2},{1,3},{2,0},{3,1},{4,6},{5,7},{6,4},{7,5},{8,10},{9,11},{10,... | collective-permute-start | bytes 589832 | tf_op jit(solution)/shard_map/ppermute | solution.py:32
  17.2 34.4 %collective-permute-start.10 = (bf16[576,768]{1,0:T(8,128)(2,1)}, bf16[576,768]{1,0:T(8,128)(2,1)S(1)}, u32[]{:S(2)}, u32[]{:S(2)}) collective-permute-start(bf16[576,768]{1,0:T(8,128)(2,1)} %get-tuple-element.80.refs_2_.refs_4_), channel_id=1, source_target_pairs={{0,4},{1,5},{2,6},{3,7},{4,0},{5,1},{6,2},{7,3},{8,12},{9,13},{10,... | collective-permute-start | bytes 2654216 | tf_op jit(solution)/shard_map/ppermute | solution.py:32
  19.1 29.6 %collective-permute-start.7 = (bf16[576,768]{1,0:T(8,128)(2,1)}, bf16[576,768]{1,0:T(8,128)(2,1)S(1)}, u32[]{:S(2)}, u32[]{:S(2)}) collective-permute-start(bf16[576,768]{1,0:T(8,128)(2,1)} %get-tuple-element.91.refs_5_), channel_id=1, source_target_pairs={{0,2},{1,3},{2,0},{3,1},{4,6},{5,7},{6,4},{7,5},{8,10},{9,11},{10,... | collective-permute-start | bytes 2654216 | tf_op jit(solution)/shard_map/ppermute | solution.py:32
  34.7 30.7 %collective-permute-start.6 = (bf16[576,768]{1,0:T(8,128)(2,1)}, bf16[576,768]{1,0:T(8,128)(2,1)}, u32[]{:S(2)}, u32[]{:S(2)}) collective-permute-start(bf16[576,768]{1,0:T(8,128)(2,1)} %get-tuple-element.80.refs_2_.refs_4_), channel_id=1, source_target_pairs={{0,2},{1,3},{2,0},{3,1},{4,6},{5,7},{6,4},{7,5},{8,10},{9,11},{10,... | collective-permute-start | bytes 2654216 | tf_op jit(solution)/shard_map/ppermute | solution.py:32
  49.6 22.8 %collective-permute-start.15 = (bf16[576,768]{1,0:T(8,128)(2,1)}, bf16[576,768]{1,0:T(8,128)(2,1)S(1)}, u32[]{:S(2)}, u32[]{:S(2)}) collective-permute-start(bf16[576,768]{1,0:T(8,128)(2,1)} %pass_after.8.refs_9_), channel_id=1, source_target_pairs={{0,4},{1,5},{2,6},{3,7},{4,0},{5,1},{6,2},{7,3},{8,12},{9,13},{10,... | collective-permute-start | bytes 2654216 | tf_op jit(solution)/shard_map/ppermute | solution.py:32
  49.7 38.9 %collective-permute-start.11 = (bf16[576,768]{1,0:T(8,128)(2,1)}, bf16[576,768]{1,0:T(8,128)(2,1)}, u32[]{:S(2)}, u32[]{:S(2)}) collective-permute-start(bf16[576,768]{1,0:T(8,128)(2,1)} %get-tuple-element.91.refs_5_), channel_id=1, source_target_pairs={{0,4},{1,5},{2,6},{3,7},{4,0},{5,1},{6,2},{7,3},{8,12},{9,13},{10,... | collective-permute-start | bytes 2654216 | tf_op jit(solution)/shard_map/ppermute | solution.py:32
  51.6 38.0 %collective-permute-start.4 = (bf16[576,768]{1,0:T(8,128)(2,1)}, bf16[576,768]{1,0:T(8,128)(2,1)}, u32[]{:S(2)}, u32[]{:S(2)}) collective-permute-start(bf16[576,768]{1,0:T(8,128)(2,1)} %get-tuple-element.80.refs_2_.refs_4_), channel_id=1, source_target_pairs={{0,1},{1,0},{2,3},{3,2},{4,5},{5,4},{6,7},{7,6},{8,9},{9,8},{10,11... | collective-permute-start | bytes 2654216 | tf_op jit(solution)/shard_map/ppermute | solution.py:32
  51.6 38.5 %collective-permute-start.5 = (bf16[576,768]{1,0:T(8,128)(2,1)}, bf16[576,768]{1,0:T(8,128)(2,1)}, u32[]{:S(2)}, u32[]{:S(2)}) collective-permute-start(bf16[576,768]{1,0:T(8,128)(2,1)} %get-tuple-element.91.refs_5_), channel_id=1, source_target_pairs={{0,1},{1,0},{2,3},{3,2},{4,5},{5,4},{6,7},{7,6},{8,9},{9,8},{10,11... | collective-permute-start | bytes 2654216 | tf_op jit(solution)/shard_map/ppermute | solution.py:32
  65.4 22.1 %collective-permute-start.14 = (bf16[576,768]{1,0:T(8,128)(2,1)S(1)}, bf16[576,768]{1,0:T(8,128)(2,1)S(1)}, u32[]{:S(2)}, u32[]{:S(2)}) collective-permute-start(bf16[576,768]{1,0:T(8,128)(2,1)S(1)} %copy-done.5), channel_id=1, source_target_pairs={{0,2},{1,3},{2,0},{3,1},{4,6},{5,7},{6,4},{7,5},{8,10},{9,11},{10,... | collective-permute-start | bytes 2654216 | tf_op jit(solution)/shard_map/ppermute | solution.py:32
  72.4 18.2 %collective-permute-start.12 = (bf16[576,768]{1,0:T(8,128)(2,1)S(1)}, bf16[576,768]{1,0:T(8,128)(2,1)}, u32[]{:S(2)}, u32[]{:S(2)}) collective-permute-start(bf16[576,768]{1,0:T(8,128)(2,1)S(1)} %copy-done.5), channel_id=1, source_target_pairs={{0,1},{1,0},{2,3},{3,2},{4,5},{5,4},{6,7},{7,6},{8,9},{9,8},{10,11... | collective-permute-start | bytes 2654216 | tf_op jit(solution)/shard_map/ppermute | solution.py:32
  87.5 2.7 collective-permute-start.3
  89.6 3.6 collective-permute-start.9
  89.6 4.8 collective-permute-start.8
  90.1 5.9 %collective-permute-start.13 = (bf16[576,768]{1,0:T(8,128)(2,1)}, bf16[576,768]{1,0:T(8,128)(2,1)S(1)}, u32[]{:S(2)}, u32[]{:S(2)}) collective-permute-start(bf16[576,768]{1,0:T(8,128)(2,1)} %collective-permute-done.11.refs_13_), channel_id=1, source_target_pairs={{0,1},{1,0},{2,3},{3,2},{4,5},{5,4},{6,7},{7,6},{8,9},{9,8},{10,11... | collective-permute-start | bytes 2654216 | tf_op jit(solution)/shard_map/ppermute | solution.py:32
  90.2 5.8 %collective-permute-start.17 = (bf16[576,768]{1,0:T(8,128)(2,1)S(1)}, bf16[576,768]{1,0:T(8,128)(2,1)S(1)}, u32[]{:S(2)}, u32[]{:S(2)}) collective-permute-start(bf16[576,768]{1,0:T(8,128)(2,1)S(1)} %copy-done.9), channel_id=1, source_target_pairs={{0,1},{1,0},{2,3},{3,2},{4,5},{5,4},{6,7},{7,6},{8,9},{9,8},{10,11... | collective-permute-start | bytes 2654216 | tf_op jit(solution)/shard_map/ppermute | solution.py:32
  90.6 7.2 %collective-permute-start.16 = (bf16[576,768]{1,0:T(8,128)(2,1)}, bf16[576,768]{1,0:T(8,128)(2,1)S(1)}, u32[]{:S(2)}, u32[]{:S(2)}) collective-permute-start(bf16[576,768]{1,0:T(8,128)(2,1)} %pass_after.10.refs_16_), channel_id=1, source_target_pairs={{0,1},{1,0},{2,3},{3,2},{4,5},{5,4},{6,7},{7,6},{8,9},{9,8},{10,11... | collective-permute-start | bytes 2654216 | tf_op jit(solution)/shard_map/ppermute | solution.py:32
  109.4 33.3 %collective-permute-start.25 = (bf16[512,4096]{1,0:T(8,128)(2,1)}, bf16[512,4096]{1,0:T(8,128)(2,1)}, u32[]{:S(2)}, u32[]{:S(2)}) collective-permute-start(bf16[512,4096]{1,0:T(8,128)(2,1)} %pass_after.13), channel_id=1, source_target_pairs={{0,1},{1,0},{2,3},{3,2},{4,5},{5,4},{6,7},{7,6},{8,9},{9,8},{10,11... | collective-permute-start | bytes 12582920 | tf_op jit(solution)/shard_map/ppermute | solution.py:32
  109.6 13.2 %collective-permute-start.18 = (f32[1,128]{1,0:T(1,128)}, f32[1,128]{1,0:T(1,128)S(1)}, u32[]{:S(2)}, u32[]{:S(2)}) collective-permute-start(f32[1,128]{1,0:T(1,128)} %pass_after.12), channel_id=1, source_target_pairs={{0,8},{8,0},{16,24},{24,16},{1,9},{9,1},{17,25},{25,17},{2,10},{10... | collective-permute-start | bytes 1544 | tf_op jit(solution)/shard_map/ppermute | solution.py:32
  111.2 11.9 %collective-permute-start.19 = (f32[1,128]{1,0:T(1,128)}, f32[1,128]{1,0:T(1,128)S(1)}, u32[]{:S(2)}, u32[]{:S(2)}) collective-permute-start(f32[1,128]{1,0:T(1,128)} %pass_after.12), channel_id=1, source_target_pairs={{0,16},{8,24},{16,0},{24,8},{1,17},{9,25},{17,1},{25,9},{2,18},{10... | collective-permute-start | bytes 1544 | tf_op jit(solution)/shard_map/ppermute | solution.py:32
  113.8 11.0 %collective-permute-start.20 = (f32[1,128]{1,0:T(1,128)}, f32[1,128]{1,0:T(1,128)S(1)}, u32[]{:S(2)}, u32[]{:S(2)}) collective-permute-start(f32[1,128]{1,0:T(1,128)} %pass_after.12), channel_id=1, source_target_pairs={{0,24},{8,16},{16,8},{24,0},{1,25},{9,17},{17,9},{25,1},{2,26},{10... | collective-permute-start | bytes 1544 | tf_op jit(solution)/shard_map/ppermute | solution.py:32
  114.0 18.6 %collective-permute-start.21 = (bf16[128,768]{1,0:T(8,128)(2,1)S(1)}, bf16[128,768]{1,0:T(8,128)(2,1)S(1)}, u32[]{:S(2)}, u32[]{:S(2)}) collective-permute-start(bf16[128,768]{1,0:T(8,128)(2,1)S(1)} %copy-done.12), channel_id=1, source_target_pairs={{0,2},{1,3},{2,0},{3,1},{4,6},{5,7},{6,4},{7,5},{8,10},{9,11},{10,... | collective-permute-start | bytes 589832 | tf_op jit(solution)/shard_map/ppermute | solution.py:32
  122.8 9.8 %collective-permute-start.22 = (bf16[128,768]{1,0:T(8,128)(2,1)S(1)}, bf16[128,768]{1,0:T(8,128)(2,1)S(1)}, u32[]{:S(2)}, u32[]{:S(2)}) collective-permute-start(bf16[128,768]{1,0:T(8,128)(2,1)S(1)} %copy-done.13), channel_id=1, source_target_pairs={{0,6},{1,7},{2,4},{3,5},{4,2},{5,3},{6,0},{7,1},{8,14},{9,15},{10,... | collective-permute-start | bytes 589832 | tf_op jit(solution)/shard_map/ppermute | solution.py:32
  123.0 10.3 %collective-permute-start.23 = (bf16[128,768]{1,0:T(8,128)(2,1)S(1)}, bf16[128,768]{1,0:T(8,128)(2,1)S(1)}, u32[]{:S(2)}, u32[]{:S(2)}) collective-permute-start(bf16[128,768]{1,0:T(8,128)(2,1)S(1)} %copy-done.13), channel_id=1, source_target_pairs={{0,4},{1,5},{2,6},{3,7},{4,0},{5,1},{6,2},{7,3},{8,12},{9,13},{10,... | collective-permute-start | bytes 589832 | tf_op jit(solution)/shard_map/ppermute | solution.py:32
  136.2 6.5 %collective-permute-start.24 = (bf16[512,768]{1,0:T(8,128)(2,1)}, bf16[512,768]{1,0:T(8,128)(2,1)S(1)}, u32[]{:S(2)}, u32[]{:S(2)}) collective-permute-start(bf16[512,768]{1,0:T(8,128)(2,1)} %assemble.3.refs_0_.refs_3_.refs_1_), channel_id=1, source_target_pairs={{0,1},{1,0},{2,3},{3,2},{4,5},{5,4},{6,7},{7,6},{8,9},{9,8},{10,11... | collective-permute-start | bytes 2359304 | tf_op jit(solution)/shard_map/ppermute | solution.py:32
  136.2 137.5 %reduce-scatter.2.cloned.1.call-start = ((), (), s32[]{:S(2)}) async-start(), calls=%async_computation.1 | async-start | bytes 3538944 | tf_op jit(solution)/shard_map/reduce_scatter | solution.py:1222
  156.1 13.9 %collective-permute-start.26 = (f32[512,768]{1,0:T(8,128)}, f32[512,768]{1,0:T(8,128)S(1)}, u32[]{:S(2)}, u32[]{:S(2)}) collective-permute-start(f32[512,768]{1,0:T(8,128)} %get-tuple-element.97.refs_5_), channel_id=1, source_target_pairs={{0,1},{1,0},{2,3},{3,2},{4,5},{5,4},{6,7},{7,6},{8,9},{9,8},{10,11... | collective-permute-start | bytes 4718600 | tf_op jit(solution)/shard_map/ppermute | solution.py:32
  174.0 18.1 %collective-permute-start.27 = (bf16[128,768]{1,0:T(8,128)(2,1)}, bf16[128,768]{1,0:T(8,128)(2,1)S(1)}, u32[]{:S(2)}, u32[]{:S(2)}) collective-permute-start(bf16[128,768]{1,0:T(8,128)(2,1)} %get-tuple-element.99), channel_id=1, source_target_pairs={{0,2},{1,3},{2,0},{3,1},{4,6},{5,7},{6,4},{7,5},{8,10},{9,11},{10,... | collective-permute-start | bytes 589832 | tf_op jit(solution)/shard_map/ppermute | solution.py:32
  175.6 16.6 %collective-permute-start.28 = (bf16[128,768]{1,0:T(8,128)(2,1)}, bf16[128,768]{1,0:T(8,128)(2,1)S(1)}, u32[]{:S(2)}, u32[]{:S(2)}) collective-permute-start(bf16[128,768]{1,0:T(8,128)(2,1)} %get-tuple-element.100), channel_id=1, source_target_pairs={{0,6},{1,7},{2,4},{3,5},{4,2},{5,3},{6,0},{7,1},{8,14},{9,15},{10,... | collective-permute-start | bytes 589832 | tf_op jit(solution)/shard_map/ppermute | solution.py:32
  176.7 15.4 %collective-permute-start.29 = (bf16[128,768]{1,0:T(8,128)(2,1)}, bf16[128,768]{1,0:T(8,128)(2,1)S(1)}, u32[]{:S(2)}, u32[]{:S(2)}) collective-permute-start(bf16[128,768]{1,0:T(8,128)(2,1)} %get-tuple-element.101), channel_id=1, source_target_pairs={{0,4},{1,5},{2,6},{3,7},{4,0},{5,1},{6,2},{7,3},{8,12},{9,13},{10,... | collective-permute-start | bytes 589832 | tf_op jit(solution)/shard_map/ppermute | solution.py:32
  189.2 138.7 %all-gather.7.cloned.1.call-start = ((), (), s32[]{:S(2)}) async-start(), calls=%async_computation.3 | async-start | bytes 1769472 | tf_op jit(solution)/shard_map/all_gather | solution.py:333
  196.6 21.5 %collective-permute-start.30 = (bf16[128,768]{1,0:T(8,128)(2,1)S(1)}, bf16[128,768]{1,0:T(8,128)(2,1)S(1)}, u32[]{:S(2)}, u32[]{:S(2)}) collective-permute-start(bf16[128,768]{1,0:T(8,128)(2,1)S(1)} %add_convert_fusion.1.refs_2_.refs_3_), channel_id=1, source_target_pairs={{0,2},{1,3},{2,0},{3,1},{4,6},{5,7},{6,4},{7,5},{8,10},{9,11},{10,... | collective-permute-start | bytes 589832 | tf_op jit(solution)/shard_map/ppermute | solution.py:32
  198.2 19.9 %collective-permute-start.31 = (bf16[128,768]{1,0:T(8,128)(2,1)S(1)}, bf16[128,768]{1,0:T(8,128)(2,1)S(1)}, u32[]{:S(2)}, u32[]{:S(2)}) collective-permute-start(bf16[128,768]{1,0:T(8,128)(2,1)S(1)} %add_convert_fusion.1.refs_2_.refs_3_), channel_id=1, source_target_pairs={{0,6},{1,7},{2,4},{3,5},{4,2},{5,3},{6,0},{7,1},{8,14},{9,15},{10,... | collective-permute-start | bytes 589832 | tf_op jit(solution)/shard_map/ppermute | solution.py:32
  199.4 18.8 %collective-permute-start.32 = (bf16[128,768]{1,0:T(8,128)(2,1)S(1)}, bf16[128,768]{1,0:T(8,128)(2,1)S(1)}, u32[]{:S(2)}, u32[]{:S(2)}) collective-permute-start(bf16[128,768]{1,0:T(8,128)(2,1)S(1)} %add_convert_fusion.1.refs_2_.refs_3_), channel_id=1, source_target_pairs={{0,4},{1,5},{2,6},{3,7},{4,0},{5,1},{6,2},{7,3},{8,12},{9,13},{10,... | collective-permute-start | bytes 589832 | tf_op jit(solution)/shard_map/ppermute | solution.py:32
  221.7 18.9 %collective-permute-start.33 = (f32[512,896]{1,0:T(8,128)}, f32[512,896]{1,0:T(8,128)S(1)}, u32[]{:S(2)}, u32[]{:S(2)}) collective-permute-start(f32[512,896]{1,0:T(8,128)} %pass_after.14), channel_id=1, source_target_pairs={{0,1},{1,0},{2,3},{3,2},{4,5},{5,4},{6,7},{7,6},{8,9},{9,8},{10,11... | collective-permute-start | bytes 5505032 | tf_op jit(solution)/shard_map/ppermute | solution.py:32
  222.9 25.8 %collective-permute-start.37 = (bf16[512,768]{1,0:T(8,128)(2,1)S(1)}, bf16[512,768]{1,0:T(8,128)(2,1)S(1)}, u32[]{:S(2)}, u32[]{:S(2)}) collective-permute-start(bf16[512,768]{1,0:T(8,128)(2,1)S(1)} %copy-done.15), channel_id=1, source_target_pairs={{0,1},{1,0},{2,3},{3,2},{4,5},{5,4},{6,7},{7,6},{8,9},{9,8},{10,11... | collective-permute-start | bytes 2359304 | tf_op jit(solution)/shard_map/ppermute | solution.py:32
  245.2 22.5 %collective-permute-start.34 = (bf16[128,896]{1,0:T(8,128)(2,1)}, bf16[128,896]{1,0:T(8,128)(2,1)S(1)}, u32[]{:S(2)}, u32[]{:S(2)}) collective-permute-start(bf16[128,896]{1,0:T(8,128)(2,1)} %get-tuple-element.109), channel_id=1, source_target_pairs={{0,2},{1,3},{2,0},{3,1},{4,6},{5,7},{6,4},{7,5},{8,10},{9,11},{10,... | collective-permute-start | bytes 688136 | tf_op jit(solution)/shard_map/ppermute | solution.py:32
  246.8 21.0 %collective-permute-start.35 = (bf16[128,896]{1,0:T(8,128)(2,1)}, bf16[128,896]{1,0:T(8,128)(2,1)S(1)}, u32[]{:S(2)}, u32[]{:S(2)}) collective-permute-start(bf16[128,896]{1,0:T(8,128)(2,1)} %get-tuple-element.110), channel_id=1, source_target_pairs={{0,6},{1,7},{2,4},{3,5},{4,2},{5,3},{6,0},{7,1},{8,14},{9,15},{10,... | collective-permute-start | bytes 688136 | tf_op jit(solution)/shard_map/ppermute | solution.py:32
  248.0 19.8 %collective-permute-start.36 = (bf16[128,896]{1,0:T(8,128)(2,1)}, bf16[128,896]{1,0:T(8,128)(2,1)S(1)}, u32[]{:S(2)}, u32[]{:S(2)}) collective-permute-start(bf16[128,896]{1,0:T(8,128)(2,1)} %get-tuple-element.111), channel_id=1, source_target_pairs={{0,4},{1,5},{2,6},{3,7},{4,0},{5,1},{6,2},{7,3},{8,12},{9,13},{10,... | collective-permute-start | bytes 688136 | tf_op jit(solution)/shard_map/ppermute | solution.py:32
  271.9 22.0 %collective-permute-start.38 = (f32[512,896]{1,0:T(8,128)}, f32[512,896]{1,0:T(8,128)S(1)}, u32[]{:S(2)}, u32[]{:S(2)}) collective-permute-start(f32[512,896]{1,0:T(8,128)} %pass_after.15), channel_id=1, source_target_pairs={{0,1},{1,0},{2,3},{3,2},{4,5},{5,4},{6,7},{7,6},{8,9},{9,8},{10,11... | collective-permute-start | bytes 5505032 | tf_op jit(solution)/shard_map/ppermute | solution.py:32
  298.4 18.0 %collective-permute-start.39 = (bf16[128,896]{1,0:T(8,128)(2,1)}, bf16[128,896]{1,0:T(8,128)(2,1)S(1)}, u32[]{:S(2)}, u32[]{:S(2)}) collective-permute-start(bf16[128,896]{1,0:T(8,128)(2,1)} %get-tuple-element.114), channel_id=1, source_target_pairs={{0,2},{1,3},{2,0},{3,1},{4,6},{5,7},{6,4},{7,5},{8,10},{9,11},{10,... | collective-permute-start | bytes 688136 | tf_op jit(solution)/shard_map/ppermute | solution.py:32
  300.0 16.4 %collective-permute-start.40 = (bf16[128,896]{1,0:T(8,128)(2,1)}, bf16[128,896]{1,0:T(8,128)(2,1)S(1)}, u32[]{:S(2)}, u32[]{:S(2)}) collective-permute-start(bf16[128,896]{1,0:T(8,128)(2,1)} %get-tuple-element.115), channel_id=1, source_target_pairs={{0,6},{1,7},{2,4},{3,5},{4,2},{5,3},{6,0},{7,1},{8,14},{9,15},{10,... | collective-permute-start | bytes 688136 | tf_op jit(solution)/shard_map/ppermute | solution.py:32
  301.2 15.3 %collective-permute-start.41 = (bf16[128,896]{1,0:T(8,128)(2,1)}, bf16[128,896]{1,0:T(8,128)(2,1)S(1)}, u32[]{:S(2)}, u32[]{:S(2)}) collective-permute-start(bf16[128,896]{1,0:T(8,128)(2,1)} %get-tuple-element.116), channel_id=1, source_target_pairs={{0,4},{1,5},{2,6},{3,7},{4,0},{5,1},{6,2},{7,3},{8,12},{9,13},{10,... | collective-permute-start | bytes 688136 | tf_op jit(solution)/shard_map/ppermute | solution.py:32
  323.4 19.4 %collective-permute-start.42 = (bf16[128,768]{1,0:T(8,128)(2,1)S(1)}, bf16[128,768]{1,0:T(8,128)(2,1)S(1)}, u32[]{:S(2)}, u32[]{:S(2)}) collective-permute-start(bf16[128,768]{1,0:T(8,128)(2,1)S(1)} %add_convert_fusion.refs_1_.refs_3_.refs_10_), channel_id=1, source_target_pairs={{0,2},{1,3},{2,0},{3,1},{4,6},{5,7},{6,4},{7,5},{8,10},{9,11},{10,... | collective-permute-start | bytes 589832 | tf_op jit(solution)/shard_map/ppermute | solution.py:32
  325.0 17.7 %collective-permute-start.43 = (bf16[128,768]{1,0:T(8,128)(2,1)S(1)}, bf16[128,768]{1,0:T(8,128)(2,1)S(1)}, u32[]{:S(2)}, u32[]{:S(2)}) collective-permute-start(bf16[128,768]{1,0:T(8,128)(2,1)S(1)} %add_convert_fusion.refs_1_.refs_3_.refs_10_), channel_id=1, source_target_pairs={{0,6},{1,7},{2,4},{3,5},{4,2},{5,3},{6,0},{7,1},{8,14},{9,15},{10,... | collective-permute-start | bytes 589832 | tf_op jit(solution)/shard_map/ppermute | solution.py:32
  326.2 16.5 %collective-permute-start.44 = (bf16[128,768]{1,0:T(8,128)(2,1)S(1)}, bf16[128,768]{1,0:T(8,128)(2,1)S(1)}, u32[]{:S(2)}, u32[]{:S(2)}) collective-permute-start(bf16[128,768]{1,0:T(8,128)(2,1)S(1)} %add_convert_fusion.refs_1_.refs_3_.refs_10_), channel_id=1, source_target_pairs={{0,4},{1,5},{2,6},{3,7},{4,0},{5,1},{6,2},{7,3},{8,12},{9,13},{10,... | collective-permute-start | bytes 589832 | tf_op jit(solution)/shard_map/ppermute | solution.py:32
  345.7 17.2 %collective-permute-start.45 = (bf16[512,768]{1,0:T(8,128)(2,1)}, bf16[512,768]{1,0:T(8,128)(2,1)S(1)}, u32[]{:S(2)}, u32[]{:S(2)}) collective-permute-start(bf16[512,768]{1,0:T(8,128)(2,1)} %assemble.5.refs_6_.refs_1_.refs_7_.refs_3_), channel_id=1, source_target_pairs={{0,1},{1,0},{2,3},{3,2},{4,5},{5,4},{6,7},{7,6},{8,9},{9,8},{10,11... | collective-permute-start | bytes 2359304 | tf_op jit(solution)/shard_map/ppermute | solution.py:32
  386.2 9.4 %collective-permute-start.46 = (f32[24,768]{1,0:T(8,128)}, f32[24,768]{1,0:T(8,128)S(1)}, u32[]{:S(2)}, u32[]{:S(2)}) collective-permute-start(f32[24,768]{1,0:T(8,128)} %left_sums.1.refs_5_), channel_id=1, source_target_pairs={{0,1},{1,0},{2,3},{3,2},{4,5},{5,4},{6,7},{7,6},{8,9},{9,8},{10,11... | collective-permute-start | bytes 221192 | tf_op jit(solution)/shard_map/ppermute | solution.py:32
  395.6 12.2 %collective-permute-start.47 = (f32[24,768]{1,0:T(8,128)S(1)}, f32[24,768]{1,0:T(8,128)S(1)}, u32[]{:S(2)}, u32[]{:S(2)}) collective-permute-start(f32[24,768]{1,0:T(8,128)S(1)} %add.137.refs_5_), channel_id=1, source_target_pairs={{0,2},{1,3},{2,0},{3,1},{4,6},{5,7},{6,4},{7,5},{8,10},{9,11},{10,... | collective-permute-start | bytes 221192 | tf_op jit(solution)/shard_map/ppermute | solution.py:32
  397.2 10.6 %collective-permute-start.48 = (f32[24,768]{1,0:T(8,128)S(1)}, f32[24,768]{1,0:T(8,128)S(1)}, u32[]{:S(2)}, u32[]{:S(2)}) collective-permute-start(f32[24,768]{1,0:T(8,128)S(1)} %add.137.refs_5_), channel_id=1, source_target_pairs={{0,4},{1,5},{2,6},{3,7},{4,0},{5,1},{6,2},{7,3},{8,12},{9,13},{10,... | collective-permute-start | bytes 221192 | tf_op jit(solution)/shard_map/ppermute | solution.py:32
  398.0 9.9 %collective-permute-start.49 = (f32[24,768]{1,0:T(8,128)S(1)}, f32[24,768]{1,0:T(8,128)S(1)}, u32[]{:S(2)}, u32[]{:S(2)}) collective-permute-start(f32[24,768]{1,0:T(8,128)S(1)} %add.137.refs_5_), channel_id=1, source_target_pairs={{0,6},{1,7},{2,4},{3,5},{4,2},{5,3},{6,0},{7,1},{8,14},{9,15},{10,... | collective-permute-start | bytes 221192 | tf_op jit(solution)/shard_map/ppermute | solution.py:32
  408.8 19.7 %collective-permute-start.50 = (f32[24,768]{1,0:T(8,128)S(1)}, f32[24,768]{1,0:T(8,128)S(1)}, u32[]{:S(2)}, u32[]{:S(2)}) collective-permute-start(f32[24,768]{1,0:T(8,128)S(1)} %add_add_fusion.4.refs_5_), channel_id=1, source_target_pairs={{0,8},{8,0},{16,24},{24,16},{1,9},{9,1},{17,25},{25,17},{2,10},{10... | collective-permute-start | bytes 221192 | tf_op jit(solution)/shard_map/ppermute | solution.py:32
  409.8 18.7 %collective-permute-start.51 = (f32[24,768]{1,0:T(8,128)S(1)}, f32[24,768]{1,0:T(8,128)S(1)}, u32[]{:S(2)}, u32[]{:S(2)}) collective-permute-start(f32[24,768]{1,0:T(8,128)S(1)} %add_add_fusion.4.refs_5_), channel_id=1, source_target_pairs={{0,16},{8,24},{16,0},{24,8},{1,17},{9,25},{17,1},{25,9},{2,18},{10... | collective-permute-start | bytes 221192 | tf_op jit(solution)/shard_map/ppermute | solution.py:32
  413.0 15.5 %collective-permute-start.52 = (f32[24,768]{1,0:T(8,128)S(1)}, f32[24,768]{1,0:T(8,128)S(1)}, u32[]{:S(2)}, u32[]{:S(2)}) collective-permute-start(f32[24,768]{1,0:T(8,128)S(1)} %add_add_fusion.4.refs_5_), channel_id=1, source_target_pairs={{0,24},{8,16},{16,8},{24,0},{1,25},{9,17},{17,9},{25,1},{2,26},{10... | collective-permute-start | bytes 221192 | tf_op jit(solution)/shard_map/ppermute | solution.py:32
  439.8 12.2 %collective-permute-start.53 = (bf16[8,4096]{1,0:T(8,128)(2,1)}, bf16[8,4096]{1,0:T(8,128)(2,1)S(1)}, u32[]{:S(2)}, u32[]{:S(2)}) collective-permute-start(bf16[8,4096]{1,0:T(8,128)(2,1)} %right_part.2.refs_2_), channel_id=1, source_target_pairs={{0,8},{8,0},{16,24},{24,16},{1,9},{9,1},{17,25},{25,17},{2,10},{10... | collective-permute-start | bytes 196616 | tf_op jit(solution)/shard_map/ppermute | solution.py:32
  440.2 11.8 %collective-permute-start.54 = (bf16[8,4096]{1,0:T(8,128)(2,1)}, bf16[8,4096]{1,0:T(8,128)(2,1)S(1)}, u32[]{:S(2)}, u32[]{:S(2)}) collective-permute-start(bf16[8,4096]{1,0:T(8,128)(2,1)} %right_part.2.refs_2_), channel_id=1, source_target_pairs={{0,16},{8,24},{16,0},{24,8},{1,17},{9,25},{17,1},{25,9},{2,18},{10... | collective-permute-start | bytes 196616 | tf_op jit(solution)/shard_map/ppermute | solution.py:32
  444.0 8.0 %collective-permute-start.55 = (bf16[8,4096]{1,0:T(8,128)(2,1)}, bf16[8,4096]{1,0:T(8,128)(2,1)S(1)}, u32[]{:S(2)}, u32[]{:S(2)}) collective-permute-start(bf16[8,4096]{1,0:T(8,128)(2,1)} %right_part.2.refs_2_), channel_id=1, source_target_pairs={{0,24},{8,16},{16,8},{24,0},{1,25},{9,17},{17,9},{25,1},{2,26},{10... | collective-permute-start | bytes 196616 | tf_op jit(solution)/shard_map/ppermute | solution.py:32
  454.3 30.0 %collective-permute-start.56 = (bf16[16,4096]{1,0:T(8,128)(2,1)}, bf16[16,4096]{1,0:T(8,128)(2,1)S(1)}, u32[]{:S(2)}, u32[]{:S(2)}) collective-permute-start(bf16[16,4096]{1,0:T(8,128)(2,1)} %stack.1), channel_id=1, source_target_pairs={{0,8},{8,0},{16,24},{24,16},{1,9},{9,1},{17,25},{25,17},{2,10},{10... | collective-permute-start | bytes 393224 | tf_op jit(solution)/shard_map/ppermute | solution.py:32
  454.7 29.7 %collective-permute-start.57 = (bf16[16,4096]{1,0:T(8,128)(2,1)}, bf16[16,4096]{1,0:T(8,128)(2,1)S(1)}, u32[]{:S(2)}, u32[]{:S(2)}) collective-permute-start(bf16[16,4096]{1,0:T(8,128)(2,1)} %stack.1), channel_id=1, source_target_pairs={{0,16},{8,24},{16,0},{24,8},{1,17},{9,25},{17,1},{25,9},{2,18},{10... | collective-permute-start | bytes 393224 | tf_op jit(solution)/shard_map/ppermute | solution.py:32
  458.5 25.8 %collective-permute-start.58 = (bf16[16,4096]{1,0:T(8,128)(2,1)}, bf16[16,4096]{1,0:T(8,128)(2,1)S(1)}, u32[]{:S(2)}, u32[]{:S(2)}) collective-permute-start(bf16[16,4096]{1,0:T(8,128)(2,1)} %stack.1), channel_id=1, source_target_pairs={{0,24},{8,16},{16,8},{24,0},{1,25},{9,17},{17,9},{25,1},{2,26},{10... | collective-permute-start | bytes 393224 | tf_op jit(solution)/shard_map/ppermute | solution.py:32
  459.8 24.5 %copy-start.31 = (bf16[16,4096]{1,0:T(8,128)(2,1)S(1)}, bf16[16,4096]{1,0:T(8,128)(2,1)}, u32[]{:S(2)}) copy-start(bf16[16,4096]{1,0:T(8,128)(2,1)} %stack.1) | copy-start | bytes 393220
  485.2 24.3 %copy-start.57 = (f32[4096]{0:T(1024)S(1)}, f32[4096]{0:T(1024)}, u32[]{:S(2)}) copy-start(f32[4096]{0:T(1024)} %param.41) | copy-start | bytes 49156
  (67 other events, 323.4 us)
Sparse Core Ops, SparseCore 0:
  136.3 26.1 all-gather.4
  189.3 46.5 reduce-scatter.1
  276.1 26.3 all-gather.6
